TPU v7x, 32 devices: a whole 2x2x4 slice. The times are simulated.
32 devices in a mesh: row: 8 (over z, core), col: 4 (over y, x).
Axes of the slice: x: 2, y: 2, z: 4, core: 2. Of those that a mesh axis runs over, the one named last changes fastest.
Arguments:
- tokens: bfloat16 [1024, 12288], P('col', 'row'), may hold values from -6 to 6
- weight: bfloat16 [12288, 24576], P('row', 'col'), may hold values from -0.0546875 to 0.0546875
- cotangent: bfloat16 [1024, 24576], P('row', 'col'), may hold values from -6 to 6
Outputs:
- activated: bfloat16 [1024, 24576], P('row', 'col')
- input_grad: bfloat16 [1024, 12288], P('col', 'row')
- weight_grad: bfloat16 [12288, 24576], P('row', 'col')
All inputs are finite; a program needn't handle non-finite values.
Results may differ from a plain program's by a relative error of at most 0.03.
Values may be sent and summed in bfloat16 or wider, within the bound.
No kernel may reach another device: no remote copies, remote signals or barrier semaphores. Data moves between devices by JAX's collectives and lax.ppermute only.
A program may use at most 128 MiB of HBM per device.

v0:
```python
import math

import jax
import jax.numpy as jnp
from jax import lax
from jax.sharding import PartitionSpec as P


def gelu_exact(value):
    return 0.5 * value * (1.0 + jax.scipy.special.erf(value / math.sqrt(2.0)))


def gelu_slope(value):
    return 0.5 * (1.0 + jax.scipy.special.erf(value / math.sqrt(2.0))) + value * jnp.exp(
        -0.5 * value * value
    ) / math.sqrt(2.0 * math.pi)


def on_device(tokens, weight, cotangent):
    gathered = lax.all_gather(tokens, "col", axis=0, tiled=True)
    block = gathered
    pre = lax.psum_scatter(
        jnp.dot(block, weight, preferred_element_type=jnp.float32).astype(jnp.bfloat16),
        "row",
        scatter_dimension=0,
        tiled=True,
    ).astype(jnp.float32)
    activated = gelu_exact(pre).astype(jnp.bfloat16)
    slope_grad = (cotangent.astype(jnp.float32) * gelu_slope(pre)).astype(jnp.bfloat16)
    grad_full = lax.all_gather(slope_grad, "row", axis=0, tiled=True)
    block = grad_full
    input_grad = lax.psum_scatter(
        lax.dot_general(
            block, weight, (((1,), (1,)), ((), ())), preferred_element_type=jnp.float32
        ).astype(jnp.bfloat16),
        "col",
        scatter_dimension=0,
        tiled=True,
    )
    weight_grad = lax.dot_general(
        gathered, grad_full, (((0,), (0,)), ((), ())), preferred_element_type=jnp.float32
    ).astype(jnp.bfloat16)
    return (activated, input_grad, weight_grad)


def solution(mesh):
    return jax.shard_map(
        on_device,
        mesh=mesh,
        in_specs=(P("col", "row"), P("row", "col"), P("row", "col")),
        out_specs=(P("row", "col"), P("col", "row"), P("row", "col")),
        check_vma=False,
    )
```

profile of v0, /device:TPU:0, one launch (start us, length us, event | category | flops | bytes accessed | tf_op | source)
XLA Modules:
  0.0 420.3 jit_solution(12825214698803593680)
XLA Ops:
  7.2 0.0 all-gather.3.cloned.1.call-start
  7.2 0.7 all-gather.3.cloned.1.call-update
  7.9 0.0 reduce-scatter.3.cloned.1.call-start
  7.9 48.6 %all-gather.3.cloned.1.call-done = bf16[1024,1536]{1,0:T(8,128)(2,1)} async-done(((bf16[256,1536]{1,0:T(8,128)(2,1)}), bf16[1024,1536]{1,0:T(8,128)(2,1)}) %all-gather.3.cloned.1.call-update) | async-done | bytes 3145744 | tf_op jit(solution)/shard_map/all_gather | solution.py:20
  56.5 25.7 %convolution_convert_fusion.1 = bf16[1024,6144]{1,0:T(8,128)(2,1)} fusion(bf16[1024,1536]{1,0:T(8,128)(2,1)} %all-gather.3.cloned.1.call-done, bf16[1536,6144]{1,0:T(8,128)(2,1)} %param.4), kind=kOutput, calls=%fused_computation.2 | convolution fusion | flops 19333644288 | bytes 34603008 | tf_op jit(solution)/shard_map/dot_general | solution.py:23
  82.3 0.0 copy-start
  82.3 0.0 reduce-scatter.3.cloned.1.call-update
  82.3 0.0 all-gather.5.cloned.1.call-start
  82.4 129.3 %reduce-scatter.3.cloned.1.call-done = bf16[128,6144]{1,0:T(8,128)(2,1)} async-done(((bf16[1024,6144]{1,0:T(8,128)(2,1)}), bf16[128,6144]{1,0:T(8,128)(2,1)}) %reduce-scatter.3.cloned.1.call-update) | async-done | bytes 1572880 | tf_op jit(solution)/shard_map/reduce_scatter | solution.py:22
  211.7 0.0 copy-done
  211.7 4.0 fusion.9
  215.7 0.0 all-gather.5.cloned.1.call-update
  215.7 0.2 reduce-scatter.5.cloned.1.call-start
  215.9 115.0 %all-gather.5.cloned.1.call-done = bf16[1024,6144]{1,0:T(8,128)(2,1)} async-done(((bf16[128,6144]{1,0:T(8,128)(2,1)}), bf16[1024,6144]{1,0:T(8,128)(2,1)}) %all-gather.5.cloned.1.call-update) | async-done | bytes 12582928 | tf_op jit(solution)/shard_map/all_gather | solution.py:30
  331.0 27.4 %convolution_convert_fusion.2 = bf16[1024,1536]{1,0:T(8,128)(2,1)} fusion(bf16[1024,6144]{1,0:T(8,128)(2,1)} %all-gather.5.cloned.1.call-done, bf16[1536,6144]{1,0:T(8,128)(2,1)} %param.4), kind=kOutput, calls=%fused_computation.8 | convolution fusion | flops 19328925696 | bytes 34603008 | tf_op jit(solution)/shard_map/dot_general | solution.py:33
  358.4 0.0 copy-start.1
  358.4 0.0 reduce-scatter.5.cloned.1.call-update
  358.5 1.9 copy-done.1
  360.3 28.9 %fusion = bf16[1536,6144]{0,1:T(8,128)(2,1)} fusion(bf16[1024,6144]{1,0:T(8,128)(2,1)} %all-gather.5.cloned.1.call-done, bf16[1024,1536]{1,0:T(8,128)(2,1)S(1)} %copy-done.1), kind=kOutput, calls=%fused_computation.1 | convolution fusion | flops 19336790016 | bytes 34603008 | tf_op jit(solution)/shard_map/dot_general | solution.py:40
  389.2 24.6 %copy.6 = bf16[1536,6144]{1,0:T(8,128)(2,1)} copy(bf16[1536,6144]{0,1:T(8,128)(2,1)} %fusion) | data formatting | bytes 37748736
  413.8 0.0 reduce-scatter.5.cloned.1.call-done
Async XLA Ops:
  7.2 49.4 %all-gather.3.cloned.1.call-start = ((), (), s32[]{:S(2)}) async-start(), calls=%async_computation.2 | async-start | bytes 3932160 | tf_op jit(solution)/shard_map/all_gather | solution.py:20
  7.9 203.8 %reduce-scatter.3.cloned.1.call-start = ((), (), s32[]{:S(2)}) async-start(), calls=%async_computation.3 | async-start | bytes 14155776 | tf_op jit(solution)/shard_map/reduce_scatter | solution.py:22
  82.3 129.4 %copy-start = (bf16[128,6144]{1,0:T(8,128)(2,1)S(1)}, bf16[128,6144]{1,0:T(8,128)(2,1)}, u32[]{:S(2)}) copy-start(bf16[128,6144]{1,0:T(8,128)(2,1)} %param.5) | copy-start | bytes 4718596
  82.3 248.7 %all-gather.5.cloned.1.call-start = ((), (), s32[]{:S(2)}) async-start(), calls=%async_computation.4 | async-start | bytes 14155776 | tf_op jit(solution)/shard_map/all_gather | solution.py:30
  215.7 198.1 %reduce-scatter.5.cloned.1.call-start = ((), (), s32[]{:S(2)}) async-start(), calls=%async_computation.5 | async-start | bytes 3932160 | tf_op jit(solution)/shard_map/reduce_scatter | solution.py:32
  358.4 1.9 copy-start.1
Sparse Core Ops, SparseCore 0:
  9.8 46.6 all-gather.2
  82.4 129.1 reduce-scatter.2
  215.8 115.0 all-gather.4
  358.6 42.1 reduce-scatter.4
where the time goes:
time: 421 us; the launch traced here: 420 us
  waiting for transfers between devices  294 us (70%)
  matrix products  82.1 us (20%)
  local copies, waits for them, and re-layouts  26.5 us (6%)
  between operations  13.8 us (3%)
    reduce_scatter x1, waiting for transfers between devices, on_device(): lax.psum_scatter(jnp.dot(block, weight, preferred_element_type=jnp.float3...  129 us
    all_gather x1, waiting for transfers between devices, on_device(): grad_full = lax.all_gather(slope_grad, 'row', axis=0, tiled=True)  115 us
    all_gather x1, waiting for transfers between devices, on_device(): gathered = lax.all_gather(tokens, 'col', axis=0, tiled=True)  48.6 us
    dot_general x1, matrix products, on_device(): lax.dot_general(gathered, grad_full, (((0,), (0,)), ((), ())), preferred_...  28.9 us
    dot_general x1, matrix products, on_device(): lax.dot_general(block, weight, (((1,), (1,)), ((), ())), preferred_elemen...  27.4 us
    unnamed x5, local copies, waits for them, and re-layouts  26.5 us
    dot_general x1, matrix products, on_device(): jnp.dot(block, weight, preferred_element_type=jnp.float32)  25.7 us
  transfers between devices with their start and end apart: 4, of which 3 were waited for; matrix products, arithmetic and copies ran while one was open for 13% of the time, Pallas kernels for 0%

commit v1 on v0

v1 whole, which is shorter than its diff:
```python
import math

import jax
import jax.numpy as jnp
from jax import lax
from jax.experimental import pallas as pl
from jax.experimental.pallas import tpu as pltpu
from jax.sharding import PartitionSpec as P

BF16 = jnp.bfloat16
F32 = jnp.float32
CORES = 2
CHUNKS = 2
STREAMS = 2
HALVES = 2
PIECES = 1
EXCHANGE = 3


def gelu_and_slope(value):
    below = 0.5 * (1.0 + lax.erf(value / math.sqrt(2.0)))
    density = jnp.exp(-0.5 * value * value) / math.sqrt(2.0 * math.pi)
    return value * below, below + value * density


def tile(extent, limit):
    best = 128
    for size in range(128, min(extent, limit) + 1, 128):
        if extent % size == 0:
            best = size
    return best


chain = []


def chained_call(body, name, grid, flops, moved, in_specs, out_specs, out_shape, vmem=24, prefetch=0, **spec):
    several = isinstance(out_specs, list)
    outs = out_specs if several else [out_specs]
    shapes = out_shape if several else [out_shape]
    token = jax.ShapeDtypeStruct((8, 128), F32)

    def with_token(*refs):
        ends = prefetch + len(in_specs), prefetch + len(in_specs) + 1 + len(outs)
        refs[ends[1]][...] = jnp.zeros((8, 128), F32)
        body(*refs[: ends[0]], *refs[ends[0] + 1 : ends[1]])

    def run(*args):
        *values, after = pl.pallas_call(
            with_token,
            grid_spec=pltpu.PrefetchScalarGridSpec(
                num_scalar_prefetch=prefetch,
                grid=grid,
                in_specs=in_specs + [pl.BlockSpec(memory_space=pl.ANY)],
                out_specs=outs + [pl.BlockSpec((8, 128), lambda *_: (0, 0))],
            ),
            out_shape=shapes + [token],
            compiler_params=pltpu.CompilerParams(vmem_limit_bytes=vmem * 2**20),
            cost_estimate=pl.CostEstimate(flops=flops, bytes_accessed=moved, transcendentals=0),
            name=name,
            **spec,
        )(*args, chain[-1])
        chain.append(after)
        return values if several else values[0]

    return run


def forward_matmul(x, weight, chunk, f):
    rows, width = x.shape
    bn = tile(f, 512)
    steps = f // bn
    part = rows // HALVES

    def body(x_ref, w_ref, *outs):
        total = jnp.dot(x_ref[...], w_ref[...], preferred_element_type=F32).astype(BF16)
        for half, out in enumerate(outs):
            out[...] = total[half * part : (half + 1) * part]

    return chained_call(
        body,
        "forward",
        (steps,),
        2 * rows * width * f,
        2 * (rows * width + width * f + rows * f),
        vmem=47,
        in_specs=[
            pl.BlockSpec((rows, width), lambda j: (0, 0)),
            pl.BlockSpec((width, bn), lambda j: (0, chunk * steps + j)),
        ],
        out_specs=[pl.BlockSpec((part, bn), lambda j: (0, j))] * HALVES,
        out_shape=[jax.ShapeDtypeStruct((part, f), BF16)] * HALVES,
    )(x, weight)


def input_grad_matmul(g, half, weight, chunk, total, buffer, last, first, pieces):
    rows, f = g.shape[0] // HALVES, g.shape[1]
    width = weight.shape[0]
    span = width // PIECES * pieces
    bn = tile(width // PIECES, 256)
    steps = span // bn
    start = first * (width // PIECES // bn)
    added = [] if total is None else [total]
    kept = [] if buffer is None else [buffer]

    def body(g_ref, w_ref, *rest):
        part = lax.dot_general(
            g_ref[...], w_ref[...], (((1,), (1,)), ((), ())), preferred_element_type=F32
        )
        if added:
            part += rest[0][...]
        rest[-1][...] = part.astype(rest[-1].dtype)

    out = pl.BlockSpec((rows, bn), lambda j: (0, start + j))
    return chained_call(
        body,
        "input_grad",
        (steps,),
        2 * rows * span * f,
        2 * (rows * f + span * f + 4 * rows * span),
        vmem=47,
        in_specs=[
            pl.BlockSpec((rows, f), lambda j: (half, 0)),
            pl.BlockSpec((bn, f), lambda j: (start + j, chunk)),
        ]
        + [out] * len(added)
        + [pl.BlockSpec(memory_space=pl.ANY)] * len(kept),
        out_specs=out,
        out_shape=jax.ShapeDtypeStruct((rows, width), BF16 if last else F32),
        input_output_aliases={2 + len(added): 0} if kept else {},
    )(g, weight, *added, *kept)


def weight_grad_matmul(x_t, g, buffer, chunk, units):
    width, rows = x_t.shape
    f = g.shape[1]
    bn = tile(f, 512)
    steps = f // bn
    kept = [] if buffer is None else [buffer]

    def body(x_ref, g_ref, *rest):
        part = jnp.dot(x_ref[...], g_ref[...], preferred_element_type=F32)
        rest[-1][...] = part.astype(BF16)

    return chained_call(
        body,
        "weight_grad",
        (steps,),
        2 * rows * width * f,
        2 * (rows * width + rows * f + width * f),
        vmem=47,
        in_specs=[
            pl.BlockSpec((width, rows), lambda j: (0, 0)),
            pl.BlockSpec((rows, bn), lambda j: (0, j)),
        ]
        + [pl.BlockSpec(memory_space=pl.ANY)] * len(kept),
        out_specs=pl.BlockSpec((width, bn), lambda j: (0, chunk * steps + j)),
        out_shape=jax.ShapeDtypeStruct((width, units), BF16),
        input_output_aliases={2: 0} if kept else {},
    )(x_t, g, *kept)


def message_kernel(where, part, theirs, came, keep):
    _, cores, few, f = part.shape
    bn = tile(f, 768)

    def body(where_ref, part_ref, theirs_ref, *rest):
        out = rest[-1]
        mine = part_ref[0].astype(F32) + theirs_ref[0].astype(F32)
        if came is not None:
            here = rest[0][...].astype(F32)
            summing = where_ref[1] > 0
            mine = jnp.where(summing, mine, here if keep else 0.0)
            if not keep:
                mine += here
        out[...] = mine.astype(BF16)

    block = pl.BlockSpec((1, cores, few, bn), lambda j, where: (where[0], 0, 0, j))
    flat = pl.BlockSpec((cores, few, bn), lambda j, where: (0, 0, j))
    given = [] if came is None else [came]
    return chained_call(
        body,
        "message",
        (f // bn,),
        0,
        0,
        prefetch=1,
        in_specs=[block, block] + [flat] * len(given),
        out_specs=flat,
        out_shape=jax.ShapeDtypeStruct((cores, few, f), BF16),
    )(where, part, theirs, *given)


def gelu_kernel(core, part, theirs, came, came_there, cotangent, cotangent_there, half, chunk, kept):
    _, cores, few, f = part.shape
    bn = tile(f, 512)
    steps = f // bn
    kept = [] if kept is None else [kept]

    def body(core_ref, part_ref, theirs_ref, came_ref, there_ref, mine_ref, other_ref, *rest):
        slope, activated = rest[-2:]
        first = core_ref[0] == 0
        values = []
        for c in range(cores):
            pre = part_ref[0, c].astype(F32) + theirs_ref[0, c].astype(F32)
            pre = pre + came_ref[c].astype(F32) + there_ref[c].astype(F32)
            value, grad = gelu_and_slope(pre)
            values.append(value)
            mine, other = mine_ref[...].astype(F32), other_ref[...].astype(F32)
            cot = jnp.where(first == (c == 0), mine, other)
            slope[c] = (cot * grad).astype(BF16)
        activated[...] = jnp.where(first, values[0], values[1]).astype(BF16)

    block = pl.BlockSpec((1, cores, few, bn), lambda j, core: (0, 0, 0, j))
    flat = pl.BlockSpec((cores, few, bn), lambda j, core: (0, 0, j))
    rows = pl.BlockSpec((few, bn), lambda j, core: (half, chunk * steps + j))
    return chained_call(
        body,
        "gelu",
        (steps,),
        0,
        0,
        prefetch=1,
        in_specs=[block, block, flat, flat, rows, rows]
        + [pl.BlockSpec(memory_space=pl.ANY)] * len(kept),
        out_specs=[flat, rows],
        out_shape=[
            jax.ShapeDtypeStruct((cores, few, f), BF16),
            jax.ShapeDtypeStruct(cotangent.shape, BF16),
        ],
        input_output_aliases={7: 1} if kept else {},
    )(core, part, theirs, came, came_there, cotangent, cotangent_there, *kept)


def collect_kernel(place, slope, mine, theirs, depth, half, buffer):
    cores, few, f = slope.shape
    bn = tile(f, 1024)
    kept = [] if buffer is None else [buffer]

    def body(place_ref, *refs):
        slope_ref, out = refs[0], refs[-1]
        mine_refs, their_refs = refs[1:depth], refs[depth : 2 * depth - 1]
        z, core = place_ref[0], place_ref[1]
        out[0, 0] = slope_ref[...]
        for j in range(1, depth):
            above = z + j < depth
            here = above == (core == 1)
            for down in (True, False):
                step = j if down else depth - j
                side = above if down else jnp.logical_not(above)

                @pl.when(side & here)
                def _():
                    out[0, j] = mine_refs[step - 1][...]

                @pl.when(side & jnp.logical_not(here))
                def _():
                    out[0, j] = their_refs[step - 1][...]

    flat = pl.BlockSpec((cores, few, bn), lambda j, place: (0, 0, j))
    return chained_call(
        body,
        "collect",
        (f // bn,),
        0,
        0,
        prefetch=1,
        in_specs=[flat] * (2 * depth - 1) + [pl.BlockSpec(memory_space=pl.ANY)] * len(kept),
        out_specs=pl.BlockSpec(
            (1, depth, cores, few, bn), lambda j, place: (half, 0, 0, 0, j)
        ),
        out_shape=jax.ShapeDtypeStruct((HALVES, depth, cores, few, f), BF16),
        input_output_aliases={2 * depth: 0} if kept else {},
    )(place, slope, *mine, *theirs, *kept)


def on_device(tokens, weight, cotangent):
    n_row, n_col = lax.axis_size("row"), lax.axis_size("col")
    depth = n_row // CORES
    row, col = lax.axis_index("row"), lax.axis_index("col")
    z, core = row // CORES, row % CORES
    place = jnp.where(core == 0, z, depth - 1 - z)
    width, units = weight.shape
    share = cotangent.shape[0]
    few = share // HALVES
    f = units // CHUNKS
    square = n_col == 4 and depth == 4

    def swap(value):
        return lax.ppermute(value, "row", [(r, r ^ 1) for r in range(n_row)])

    def onward(value, places):
        up = [(p * CORES, (p + 1) * CORES) for p in places]
        down = [((depth - 1 - p) * CORES + 1, (depth - 2 - p) * CORES + 1) for p in places]
        return lax.ppermute(value, "row", up + down)

    def cross(value, offset):
        return lax.ppermute(value, "col", [(c, c ^ offset) for c in range(4)])

    chain[:] = [jnp.zeros((8, 128), F32)]
    env = {"tokens": tokens, "cotangent": cotangent}

    def fence(*names):
        names = list(dict.fromkeys(n for n in names if n in env))
        for name, value in zip(names, lax.optimization_barrier([env[n] for n in names])):
            env[name] = value

    def gather():
        if square:
            mine = tokens.reshape(CORES, share, width)
            by_x, by_y = cross(mine, 1), cross(mine, 2)
            far = jnp.stack([cross(by_x[0], 2), cross(by_y[1], 1)])
            held = jnp.stack([mine, by_x, by_y, far])
            order = [col ^ ((z + j) % depth) for j in range(depth)]
        else:
            held = lax.all_gather(tokens, "col", axis=0, tiled=True)
            held = held.reshape(depth, CORES, share, width)
            order = [(z + j) % depth for j in range(depth)]
        blocks = [lax.dynamic_index_in_dim(held, b, 0, keepdims=False) for b in order]
        parts = [
            b[:, half * few : (half + 1) * few] for half in range(HALVES) for b in blocks
        ]
        env["x"] = jnp.concatenate(parts).reshape(HALVES * n_row * few, width)

    def columns_of(chunk):
        return slice(chunk * f, (chunk + 1) * f)

    sequence = [(half, chunk) for half in range(HALVES) for chunk in range(CHUNKS)]
    items = [sequence[q::STREAMS] for q in range(STREAMS)]
    count = len(sequence) // STREAMS
    steps = [(i, t) for i in range(count) for t in range(depth)]
    steps += [(count, t) for t in range(depth - 2)]

    input_grad, done = {}, []
    pending = []

    def forward(q):
        for i, part in enumerate(forward_matmul(env["x"], weight, q, f)):
            env["part", q, i] = part.reshape(depth, CORES, few, f)

    def exchange(q, i):
        env["theirs", q, i] = swap(env["part", q, i])
        pending.append(("theirs", q, i))

    def transpose():
        env["x_t"] = env["x"].T
        done.append("x_t")

    def backward_input(q, i, first=0, pieces=PIECES, before=None, last=False):
        half, chunk = items[q][i]
        if first == 0:
            collect(q, i)
        key = ("total", q, i)
        env[key] = input_grad_matmul(
            env["g", chunk].reshape(-1, f),
            half,
            weight,
            chunk,
            env.get(before),
            env.get(key),
            last,
            first,
            pieces,
        )
        done.append(key)

    def backward_weight(chunk):
        env["weight_grad"] = weight_grad_matmul(
            env["x_t"], env["g", chunk].reshape(-1, f), env.get("weight_grad"), chunk, units
        )

    def scatter_input(half, direct, total):
        pair = total.astype(BF16).reshape(depth, CORES, few, width)
        if direct:
            blocks = []
            for offset in range(4):
                at = ((col ^ offset) + depth - z) % depth
                block = lax.dynamic_index_in_dim(pair, at, 0, keepdims=False)
                blocks.append(cross(block, offset) if offset else block)
            input_grad[half] = sum(b.astype(F32) for b in blocks).astype(BF16)
        else:
            pair = lax.dynamic_slice(
                jnp.concatenate([pair, pair]), ((depth - z) % depth, 0, 0, 0), pair.shape
            )
            got = lax.psum_scatter(
                pair.reshape(n_col, -1, few, width), "col", scatter_dimension=0, tiled=True
            )
            input_grad[half] = got.reshape(-1, few, width)

    core_there = core.astype(jnp.int32).reshape(1)
    place_there = jnp.stack([z, core]).astype(jnp.int32)

    def gelu(q, i):
        half, chunk = items[q][i]
        env["slope", q, i], env["activated"] = gelu_kernel(
            core_there,
            env["part", q, i],
            env["theirs", q, i],
            env["came", q],
            env["came_there", q],
            cotangent,
            env["cotangent_there"],
            half,
            chunk,
            env.get("activated"),
        )
        done.append(("slope", q, i))

    def collect(q, i):
        half, chunk = items[q][i]
        order = range(1, depth)
        env["g", chunk] = collect_kernel(
            place_there,
            env["slope", q, i],
            [env["got", q, i, j] for j in order],
            [env["got_there", q, i, j] for j in order],
            depth,
            half,
            env.get(("g", chunk)),
        )

    def message(q, step):
        i, t = steps[step]
        if t == depth - 1:
            env["msg", q] = env["slope", q, i]
        elif i == count:
            env["msg", q] = env["came", q]
        else:
            at = jnp.where(core == 0, depth - 1 - t, t + 1)
            env["msg", q] = message_kernel(
                jnp.stack([at, place <= t]).astype(jnp.int32),
                env["part", q, i],
                env["theirs", q, i],
                None if i == 0 and t == 0 else env["came", q],
                t == 0,
            )

    def start(q, step):
        i, t = steps[step]
        first = t + 1 if i == count else 0
        last = t + 1 if (i == 0 and t < depth - 2) else depth - 1
        env["came", q] = onward(env["msg", q], range(first, last))

    def receive(q, i, t):
        env["got", q, i, t] = env["came", q]
        env["got_there", q, i, t] = swap(env["came", q])
        pending.append(("got_there", q, i, t))

    env["cotangent_there"] = swap(cotangent)
    gather()
    fence("x", "cotangent_there")
    for q in range(STREAMS):
        forward(q)
        exchange(q, 0)
        fence(("part", q, 0), "x")
    fence(("theirs", 0, 0), ("part", STREAMS - 1, 0))
    for q in range(STREAMS):
        message(q, 0)
        start(q, 0)
    done.clear()
    pending.clear()
    for step in range(len(steps)):
        i, t = steps[step]
        for q in range(STREAMS):
            env["chain"] = chain[-1]
            fence(("came", q), "chain", *done, *pending)
            chain[-1] = env["chain"]
            done.clear()
            pending.clear()
            if t == depth - 2:
                env["came_there", q] = swap(env["came", q])
                gelu(q, i)
            elif t == depth - 1:
                receive(q, i, 1)
            elif i > 0:
                receive(q, i - 1, t + 2)
            if step + 1 == len(steps):
                before = ("total", q - 1, count - 1)
                backward_input(q, count - 1, before=before, last=q == STREAMS - 1)
                continue
            if i == 1 and t == 0 and q == 0:
                fence(("came", q), "x")
                transpose()
            if i == 1 and t == depth - 1:
                fence(("came", q), ("got_there", q, 0, depth - 1))
                backward_input(q, 0)
            fence(("came", q), *done)
            done.clear()
            message(q, step + 1)
            start(q, step + 1)
            if EXCHANGE < 3 and step == EXCHANGE:
                fence(("msg", q), ("part", q, 1))
                exchange(q, 1)
            if EXCHANGE == 3 and step == 2 and q == 1:
                for p in range(STREAMS):
                    fence(("msg", q), ("part", p, 1))
                    exchange(p, 1)
        if t == 0 and i == count:
            total = sum(env["total", p, i - 2] for p in range(STREAMS))
            scatter_input(0, False, total)
    last_total = ("total", STREAMS - 1, count - 1)
    scatter_input(HALVES - 1, square, env[last_total])
    for chunk in range(CHUNKS):
        fence(("g", chunk), last_total)
        backward_weight(chunk)

    input_grad = jnp.concatenate([input_grad[h] for h in range(HALVES)], axis=-2)
    return env["activated"], input_grad.reshape(tokens.shape), env["weight_grad"]


def solution(mesh):
    return jax.shard_map(
        on_device,
        mesh=mesh,
        in_specs=(P("col", "row"), P("row", "col"), P("row", "col")),
        out_specs=(P("row", "col"), P("col", "row"), P("row", "col")),
        check_vma=False,
    )
```

time: 421 us -> 402 us (0.955)
  waiting for transfers between devices: 294 us -> 80.9 us
  Pallas kernels: 0 us -> 155 us
  starting transfers between devices: 0.34 us -> 99 us
  matrix products: 82.1 us -> 0 us
  local copies, waits for them, and re-layouts: 26.5 us -> 42 us
    all_gather x2 -> x0, waiting for transfers between devices: 164 us -> none  [the longest x1 115 us: on_device(): grad_full = lax.all_gather(slope_grad, 'row', axis=0, tiled=True)]
    pallas_call x0 -> x28, Pallas kernels: none -> 155 us  [run(): pl.pallas_call(with_token, grid_spec=pltpu.PrefetchScalarGridSpec(num_sca...]
    reduce_scatter x2 -> x0, waiting for transfers between devices: 129 us -> none  [the longest x1 129 us: on_device(): lax.psum_scatter(jnp.dot(block, weight, preferred_element_type=jnp.float3...]
    ppermute x0 -> x48, starting transfers between devices: none -> 99 us  [the longest x20 70.6 us: onward(): return lax.ppermute(value, 'row', up + down)]
    dot_general x3 -> x0, matrix products: 82.1 us -> none  [the longest x1 28.9 us: on_device(): lax.dot_general(gathered, grad_full, (((0,), (0,)), ((), ())), preferred_...]
    ppermute x0 -> x48, waiting for transfers between devices: none -> 80.9 us  [the longest x20 51.5 us: onward(): return lax.ppermute(value, 'row', up + down)]
    unnamed x5 -> x117, local copies, waits for them, and re-layouts: 26.5 us -> 36.2 us
    optimization_barrier x0 -> x1, local copies, waits for them, and re-layouts: none -> 4.64 us  [fence(): lax.optimization_barrier([env[n] for n in names])]
  transfers between devices with their start and end apart: 4 -> 49, of which waited for: 3 -> 20; matrix products, arithmetic and copies ran while one was open for 13% -> 3% of each run, Pallas kernels for 0% -> 35%
where the time goes in v1:
time: 402 us; the launch traced here: 400 us
  Pallas kernels  155 us (39%)
  starting transfers between devices  99 us (25%)
  waiting for transfers between devices  80.9 us (20%)
  local copies, waits for them, and re-layouts  42 us (10%)
  between operations  14.9 us (4%)
  other arithmetic  7.51 us (2%)
    pallas_call x28, Pallas kernels, run(): pl.pallas_call(with_token, grid_spec=pltpu.PrefetchScalarGridSpec(num_sca...  155 us
    ppermute x20, starting transfers between devices, onward(): return lax.ppermute(value, 'row', up + down)  70.6 us
    ppermute x20, waiting for transfers between devices, onward(): return lax.ppermute(value, 'row', up + down)  51.5 us
    unnamed x117, local copies, waits for them, and re-layouts  36.2 us
    ppermute x7, waiting for transfers between devices, cross(): return lax.ppermute(value, 'col', [(c, c ^ offset) for c in range(4)])  24.8 us
    ppermute x21, starting transfers between devices, swap(): return lax.ppermute(value, 'row', [(r, r ^ 1) for r in range(n_row)])  17 us
    ppermute x7, starting transfers between devices, cross(): return lax.ppermute(value, 'col', [(c, c ^ offset) for c in range(4)])  11.4 us
  transfers between devices with their start and end apart: 49, of which 20 were waited for; matrix products, arithmetic and copies ran while one was open for 3% of the time, Pallas kernels for 35%

profile of v1, /device:TPU:0, one launch (start us, length us, event | category | flops | bytes accessed | tf_op | source)
XLA Modules:
  0.0 399.6 jit_solution(17486784775814131398)
XLA Ops:
  11.7 16.3 %collective-permute-done.1 = bf16[2,128,1536]{2,1,0:T(8,128)(2,1)S(1)} collective-permute-done((bf16[2,128,1536]{2,1,0:T(8,128)(2,1)}, bf16[2,128,1536]{2,1,0:T(8,128)(2,1)S(1)}, u32[]{:S(2)}, u32[]{:S(2)}) %collective-permute-start.1) | collective-permute-done | bytes 786464 | tf_op jit(solution)/shard_map/ppermute | solution.py:298
  32.1 6.4 %collective-permute-done.3 = bf16[128,1536]{1,0:T(8,128)(2,1)} collective-permute-done((bf16[128,1536]{1,0:T(8,128)(2,1)S(1)}, bf16[128,1536]{1,0:T(8,128)(2,1)}, u32[]{:S(2)}, u32[]{:S(2)}) %collective-permute-start.3) | collective-permute-done | bytes 393248 | tf_op jit(solution)/shard_map/ppermute | solution.py:298
  45.4 14.0 %forward.2 = (bf16[512,3072]{1,0:T(8,128)(2,1)}, bf16[512,3072]{1,0:T(8,128)(2,1)S(1)}, f32[8,128]{1,0:T(8,128)S(1)}) custom-call(bf16[1024,1536]{1,0:T(8,128)(2,1)} %bitcast.74, bf16[1536,6144]{1,0:T(8,128)(2,1)} %refs_1_.11, f32[8,128]{1,0:T(8,128)S(1)} %broadcast_in_dim.3.refs_2_), custom_call_target="tpu_custom_call" | custom-call | flops 9663676416 | bytes 18874368 | tf_op jit(solution)/shard_map/forward/pallas_call | solution.py:49
  59.4 15.2 %forward.3 = (bf16[512,3072]{1,0:T(8,128)(2,1)}, bf16[512,3072]{1,0:T(8,128)(2,1)S(1)}, f32[8,128]{1,0:T(8,128)S(1)}) custom-call(bf16[1024,1536]{1,0:T(8,128)(2,1)} %bitcast.75, bf16[1536,6144]{1,0:T(8,128)(2,1)} %refs_1_.11, f32[8,128]{1,0:T(8,128)S(1)} %get-tuple-element.146.refs_2_), custom_call_target="tpu_custom_call" | custom-call | flops 9663676416 | bytes 18874368 | tf_op jit(solution)/shard_map/forward/pallas_call | solution.py:49
  87.6 4.5 %collective-permute-done.6.refs_3_ = bf16[2,64,3072]{2,1,0:T(8,128)(2,1)} collective-permute-done((bf16[2,64,3072]{2,1,0:T(8,128)(2,1)}, bf16[2,64,3072]{2,1,0:T(8,128)(2,1)}, u32[]{:S(2)}, u32[]{:S(2)}) %collective-permute-start.6) | collective-permute-done | bytes 786464 | tf_op jit(solution)/shard_map/ppermute | solution.py:295
  121.0 5.2 %collective-permute-done.10.refs_3_ = bf16[2,64,3072]{2,1,0:T(8,128)(2,1)S(1)} collective-permute-done((bf16[2,64,3072]{2,1,0:T(8,128)(2,1)S(1)}, bf16[2,64,3072]{2,1,0:T(8,128)(2,1)S(1)}, u32[]{:S(2)}, u32[]{:S(2)}) %collective-permute-start.10) | collective-permute-done | bytes 786464 | tf_op jit(solution)/shard_map/ppermute | solution.py:295
  130.6 4.9 %gelu.4 = (bf16[2,64,3072]{2,1,0:T(8,128)(2,1)S(1)}, bf16[128,6144]{1,0:T(8,128)(2,1)}, f32[8,128]{1,0:T(8,128)S(1)}) custom-call(s32[1]{0:T(128)} %bitcast.refs_0_, bf16[4,2,64,3072]{3,2,1,0:T(8,128)(2,1)} %bitcast.15.refs_1_, bf16[4,2,64,3072]{3,2,1,0:T(8,128)(2,1)} %collective-permute-done.5.refs_2_, ...), custom_call_target="tpu_custom_call" | custom-call | tf_op jit(solution)/shard_map/gelu/pallas_call | solution.py:49
  135.6 4.5 %collective-permute-done.14.refs_3_ = bf16[2,64,3072]{2,1,0:T(8,128)(2,1)S(1)} collective-permute-done((bf16[2,64,3072]{2,1,0:T(8,128)(2,1)S(1)}, bf16[2,64,3072]{2,1,0:T(8,128)(2,1)S(1)}, u32[]{:S(2)}, u32[]{:S(2)}) %collective-permute-start.14) | collective-permute-done | bytes 786464 | tf_op jit(solution)/shard_map/ppermute | solution.py:295
  142.3 5.1 %gelu.5 = (bf16[2,64,3072]{2,1,0:T(8,128)(2,1)S(1)}, bf16[128,6144]{1,0:T(8,128)(2,1)}, f32[8,128]{1,0:T(8,128)S(1)}) custom-call(s32[1]{0:T(128)} %bitcast.refs_0_, bf16[4,2,64,3072]{3,2,1,0:T(8,128)(2,1)} %bitcast.19.refs_1_, bf16[4,2,64,3072]{3,2,1,0:T(8,128)(2,1)} %collective-permute-done.7.refs_2_, ...), custom_call_target="tpu_custom_call", output_to_operand_aliasing={{1}: (7, {})} | custom-call | tf_op jit(solution)/shard_map/gelu/pallas_call | solution.py:49
  155.2 6.2 %collective-permute-done.13.refs_3_.refs_2_ = bf16[2,64,3072]{2,1,0:T(8,128)(2,1)S(1)} collective-permute-done((bf16[2,64,3072]{2,1,0:T(8,128)(2,1)S(1)}, bf16[2,64,3072]{2,1,0:T(8,128)(2,1)S(1)}, u32[]{:S(2)}, u32[]{:S(2)}) %collective-permute-start.13) | collective-permute-done | bytes 786464 | tf_op jit(solution)/shard_map/ppermute | solution.py:295
  163.4 5.3 %collective-permute-start.21 = (bf16[2,64,3072]{2,1,0:T(8,128)(2,1)S(1)}, bf16[2,64,3072]{2,1,0:T(8,128)(2,1)}, u32[]{:S(2)}, u32[]{:S(2)}) collective-permute-start(bf16[2,64,3072]{2,1,0:T(8,128)(2,1)S(1)} %get-tuple-element.196), channel_id=1, source_target_pairs={{0,8},{8,16},{16,24},{28,20},{20,12},{12,4},{1,9},{9,17},{17,25},{... | collective-permute-start | bytes 2359304 | tf_op jit(solution)/shard_map/ppermute | solution.py:295
  172.2 5.3 %collective-permute-start.20 = (bf16[2,64,3072]{2,1,0:T(8,128)(2,1)}, bf16[2,64,3072]{2,1,0:T(8,128)(2,1)}, u32[]{:S(2)}, u32[]{:S(2)}) collective-permute-start(bf16[2,64,3072]{2,1,0:T(8,128)(2,1)} %get-tuple-element.195), channel_id=1, source_target_pairs={{0,8},{8,16},{16,24},{28,20},{20,12},{12,4},{1,9},{9,17},{17,25},{... | collective-permute-start | bytes 2359304 | tf_op jit(solution)/shard_map/ppermute | solution.py:295
  179.3 4.6 %copy.19 = bf16[1024,1536]{0,1:T(8,128)(2,1)} copy(bf16[1024,1536]{1,0:T(8,128)(2,1)} %bitcast.76) | data formatting | bytes 6291456 | tf_op jit(solution)/shard_map/optimization_barrier | solution.py:305
  214.6 7.0 %collective-permute-done.29.refs_3_ = bf16[2,64,3072]{2,1,0:T(8,128)(2,1)S(1)} collective-permute-done((bf16[2,64,3072]{2,1,0:T(8,128)(2,1)S(1)}, bf16[2,64,3072]{2,1,0:T(8,128)(2,1)S(1)}, u32[]{:S(2)}, u32[]{:S(2)}) %collective-permute-start.29) | collective-permute-done | bytes 786464 | tf_op jit(solution)/shard_map/ppermute | solution.py:295
  229.1 6.4 %collective-permute-done.28.refs_3_ = bf16[2,64,3072]{2,1,0:T(8,128)(2,1)S(1)} collective-permute-done((bf16[2,64,3072]{2,1,0:T(8,128)(2,1)S(1)}, bf16[2,64,3072]{2,1,0:T(8,128)(2,1)S(1)}, u32[]{:S(2)}, u32[]{:S(2)}) %collective-permute-start.28) | collective-permute-done | bytes 786464 | tf_op jit(solution)/shard_map/ppermute | solution.py:295
  243.0 6.3 %collective-permute-done.33.refs_2_ = bf16[2,64,3072]{2,1,0:T(8,128)(2,1)S(1)} collective-permute-done((bf16[2,64,3072]{2,1,0:T(8,128)(2,1)S(1)}, bf16[2,64,3072]{2,1,0:T(8,128)(2,1)S(1)}, u32[]{:S(2)}, u32[]{:S(2)}) %collective-permute-start.33) | collective-permute-done | bytes 786464 | tf_op jit(solution)/shard_map/ppermute | solution.py:295
  259.8 9.7 %input_grad.4 = (f32[512,1536]{1,0:T(8,128)S(1)}, f32[8,128]{1,0:T(8,128)S(1)}) custom-call(bf16[1024,3072]{1,0:T(8,128)(2,1)} %bitcast.56, bf16[1536,6144]{1,0:T(8,128)(2,1)} %refs_1_.11, f32[8,128]{1,0:T(8,128)S(1)} %get-tuple-element.237.refs_2_), custom_call_target="tpu_custom_call" | custom-call | flops 4831838208 | bytes 18874368 | tf_op jit(solution)/shard_map/input_grad/pallas_call | solution.py:49
  277.1 9.5 %input_grad.5 = (f32[512,1536]{1,0:T(8,128)S(1)}, f32[8,128]{1,0:T(8,128)S(1)}) custom-call(bf16[1024,3072]{1,0:T(8,128)(2,1)} %bitcast.53, bf16[1536,6144]{1,0:T(8,128)(2,1)} %refs_1_.11, f32[8,128]{1,0:T(8,128)S(1)} %get-tuple-element.251.refs_2_), custom_call_target="tpu_custom_call" | custom-call | flops 4831838208 | bytes 18874368 | tf_op jit(solution)/shard_map/input_grad/pallas_call | solution.py:49
  294.1 8.6 %collective-permute-start.42 = (bf16[2,64,3072]{2,1,0:T(8,128)(2,1)}, bf16[2,64,3072]{2,1,0:T(8,128)(2,1)S(1)}, u32[]{:S(2)}, u32[]{:S(2)}) collective-permute-start(bf16[2,64,3072]{2,1,0:T(8,128)(2,1)} %collective-permute-done.36.refs_3_), channel_id=1, source_target_pairs={{0,4},{4,0},{8,12},{12,8},{16,20},{20,16},{24,28},{28,24},{1,5},{5... | collective-permute-start | bytes 2359304 | tf_op jit(solution)/shard_map/ppermute | solution.py:290
  305.7 5.4 %collective-permute-start.43 = (bf16[2,64,3072]{2,1,0:T(8,128)(2,1)}, bf16[2,64,3072]{2,1,0:T(8,128)(2,1)}, u32[]{:S(2)}, u32[]{:S(2)}) collective-permute-start(bf16[2,64,3072]{2,1,0:T(8,128)(2,1)} %collective-permute-done.41.refs_4_), channel_id=1, source_target_pairs={{0,4},{4,0},{8,12},{12,8},{16,20},{20,16},{24,28},{28,24},{1,5},{5... | collective-permute-start | bytes 2359304 | tf_op jit(solution)/shard_map/ppermute | solution.py:290
  327.7 9.7 %input_grad.6 = (f32[512,1536]{1,0:T(8,128)S(1)}, f32[8,128]{1,0:T(8,128)S(1)}) custom-call(bf16[1024,3072]{1,0:T(8,128)(2,1)} %bitcast.57, bf16[1536,6144]{1,0:T(8,128)(2,1)} %refs_1_.11, f32[8,128]{1,0:T(8,128)S(1)} %get-tuple-element.266.refs_2_), custom_call_target="tpu_custom_call" | custom-call | flops 4831838208 | bytes 18874368 | tf_op jit(solution)/shard_map/input_grad/pallas_call | solution.py:49
  350.4 9.8 %input_grad.7 = (bf16[512,1536]{1,0:T(8,128)(2,1)S(1)}, f32[8,128]{1,0:T(8,128)S(1)}) custom-call(bf16[1024,3072]{1,0:T(8,128)(2,1)} %bitcast.54, bf16[1536,6144]{1,0:T(8,128)(2,1)} %refs_1_.11, f32[512,1536]{1,0:T(8,128)S(1)} %copy-done.27, f32[8,128]{1,0:T(8,128)S(1)} %get-tuple-element.275.refs_3_), custom_call_target="tpu_custom_call" | custom-call | flops 4831838208 | bytes 18874368 | tf_op jit(solution)/shard_map/input_grad/pallas_call | solution.py:49
  363.9 13.3 %weight_grad.2 = (bf16[1536,6144]{1,0:T(8,128)(2,1)}, f32[8,128]{1,0:T(8,128)S(1)}) custom-call(bf16[1536,1024]{1,0:T(8,128)(2,1)S(1)} %bitcast.69, bf16[1024,3072]{1,0:T(8,128)(2,1)} %bitcast.58, f32[8,128]{1,0:T(8,128)S(1)} %get-tuple-element.279.refs_2_), custom_call_target="tpu_custom_call" | custom-call | flops 9663676416 | bytes 18874368 | tf_op jit(solution)/shard_map/weight_grad/pallas_call | solution.py:49
  377.2 13.3 %weight_grad.3 = (bf16[1536,6144]{1,0:T(8,128)(2,1)}, f32[8,128]{1,0:T(8,128)}) custom-call(bf16[1536,1024]{1,0:T(8,128)(2,1)S(1)} %bitcast.70, bf16[1024,3072]{1,0:T(8,128)(2,1)} %bitcast.55, bf16[1536,6144]{1,0:T(8,128)(2,1)} %get-tuple-element.280.refs_2_, f32[8,128]{1,0:T(8,128)S(1)} %get-tuple-element.281.refs_3_), custom_call_target="tpu_custom_call", output_to_operand_aliasing={{0}: (2, {})} | custom-call | flops 9663676416 | bytes 18874368 | tf_op jit(solution)/shard_map/weight_grad/pallas_call | solution.py:49
  (236 shorter events, 188.2 us)
Async XLA Ops:
  7.2 383.6 %reduce-scatter.4.cloned.1.call-start = ((), (), s32[]{:S(2)}) async-start(), calls=%async_computation.1 | async-start | bytes 1966080
  7.2 20.8 %collective-permute-start.1 = (bf16[2,128,1536]{2,1,0:T(8,128)(2,1)}, bf16[2,128,1536]{2,1,0:T(8,128)(2,1)S(1)}, u32[]{:S(2)}, u32[]{:S(2)}) collective-permute-start(bf16[2,128,1536]{2,1,0:T(8,128)(2,1)} %bitcast.79), channel_id=1, source_target_pairs={{0,2},{1,3},{2,0},{3,1},{4,6},{5,7},{6,4},{7,5},{8,10},{9,11},{10,... | collective-permute-start | bytes 2359304 | tf_op jit(solution)/shard_map/ppermute | solution.py:298
  10.2 19.6 %collective-permute-start = (bf16[2,128,1536]{2,1,0:T(8,128)(2,1)}, bf16[2,128,1536]{2,1,0:T(8,128)(2,1)S(1)}, u32[]{:S(2)}, u32[]{:S(2)}) collective-permute-start(bf16[2,128,1536]{2,1,0:T(8,128)(2,1)} %bitcast.80), channel_id=1, source_target_pairs={{0,1},{1,0},{2,3},{3,2},{4,5},{5,4},{6,7},{7,6},{8,9},{9,8},{10,11... | collective-permute-start | bytes 2359304 | tf_op jit(solution)/shard_map/ppermute | solution.py:298
  59.4 15.2 %collective-permute-start.5 = (bf16[4,2,64,3072]{3,2,1,0:T(8,128)(2,1)}, bf16[4,2,64,3072]{3,2,1,0:T(8,128)(2,1)}, u32[]{:S(2)}, u32[]{:S(2)}) collective-permute-start(bf16[4,2,64,3072]{3,2,1,0:T(8,128)(2,1)} %bitcast.15.refs_1_), channel_id=1, source_target_pairs={{0,4},{4,0},{8,12},{12,8},{16,20},{20,16},{24,28},{28,24},{1,5},{5... | collective-permute-start | bytes 9437192 | tf_op jit(solution)/shard_map/ppermute | solution.py:290
  86.2 14.2 %collective-permute-start.9 = (bf16[2,64,3072]{2,1,0:T(8,128)(2,1)S(1)}, bf16[2,64,3072]{2,1,0:T(8,128)(2,1)S(1)}, u32[]{:S(2)}, u32[]{:S(2)}) collective-permute-start(bf16[2,64,3072]{2,1,0:T(8,128)(2,1)S(1)} %get-tuple-element.160), channel_id=1, source_target_pairs={{0,8},{28,20},{1,9},{29,21},{2,10},{30,22},{3,11},{31,23}} | collective-permute-start | bytes 2359304 | tf_op jit(solution)/shard_map/ppermute | solution.py:295
  103.5 14.1 %collective-permute-start.11 = (bf16[2,64,3072]{2,1,0:T(8,128)(2,1)S(1)}, bf16[2,64,3072]{2,1,0:T(8,128)(2,1)S(1)}, u32[]{:S(2)}, u32[]{:S(2)}) collective-permute-start(bf16[2,64,3072]{2,1,0:T(8,128)(2,1)S(1)} %get-tuple-element.168), channel_id=1, source_target_pairs={{0,8},{8,16},{28,20},{20,12},{1,9},{9,17},{29,21},{21,13},{2,10},{... | collective-permute-start | bytes 2359304 | tf_op jit(solution)/shard_map/ppermute | solution.py:295
  112.3 13.9 %collective-permute-start.10 = (bf16[2,64,3072]{2,1,0:T(8,128)(2,1)S(1)}, bf16[2,64,3072]{2,1,0:T(8,128)(2,1)S(1)}, u32[]{:S(2)}, u32[]{:S(2)}) collective-permute-start(bf16[2,64,3072]{2,1,0:T(8,128)(2,1)S(1)} %get-tuple-element.167), channel_id=1, source_target_pairs={{0,8},{8,16},{16,24},{28,20},{20,12},{12,4},{1,9},{9,17},{17,25},{... | collective-permute-start | bytes 2359304 | tf_op jit(solution)/shard_map/ppermute | solution.py:295
  140.1 15.1 %collective-permute-start.17 = (bf16[4,2,64,3072]{3,2,1,0:T(8,128)(2,1)S(1)}, bf16[4,2,64,3072]{3,2,1,0:T(8,128)(2,1)S(1)}, u32[]{:S(2)}, u32[]{:S(2)}) collective-permute-start(bf16[4,2,64,3072]{3,2,1,0:T(8,128)(2,1)S(1)} %bitcast.59), channel_id=1, source_target_pairs={{0,4},{4,0},{8,12},{12,8},{16,20},{20,16},{24,28},{28,24},{1,5},{5... | collective-permute-start | bytes 9437192 | tf_op jit(solution)/shard_map/ppermute | solution.py:290
  147.4 14.0 %collective-permute-start.16 = (bf16[4,2,64,3072]{3,2,1,0:T(8,128)(2,1)S(1)}, bf16[4,2,64,3072]{3,2,1,0:T(8,128)(2,1)S(1)}, u32[]{:S(2)}, u32[]{:S(2)}) collective-permute-start(bf16[4,2,64,3072]{3,2,1,0:T(8,128)(2,1)S(1)} %bitcast.64), channel_id=1, source_target_pairs={{0,4},{4,0},{8,12},{12,8},{16,20},{20,16},{24,28},{28,24},{1,5},{5... | collective-permute-start | bytes 9437192 | tf_op jit(solution)/shard_map/ppermute | solution.py:290
  152.0 17.9 %collective-permute-start.18 = (bf16[2,64,3072]{2,1,0:T(8,128)(2,1)S(1)}, bf16[2,64,3072]{2,1,0:T(8,128)(2,1)S(1)}, u32[]{:S(2)}, u32[]{:S(2)}) collective-permute-start(bf16[2,64,3072]{2,1,0:T(8,128)(2,1)S(1)} %get-tuple-element.185.refs_1_), channel_id=1, source_target_pairs={{0,8},{8,16},{16,24},{28,20},{20,12},{12,4},{1,9},{9,17},{17,25},{... | collective-permute-start | bytes 2359304 | tf_op jit(solution)/shard_map/ppermute | solution.py:295
  163.4 14.8 %collective-permute-start.21 = (bf16[2,64,3072]{2,1,0:T(8,128)(2,1)S(1)}, bf16[2,64,3072]{2,1,0:T(8,128)(2,1)}, u32[]{:S(2)}, u32[]{:S(2)}) collective-permute-start(bf16[2,64,3072]{2,1,0:T(8,128)(2,1)S(1)} %get-tuple-element.196), channel_id=1, source_target_pairs={{0,8},{8,16},{16,24},{28,20},{20,12},{12,4},{1,9},{9,17},{17,25},{... | collective-permute-start | bytes 2359304 | tf_op jit(solution)/shard_map/ppermute | solution.py:295
  172.2 23.1 %collective-permute-start.20 = (bf16[2,64,3072]{2,1,0:T(8,128)(2,1)}, bf16[2,64,3072]{2,1,0:T(8,128)(2,1)}, u32[]{:S(2)}, u32[]{:S(2)}) collective-permute-start(bf16[2,64,3072]{2,1,0:T(8,128)(2,1)} %get-tuple-element.195), channel_id=1, source_target_pairs={{0,8},{8,16},{16,24},{28,20},{20,12},{12,4},{1,9},{9,17},{17,25},{... | collective-permute-start | bytes 2359304 | tf_op jit(solution)/shard_map/ppermute | solution.py:295
  179.2 16.2 %collective-permute-start.23 = (bf16[2,64,3072]{2,1,0:T(8,128)(2,1)}, bf16[2,64,3072]{2,1,0:T(8,128)(2,1)}, u32[]{:S(2)}, u32[]{:S(2)}) collective-permute-start(bf16[2,64,3072]{2,1,0:T(8,128)(2,1)} %collective-permute-done.21.refs_3_), channel_id=1, source_target_pairs={{0,4},{4,0},{8,12},{12,8},{16,20},{20,16},{24,28},{28,24},{1,5},{5... | collective-permute-start | bytes 2359304 | tf_op jit(solution)/shard_map/ppermute | solution.py:290
  190.9 13.9 %collective-permute-start.25 = (bf16[2,64,3072]{2,1,0:T(8,128)(2,1)S(1)}, bf16[2,64,3072]{2,1,0:T(8,128)(2,1)S(1)}, u32[]{:S(2)}, u32[]{:S(2)}) collective-permute-start(bf16[2,64,3072]{2,1,0:T(8,128)(2,1)S(1)} %get-tuple-element.208), channel_id=1, source_target_pairs={{0,8},{8,16},{16,24},{28,20},{20,12},{12,4},{1,9},{9,17},{17,25},{... | collective-permute-start | bytes 2359304 | tf_op jit(solution)/shard_map/ppermute | solution.py:295
  198.3 14.9 %collective-permute-start.24 = (bf16[2,64,3072]{2,1,0:T(8,128)(2,1)S(1)}, bf16[2,64,3072]{2,1,0:T(8,128)(2,1)S(1)}, u32[]{:S(2)}, u32[]{:S(2)}) collective-permute-start(bf16[2,64,3072]{2,1,0:T(8,128)(2,1)S(1)} %get-tuple-element.207), channel_id=1, source_target_pairs={{0,8},{8,16},{16,24},{28,20},{20,12},{12,4},{1,9},{9,17},{17,25},{... | collective-permute-start | bytes 2359304 | tf_op jit(solution)/shard_map/ppermute | solution.py:295
  206.1 15.5 %collective-permute-start.29 = (bf16[2,64,3072]{2,1,0:T(8,128)(2,1)S(1)}, bf16[2,64,3072]{2,1,0:T(8,128)(2,1)S(1)}, u32[]{:S(2)}, u32[]{:S(2)}) collective-permute-start(bf16[2,64,3072]{2,1,0:T(8,128)(2,1)S(1)} %get-tuple-element.216), channel_id=1, source_target_pairs={{0,8},{8,16},{16,24},{28,20},{20,12},{12,4},{1,9},{9,17},{17,25},{... | collective-permute-start | bytes 2359304 | tf_op jit(solution)/shard_map/ppermute | solution.py:295
  249.4 21.0 %collective-permute-start.34 = (bf16[2,64,3072]{2,1,0:T(8,128)(2,1)S(1)}, bf16[2,64,3072]{2,1,0:T(8,128)(2,1)S(1)}, u32[]{:S(2)}, u32[]{:S(2)}) collective-permute-start(bf16[2,64,3072]{2,1,0:T(8,128)(2,1)S(1)} %get-tuple-element.241.refs_1_), channel_id=1, source_target_pairs={{0,8},{8,16},{16,24},{28,20},{20,12},{12,4},{1,9},{9,17},{17,25},{... | collective-permute-start | bytes 2359304 | tf_op jit(solution)/shard_map/ppermute | solution.py:295
  253.8 16.6 %collective-permute-start.35 = (bf16[2,64,3072]{2,1,0:T(8,128)(2,1)S(1)}, bf16[2,64,3072]{2,1,0:T(8,128)(2,1)S(1)}, u32[]{:S(2)}, u32[]{:S(2)}) collective-permute-start(bf16[2,64,3072]{2,1,0:T(8,128)(2,1)S(1)} %collective-permute-done.33.refs_2_), channel_id=1, source_target_pairs={{0,4},{4,0},{8,12},{12,8},{16,20},{20,16},{24,28},{28,24},{1,5},{5... | collective-permute-start | bytes 2359304 | tf_op jit(solution)/shard_map/ppermute | solution.py:290
  269.5 20.3 %collective-permute-start.37 = (bf16[2,64,3072]{2,1,0:T(8,128)(2,1)S(1)}, bf16[2,64,3072]{2,1,0:T(8,128)(2,1)S(1)}, u32[]{:S(2)}, u32[]{:S(2)}) collective-permute-start(bf16[2,64,3072]{2,1,0:T(8,128)(2,1)S(1)} %collective-permute-done.33.refs_2_), channel_id=1, source_target_pairs={{8,16},{16,24},{20,12},{12,4},{9,17},{17,25},{21,13},{13,5},{10,18... | collective-permute-start | bytes 2359304 | tf_op jit(solution)/shard_map/ppermute | solution.py:295
  270.5 19.4 %collective-permute-start.38 = (bf16[2,64,3072]{2,1,0:T(8,128)(2,1)S(1)}, bf16[2,64,3072]{2,1,0:T(8,128)(2,1)S(1)}, u32[]{:S(2)}, u32[]{:S(2)}) collective-permute-start(bf16[2,64,3072]{2,1,0:T(8,128)(2,1)S(1)} %collective-permute-done.34.refs_2_), channel_id=1, source_target_pairs={{0,4},{4,0},{8,12},{12,8},{16,20},{20,16},{24,28},{28,24},{1,5},{5... | collective-permute-start | bytes 2359304 | tf_op jit(solution)/shard_map/ppermute | solution.py:290
  311.1 26.3 %collective-permute-start.40 = (bf16[2,64,3072]{2,1,0:T(8,128)(2,1)}, bf16[2,64,3072]{2,1,0:T(8,128)(2,1)}, u32[]{:S(2)}, u32[]{:S(2)}) collective-permute-start(bf16[2,64,3072]{2,1,0:T(8,128)(2,1)} %collective-permute-done.36.refs_3_), channel_id=1, source_target_pairs={{16,24},{12,4},{17,25},{13,5},{18,26},{14,6},{19,27},{15,7}} | collective-permute-start | bytes 2359304 | tf_op jit(solution)/shard_map/ppermute | solution.py:295
  360.4 30.2 %collective-permute-start.45 = (bf16[2,64,1536]{2,1,0:T(8,128)(2,1)S(1)}, bf16[2,64,1536]{2,1,0:T(8,128)(2,1)S(1)}, u32[]{:S(2)}, u32[]{:S(2)}) collective-permute-start(bf16[2,64,1536]{2,1,0:T(8,128)(2,1)S(1)} %get-tuple-element.287), channel_id=1, source_target_pairs={{0,1},{1,0},{2,3},{3,2},{4,5},{5,4},{6,7},{7,6},{8,9},{9,8},{10,11... | collective-permute-start | bytes 1179656 | tf_op jit(solution)/shard_map/ppermute | solution.py:298
  361.5 29.0 %collective-permute-start.47 = (bf16[2,64,1536]{2,1,0:T(8,128)(2,1)S(1)}, bf16[2,64,1536]{2,1,0:T(8,128)(2,1)S(1)}, u32[]{:S(2)}, u32[]{:S(2)}) collective-permute-start(bf16[2,64,1536]{2,1,0:T(8,128)(2,1)S(1)} %get-tuple-element.288), channel_id=1, source_target_pairs={{0,3},{1,2},{2,1},{3,0},{4,7},{5,6},{6,5},{7,4},{8,11},{9,10},{10,... | collective-permute-start | bytes 1179656 | tf_op jit(solution)/shard_map/ppermute | solution.py:298
  363.4 27.1 %collective-permute-start.46 = (bf16[2,64,1536]{2,1,0:T(8,128)(2,1)S(1)}, bf16[2,64,1536]{2,1,0:T(8,128)(2,1)S(1)}, u32[]{:S(2)}, u32[]{:S(2)}) collective-permute-start(bf16[2,64,1536]{2,1,0:T(8,128)(2,1)S(1)} %get-tuple-element.289), channel_id=1, source_target_pairs={{0,2},{1,3},{2,0},{3,1},{4,6},{5,7},{6,4},{7,5},{8,10},{9,11},{10,... | collective-permute-start | bytes 1179656 | tf_op jit(solution)/shard_map/ppermute | solution.py:298
  (80 other events, 612.2 us)
Sparse Core Ops, SparseCore 0:
  341.0 35.1 reduce-scatter.3

commit v2 on v1

v2 whole, which is shorter than its diff:
```python
import math

import jax
import jax.numpy as jnp
from jax import lax
from jax.experimental import pallas as pl
from jax.experimental.pallas import tpu as pltpu
from jax.sharding import PartitionSpec as P

BF16 = jnp.bfloat16
F32 = jnp.float32
CORES = 2
CHUNKS = 2
STREAMS = 2
HALVES = 2


def gelu_and_slope(value):
    below = 0.5 * (1.0 + lax.erf(value / math.sqrt(2.0)))
    density = jnp.exp(-0.5 * value * value) / math.sqrt(2.0 * math.pi)
    return value * below, below + value * density


def tile(extent, limit):
    best = 128
    for size in range(128, min(extent, limit) + 1, 128):
        if extent % size == 0:
            best = size
    return best


def matmul_call(body, name, grid, flops, moved, vmem=28, **spec):
    if grid is not None:
        spec["grid"] = grid
    return pl.pallas_call(
        body,
        compiler_params=pltpu.CompilerParams(vmem_limit_bytes=vmem * 2**20),
        cost_estimate=pl.CostEstimate(flops=flops, bytes_accessed=moved, transcendentals=0),
        name=name,
        **spec,
    )


def forward_matmul(x, weight, chunk, f):
    rows, width = x.shape
    bn = tile(f, 512)
    steps = f // bn

    def body(x_ref, w_ref, out):
        out[...] = jnp.dot(x_ref[...], w_ref[...], preferred_element_type=F32).astype(BF16)

    return matmul_call(
        body,
        "forward",
        (steps,),
        2 * rows * width * f,
        2 * (rows * width + width * f + rows * f),
        vmem=47,
        in_specs=[
            pl.BlockSpec((rows, width), lambda j: (0, 0)),
            pl.BlockSpec((width, bn), lambda j: (0, chunk * steps + j)),
        ],
        out_specs=pl.BlockSpec((rows, bn), lambda j: (0, j)),
        out_shape=jax.ShapeDtypeStruct((rows, f), BF16),
    )(x, weight)


def input_grad_matmul(g, weight, chunk, total, last):
    rows, f = g.shape
    width = weight.shape[0]
    bn = tile(width, 256)
    kept = [] if total is None else [total]

    def body(g_ref, w_ref, *rest):
        part = lax.dot_general(
            g_ref[...], w_ref[...], (((1,), (1,)), ((), ())), preferred_element_type=F32
        )
        if kept:
            part += rest[0][...]
        rest[-1][...] = part.astype(rest[-1].dtype)

    return matmul_call(
        body,
        "input_grad",
        (width // bn,),
        2 * rows * width * f,
        2 * (rows * f + width * f + 4 * rows * width),
        vmem=47,
        in_specs=[
            pl.BlockSpec((rows, f), lambda j: (0, 0)),
            pl.BlockSpec((bn, f), lambda j: (j, chunk)),
        ]
        + [pl.BlockSpec((rows, bn), lambda j: (0, j))] * len(kept),
        out_specs=pl.BlockSpec((rows, bn), lambda j: (0, j)),
        out_shape=jax.ShapeDtypeStruct((rows, width), BF16 if last else F32),
    )(g, weight, *kept)


def weight_grad_matmul(lefts, rights, buffer, chunk, units):
    width, rows = lefts[0].shape
    f = rights[0].shape[1]
    bn = tile(f, 512)
    steps = f // bn
    n = len(lefts)
    kept = [] if buffer is None else [buffer]

    def body(*refs):
        total = jnp.dot(refs[0][...], refs[n][...], preferred_element_type=F32)
        for i in range(1, n):
            total += jnp.dot(refs[i][...], refs[n + i][...], preferred_element_type=F32)
        refs[-1][...] = total.astype(BF16)

    return matmul_call(
        body,
        "weight_grad",
        (steps,),
        2 * n * rows * width * f,
        2 * (n * rows * width + n * rows * f + width * f),
        vmem=56,
        in_specs=[pl.BlockSpec((width, rows), lambda j: (0, 0))] * n
        + [pl.BlockSpec((rows, bn), lambda j: (0, j))] * n
        + [pl.BlockSpec(memory_space=pl.ANY)] * len(kept),
        out_specs=pl.BlockSpec((width, bn), lambda j: (0, chunk * steps + j)),
        out_shape=jax.ShapeDtypeStruct((width, units), BF16),
        input_output_aliases={2 * n: 0} if kept else {},
    )(*lefts, *rights, *kept)


def message_kernel(where, part, theirs, came, keep):
    _, cores, few, f = part.shape
    bn = tile(f, 1536)

    def body(where_ref, part_ref, theirs_ref, *rest):
        out = rest[-1]
        mine = part_ref[0].astype(F32) + theirs_ref[0].astype(F32)
        if came is not None:
            here = rest[0][...].astype(F32)
            summing = where_ref[1] > 0
            mine = jnp.where(summing, mine, here if keep else 0.0)
            if not keep:
                mine += here
        out[...] = mine.astype(BF16)

    block = pl.BlockSpec((1, cores, few, bn), lambda j, where: (where[0], 0, 0, j))
    flat = pl.BlockSpec((cores, few, bn), lambda j, where: (0, 0, j))
    given = [] if came is None else [came]
    return matmul_call(
        body,
        "message",
        None,
        0,
        0,
        grid_spec=pltpu.PrefetchScalarGridSpec(
            num_scalar_prefetch=1,
            grid=(f // bn,),
            in_specs=[block, block] + [flat] * len(given),
            out_specs=flat,
        ),
        out_shape=jax.ShapeDtypeStruct((cores, few, f), BF16),
    )(where, part, theirs, *given)


def gelu_kernel(core, part, theirs, came, came_there, cotangent, cotangent_there, half, chunk, kept):
    _, cores, few, f = part.shape
    bn = tile(f, 512)
    steps = f // bn
    kept = [] if kept is None else [kept]

    def body(core_ref, part_ref, theirs_ref, came_ref, there_ref, mine_ref, other_ref, *rest):
        slope, activated = rest[-2:]
        first = core_ref[0] == 0
        values = []
        for c in range(cores):
            pre = part_ref[0, c].astype(F32) + theirs_ref[0, c].astype(F32)
            pre = pre + came_ref[c].astype(F32) + there_ref[c].astype(F32)
            value, grad = gelu_and_slope(pre)
            values.append(value)
            mine, other = mine_ref[...].astype(F32), other_ref[...].astype(F32)
            cot = jnp.where(first == (c == 0), mine, other)
            slope[c] = (cot * grad).astype(BF16)
        activated[...] = jnp.where(first, values[0], values[1]).astype(BF16)

    block = pl.BlockSpec((1, cores, few, bn), lambda j, core: (0, 0, 0, j))
    flat = pl.BlockSpec((cores, few, bn), lambda j, core: (0, 0, j))
    rows = pl.BlockSpec((few, bn), lambda j, core: (half, chunk * steps + j))
    return matmul_call(
        body,
        "gelu",
        None,
        0,
        0,
        grid_spec=pltpu.PrefetchScalarGridSpec(
            num_scalar_prefetch=1,
            grid=(steps,),
            in_specs=[block, block, flat, flat, rows, rows]
            + [pl.BlockSpec(memory_space=pl.ANY)] * len(kept),
            out_specs=[flat, rows],
        ),
        out_shape=[
            jax.ShapeDtypeStruct((cores, few, f), BF16),
            jax.ShapeDtypeStruct(cotangent.shape, BF16),
        ],
        input_output_aliases={7: 1} if kept else {},
    )(core, part, theirs, came, came_there, cotangent, cotangent_there, *kept)


def collect_kernel(place, slope, mine, theirs, depth):
    cores, few, f = slope.shape
    bn = tile(f, 1024)

    def body(place_ref, *refs):
        slope_ref, out = refs[0], refs[-1]
        mine_refs, their_refs = refs[1:depth], refs[depth : 2 * depth - 1]
        z, core = place_ref[0], place_ref[1]
        out[0] = slope_ref[...]
        for j in range(1, depth):
            above = z + j < depth
            here = above == (core == 1)
            for down in (True, False):
                step = j if down else depth - j
                side = above if down else jnp.logical_not(above)

                @pl.when(side & here)
                def _():
                    out[j] = mine_refs[step - 1][...]

                @pl.when(side & jnp.logical_not(here))
                def _():
                    out[j] = their_refs[step - 1][...]

    flat = pl.BlockSpec((cores, few, bn), lambda j, place: (0, 0, j))
    return matmul_call(
        body,
        "collect",
        None,
        0,
        0,
        vmem=56,
        grid_spec=pltpu.PrefetchScalarGridSpec(
            num_scalar_prefetch=1,
            grid=(f // bn,),
            in_specs=[flat] * (2 * depth - 1),
            out_specs=pl.BlockSpec((depth, cores, few, bn), lambda j, place: (0, 0, 0, j)),
        ),
        out_shape=jax.ShapeDtypeStruct((depth, *slope.shape), BF16),
    )(place, slope, *mine, *theirs)


def on_device(tokens, weight, cotangent):
    n_row, n_col = lax.axis_size("row"), lax.axis_size("col")
    depth = n_row // CORES
    row, col = lax.axis_index("row"), lax.axis_index("col")
    z, core = row // CORES, row % CORES
    place = jnp.where(core == 0, z, depth - 1 - z)
    width, units = weight.shape
    share = cotangent.shape[0]
    few = share // HALVES
    f = units // CHUNKS
    square = n_col == 4 and depth == 4

    def swap(value):
        return lax.ppermute(value, "row", [(r, r ^ 1) for r in range(n_row)])

    def onward(value, places):
        up = [(p * CORES, (p + 1) * CORES) for p in places]
        down = [((depth - 1 - p) * CORES + 1, (depth - 2 - p) * CORES + 1) for p in places]
        return lax.ppermute(value, "row", up + down)

    def cross(value, offset):
        return lax.ppermute(value, "col", [(c, c ^ offset) for c in range(4)])

    env = {"tokens": tokens, "cotangent": cotangent}

    def fence(*names):
        names = list(dict.fromkeys(n for n in names if n in env))
        for name, value in zip(names, lax.optimization_barrier([env[n] for n in names])):
            env[name] = value

    def gather_near(half):
        mine = env["tokens"].reshape(-1, share, width)[:, half * few : (half + 1) * few]
        env["mine"] = mine
        if square:
            env["by_x"], env["by_y"] = cross(mine, 1), cross(mine, 2)
        else:
            env["all"] = lax.all_gather(mine, "col", axis=0, tiled=True)

    def gather_far():
        if square:
            env["far_x"], env["far_y"] = cross(env["by_x"][0], 2), cross(env["by_y"][1], 1)

    def gather_end(half):
        if square:
            far = jnp.stack([env["far_x"], env["far_y"]])
            held = jnp.stack([env["mine"], env["by_x"], env["by_y"], far])
            order = [col ^ ((z + j) % depth) for j in range(depth)]
        else:
            held = env["all"].reshape(depth, CORES, few, width)
            order = [(z + j) % depth for j in range(depth)]
        blocks = [lax.dynamic_index_in_dim(held, b, 0, keepdims=False) for b in order]
        env["x", half] = jnp.concatenate(blocks).reshape(n_row * few, width)

    def columns_of(chunk):
        return slice(chunk * f, (chunk + 1) * f)

    sequence = [(half, chunk) for half in range(HALVES) for chunk in range(CHUNKS)]
    items = [sequence[q::STREAMS] for q in range(STREAMS)]
    count = len(sequence) // STREAMS
    steps = [(i, t) for i in range(count) for t in range(depth)]
    steps += [(count, t) for t in range(depth - 2)]

    input_grad, seen, done, pending = {}, {}, [], []

    def forward(q, i):
        half, chunk = items[q][i]
        part = forward_matmul(env["x", half], weight, chunk, f)
        env["part", q, i] = part.reshape(depth, CORES, few, f)
        env["theirs", q, i] = swap(env["part", q, i])
        done.append(("part", q, i))

    def transpose(half):
        env["x_t", half] = env["x", half].T
        done.append(("x_t", half))

    def backward_input(q, i):
        half, chunk = items[q][i]
        collect(q, i)
        seen["total", half] = seen.get(("total", half), 0) + 1
        last = seen["total", half] == CHUNKS
        env["total", half] = input_grad_matmul(
            env["g", half, chunk], weight, chunk, env.get(("total", half)), last
        )
        done.append(("total", half))

    def backward_weight(chunk):
        halves = range(HALVES)
        env["weight_grad"] = weight_grad_matmul(
            [env["x_t", h] for h in halves],
            [env["g", h, chunk] for h in halves],
            env.get("weight_grad"),
            chunk,
            units,
        )

    def scatter_input(half):
        pair = env["total", half].reshape(depth, CORES, few, width)
        if square:
            blocks = []
            for offset in range(4):
                at = ((col ^ offset) + depth - z) % depth
                block = lax.dynamic_index_in_dim(pair, at, 0, keepdims=False)
                blocks.append(cross(block, offset) if offset else block)
            input_grad[half] = sum(b.astype(F32) for b in blocks).astype(BF16)
        else:
            pair = lax.dynamic_slice(
                jnp.concatenate([pair, pair]), ((depth - z) % depth, 0, 0, 0), pair.shape
            )
            total = lax.psum_scatter(
                pair.reshape(n_col, -1, few, width), "col", scatter_dimension=0, tiled=True
            )
            input_grad[half] = total[0]

    core_there = core.astype(jnp.int32).reshape(1)
    place_there = jnp.stack([z, core]).astype(jnp.int32)

    def gelu(q, i):
        half, chunk = items[q][i]
        env["slope", q], env["activated"] = gelu_kernel(
            core_there,
            env["part", q, i],
            env["theirs", q, i],
            env["came", q],
            env["came_there", q],
            cotangent,
            env["cotangent_there"],
            half,
            chunk,
            env.get("activated"),
        )

    def collect(q, i):
        half, chunk = items[q][i]
        order = range(1, depth)
        g = collect_kernel(
            place_there,
            env["slope", q],
            [env["got", q, j] for j in order],
            [env["got_there", q, j] for j in order],
            depth,
        )
        env["g", half, chunk] = g.reshape(n_row * few, f)

    def message(q, step):
        i, t = steps[step]
        if t == depth - 1:
            env["msg", q] = env["slope", q]
        elif i == count:
            env["msg", q] = env["came", q]
        else:
            at = jnp.where(core == 0, depth - 1 - t, t + 1)
            env["msg", q] = message_kernel(
                jnp.stack([at, place <= t]).astype(jnp.int32),
                env["part", q, i],
                env["theirs", q, i],
                None if i == 0 and t == 0 else env["came", q],
                t == 0,
            )

    def start(q, step):
        i, t = steps[step]
        first = t + 1 if i == count else 0
        last = t + 1 if (i == 0 and t < depth - 2) else depth - 1
        env["came", q] = onward(env["msg", q], range(first, last))

    def receive(q, t):
        env["got", q, t] = env["came", q]
        env["got_there", q, t] = swap(env["came", q])
        pending.append(("got_there", q, t))

    gather_near(0)
    gather_far()
    gather_end(0)
    for q in range(STREAMS):
        forward(q, 0)
    for q in range(STREAMS):
        message(q, 0)
        fence(("msg", q), ("x", 0), "tokens", "cotangent")
        start(q, 0)
    done.clear()
    pending.clear()
    for step in range(len(steps)):
        i, t = steps[step]
        for q in range(STREAMS):
            fence(("came", q), *done, *pending, *(["tokens", "cotangent"] if step == 0 and q == 0 else []))
            done.clear()
            pending.clear()
            if t == depth - 2:
                env["came_there", q] = swap(env["came", q])
                gelu(q, i)
            elif t == depth - 1:
                receive(q, 1)
            elif i > 0:
                receive(q, t + 2)
            work = []
            if step + 1 < len(steps):
                message(q, step + 1)
                i_next, t_next = steps[step + 1]
                if t_next == depth - 2 and i_next + 1 < count:
                    work.append((forward, (q, i_next + 1), ("x", items[q][i_next + 1][0])))
                if t_next == 1 and i_next == 1 and q < HALVES:
                    work.append((transpose, (q,), ("x", q)))
                if t_next == depth - 2 and i_next > 0:
                    work.append((backward_input, (q, i_next - 1), ("got", q, depth - 1)))
                fence(("msg", q), *[name for _, _, name in work])
                start(q, step + 1)
            else:
                work.append((backward_input, (q, count - 1), None))
            if step == 1 and q == 0:
                fence("far_x", "far_y", "all", ("msg", q))
                gather_end(1)
            for piece, args, _ in work:
                piece(*args)
            if step == 0 and q == 0:
                env["cotangent_there"] = swap(env["cotangent"])
                gather_near(1)
            if step == 0 and q == STREAMS - 1:
                fence("by_x", "by_y", "all", ("msg", q))
                gather_far()
        if t == depth - 1 and i == count - 1:
            for half in range(HALVES - 1):
                scatter_input(half)
    scatter_input(HALVES - 1)
    for chunk in range(CHUNKS):
        fence(("g", HALVES - 1, chunk), ("total", HALVES - 1))
        backward_weight(chunk)

    input_grad = jnp.concatenate([input_grad[h] for h in range(HALVES)], axis=-2)
    return env["activated"], input_grad.reshape(tokens.shape), env["weight_grad"]


def solution(mesh):
    return jax.shard_map(
        on_device,
        mesh=mesh,
        in_specs=(P("col", "row"), P("row", "col"), P("row", "col")),
        out_specs=(P("row", "col"), P("col", "row"), P("row", "col")),
        check_vma=False,
    )
```

time: 402 us -> 368 us (0.915)
  waiting for transfers between devices: 80.9 us -> 34.8 us
  Pallas kernels: 155 us -> 170 us
  between operations: 14.9 us -> 1.28 us
  starting transfers between devices: 99 us -> 109 us
    ppermute x20, waiting for transfers between devices: 51.5 us -> 15.8 us  [onward(): return lax.ppermute(value, 'row', up + down)]
    pallas_call x28 -> x30, Pallas kernels: 155 us -> 170 us  [the longest x4 36.1 us: forward_matmul(): matmul_call(body, 'forward', (steps,), 2 * rows * width * f, 2 * (rows *...]
    ppermute x7 -> x14, waiting for transfers between devices: 24.8 us -> 12.3 us  [cross(): return lax.ppermute(value, 'col', [(c, c ^ offset) for c in range(4)])]
    ppermute x21, starting transfers between devices: 17 us -> 28.8 us  [swap(): return lax.ppermute(value, 'row', [(r, r ^ 1) for r in range(n_row)])]
    ppermute x20, starting transfers between devices: 70.6 us -> 61.1 us  [onward(): return lax.ppermute(value, 'row', up + down)]
    ppermute x7 -> x14, starting transfers between devices: 11.4 us -> 19 us  [cross(): return lax.ppermute(value, 'col', [(c, c ^ offset) for c in range(4)])]
    unnamed x117 -> x104, local copies, waits for them, and re-layouts: 36.2 us -> 31.2 us
  transfers between devices with their start and end apart: 49 -> 55, of which waited for: 20 -> 17; matrix products, arithmetic and copies ran while one was open for 3% -> 5% of each run, Pallas kernels for 35% -> 40%
where the time goes in v2:
time: 368 us; the launch traced here: 365 us
  Pallas kernels  170 us (46%)
  starting transfers between devices  109 us (30%)
  local copies, waits for them, and re-layouts  44.3 us (12%)
  waiting for transfers between devices  34.8 us (9%)
  other arithmetic  6.48 us (2%)
    ppermute x20, starting transfers between devices, onward(): return lax.ppermute(value, 'row', up + down)  61.1 us
    pallas_call x4, Pallas kernels, forward_matmul(): matmul_call(body, 'forward', (steps,), 2 * rows * width * f, 2 * (rows *...  36.1 us
    pallas_call x4, Pallas kernels, input_grad_matmul(): matmul_call(body, 'input_grad', (width // bn,), 2 * rows * width * f, 2 *...  35.6 us
    unnamed x104, local copies, waits for them, and re-layouts  31.2 us
    ppermute x21, starting transfers between devices, swap(): return lax.ppermute(value, 'row', [(r, r ^ 1) for r in range(n_row)])  28.8 us
    pallas_call x2, Pallas kernels, weight_grad_matmul(): matmul_call(body, 'weight_grad', (steps,), 2 * n * rows * width * f, 2 *...  28.6 us
    pallas_call x12, Pallas kernels, message_kernel(): matmul_call(body, 'message', None, 0, 0, grid_spec=pltpu.PrefetchScalarGr...  27.1 us
    pallas_call x4, Pallas kernels, collect_kernel(): matmul_call(body, 'collect', None, 0, 0, vmem=56, grid_spec=pltpu.Prefetc...  22.7 us
  transfers between devices with their start and end apart: 55, of which 17 were waited for; matrix products, arithmetic and copies ran while one was open for 5% of the time, Pallas kernels for 40%

profile of v2, /device:TPU:0, one launch (start us, length us, event | category | flops | bytes accessed | tf_op | source)
XLA Modules:
  0.0 365.4 jit_solution(7289117419478058043)
XLA Ops:
  6.2 7.6 %collective-permute-done = bf16[2,64,1536]{2,1,0:T(8,128)(2,1)S(1)} collective-permute-done((bf16[2,64,1536]{2,1,0:T(8,128)(2,1)S(1)}, bf16[2,64,1536]{2,1,0:T(8,128)(2,1)S(1)}, u32[]{:S(2)}, u32[]{:S(2)}) %collective-permute-start) | collective-permute-done | bytes 393248 | tf_op jit(solution)/shard_map/ppermute | solution.py:270
  22.0 10.2 %forward.4 = bf16[512,3072]{1,0:T(8,128)(2,1)} custom-call(bf16[512,1536]{1,0:T(8,128)(2,1)S(1)} %bitcast.101, bf16[1536,6144]{1,0:T(8,128)(2,1)} %w_ref.15), custom_call_target="tpu_custom_call" | custom-call | flops 4831838208 | bytes 14155776 | tf_op jit(solution)/shard_map/forward/pallas_call | solution.py:52
  32.2 8.5 %forward.5 = bf16[512,3072]{1,0:T(8,128)(2,1)S(1)} custom-call(bf16[512,1536]{1,0:T(8,128)(2,1)S(1)} %bitcast.102, bf16[1536,6144]{1,0:T(8,128)(2,1)} %w_ref.15), custom_call_target="tpu_custom_call" | custom-call | flops 4831838208 | bytes 14155776 | tf_op jit(solution)/shard_map/forward/pallas_call | solution.py:52
  64.3 5.3 %collective-permute-start.7 = (bf16[2,64,3072]{2,1,0:T(8,128)(2,1)}, bf16[2,64,3072]{2,1,0:T(8,128)(2,1)}, u32[]{:S(2)}, u32[]{:S(2)}) collective-permute-start(bf16[2,64,3072]{2,1,0:T(8,128)(2,1)} %message.14), channel_id=1, source_target_pairs={{0,8},{8,16},{28,20},{20,12},{1,9},{9,17},{29,21},{21,13},{2,10},{... | collective-permute-start | bytes 2359304 | tf_op jit(solution)/shard_map/ppermute | solution.py:267
  89.5 9.0 %forward.6 = bf16[512,3072]{1,0:T(8,128)(2,1)S(1)} custom-call(bf16[512,1536]{1,0:T(8,128)(2,1)S(1)} %bitcast.104, bf16[1536,6144]{1,0:T(8,128)(2,1)} %w_ref.15), custom_call_target="tpu_custom_call" | custom-call | flops 4831838208 | bytes 14155776 | tf_op jit(solution)/shard_map/forward/pallas_call | solution.py:52
  106.2 8.5 %forward.7 = bf16[512,3072]{1,0:T(8,128)(2,1)S(1)} custom-call(bf16[512,1536]{1,0:T(8,128)(2,1)S(1)} %bitcast.105, bf16[1536,6144]{1,0:T(8,128)(2,1)} %w_ref.15), custom_call_target="tpu_custom_call" | custom-call | flops 4831838208 | bytes 14155776 | tf_op jit(solution)/shard_map/forward/pallas_call | solution.py:52
  119.0 5.2 %gelu.4 = (bf16[2,64,3072]{2,1,0:T(8,128)(2,1)S(1)}, bf16[128,6144]{1,0:T(8,128)(2,1)}) custom-call(s32[1]{0:T(128)} %bitcast.core_ref, bf16[4,2,64,3072]{3,2,1,0:T(8,128)(2,1)} %bitcast.17.part_ref, bf16[4,2,64,3072]{3,2,1,0:T(8,128)(2,1)} %collective-permute-done.4.theirs_ref, bf16[2,64,3072]{2,1,0:T(8,128)(2,1)} %collective-permute-done.8.came_ref, ...), custom_call_target="tpu_custom_call" | custom-call | tf_op jit(solution)/shard_map/gelu/pallas_call | solution.py:186
  127.1 5.0 %gelu.5 = (bf16[2,64,3072]{2,1,0:T(8,128)(2,1)S(1)}, bf16[128,6144]{1,0:T(8,128)(2,1)}) custom-call(s32[1]{0:T(128)} %bitcast.core_ref, bf16[4,2,64,3072]{3,2,1,0:T(8,128)(2,1)S(1)} %bitcast.86, bf16[4,2,64,3072]{3,2,1,0:T(8,128)(2,1)} %collective-permute-done.6.theirs_ref, ...), custom_call_target="tpu_custom_call", output_to_operand_aliasing={{1}: (7, {})} | custom-call | tf_op jit(solution)/shard_map/gelu/pallas_call | solution.py:186
  160.0 5.4 %collective-permute-start.29 = (bf16[2,64,3072]{2,1,0:T(8,128)(2,1)}, bf16[2,64,3072]{2,1,0:T(8,128)(2,1)}, u32[]{:S(2)}, u32[]{:S(2)}) collective-permute-start(bf16[2,64,3072]{2,1,0:T(8,128)(2,1)} %copy-done.38), channel_id=1, source_target_pairs={{0,8},{8,16},{16,24},{28,20},{20,12},{12,4},{1,9},{9,17},{17,25},{... | collective-permute-start | bytes 2359304 | tf_op jit(solution)/shard_map/ppermute | solution.py:267
  186.8 5.7 %collect.4 = bf16[4,2,64,3072]{3,2,1,0:T(8,128)(2,1)} custom-call(s32[2]{0:T(128)} %pad_add_fusion.3.place_ref, bf16[2,64,3072]{2,1,0:T(8,128)(2,1)} %copy-done.31, bf16[2,64,3072]{2,1,0:T(8,128)(2,1)} %copy-done.26, bf16[2,64,3072]{2,1,0:T(8,128)(2,1)} %collective-permute-done.25.rest_0_.refs_2_, ...), custom_call_target="tpu_custom_call" | custom-call | tf_op jit(solution)/shard_map/collect/pallas_call | solution.py:232
  194.4 8.7 %input_grad.4.rest_0_ = f32[512,1536]{1,0:T(8,128)S(1)} custom-call(bf16[512,3072]{1,0:T(8,128)(2,1)S(1)} %bitcast.108, bf16[1536,6144]{1,0:T(8,128)(2,1)} %w_ref.15), custom_call_target="tpu_custom_call" | custom-call | flops 4831838208 | bytes 18874368 | tf_op jit(solution)/shard_map/input_grad/pallas_call | solution.py:82
  212.0 5.7 %collect.5 = bf16[4,2,64,3072]{3,2,1,0:T(8,128)(2,1)} custom-call(s32[2]{0:T(128)} %pad_add_fusion.3.place_ref, bf16[2,64,3072]{2,1,0:T(8,128)(2,1)} %copy-done.30, bf16[2,64,3072]{2,1,0:T(8,128)(2,1)} %copy-done.25, bf16[2,64,3072]{2,1,0:T(8,128)(2,1)} %collective-permute-done.23.rest_0_.refs_2_, bf16[2,64,3072]{2,1,0:T(8,128)(2,1)} %copy-done.27, ...), custom_call_target="tpu_custom_call" | custom-call | tf_op jit(solution)/shard_map/collect/pallas_call | solution.py:232
  219.6 9.4 %input_grad.5 = bf16[512,1536]{1,0:T(8,128)(2,1)S(1)} custom-call(bf16[512,3072]{1,0:T(8,128)(2,1)S(1)} %bitcast.98, bf16[1536,6144]{1,0:T(8,128)(2,1)} %w_ref.15, f32[512,1536]{1,0:T(8,128)} %copy-done.21), custom_call_target="tpu_custom_call" | custom-call | flops 4831838208 | bytes 18874368 | tf_op jit(solution)/shard_map/input_grad/pallas_call | solution.py:82
  241.5 4.8 %gelu.7 = (bf16[2,64,3072]{2,1,0:T(8,128)(2,1)S(1)}, bf16[128,6144]{1,0:T(8,128)(2,1)}) custom-call(s32[1]{0:T(128)} %bitcast.core_ref, bf16[4,2,64,3072]{3,2,1,0:T(8,128)(2,1)S(1)} %bitcast.91, bf16[4,2,64,3072]{3,2,1,0:T(8,128)(2,1)S(1)} %copy-done.10, bf16[2,64,3072]{2,1,0:T(8,128)(2,1)} %collective-permute-done.32.came_ref, ...), custom_call_target="tpu_custom_call", output_to_operand_aliasing={{1}: (7, {})} | custom-call | tf_op jit(solution)/shard_map/gelu/pallas_call | solution.py:186
  253.8 5.9 %collective-permute-done.40.refs_1_ = bf16[2,64,3072]{2,1,0:T(8,128)(2,1)S(1)} collective-permute-done((bf16[2,64,3072]{2,1,0:T(8,128)(2,1)S(1)}, bf16[2,64,3072]{2,1,0:T(8,128)(2,1)S(1)}, u32[]{:S(2)}, u32[]{:S(2)}) %collective-permute-start.40) | collective-permute-done | bytes 786464 | tf_op jit(solution)/shard_map/ppermute | solution.py:267
  263.5 6.5 %collective-permute-start.46 = (bf16[2,64,3072]{2,1,0:T(8,128)(2,1)S(1)}, bf16[2,64,3072]{2,1,0:T(8,128)(2,1)S(1)}, u32[]{:S(2)}, u32[]{:S(2)}) collective-permute-start(bf16[2,64,3072]{2,1,0:T(8,128)(2,1)S(1)} %collective-permute-done.44.refs_2_), channel_id=1, source_target_pairs={{0,4},{4,0},{8,12},{12,8},{16,20},{20,16},{24,28},{28,24},{1,5},{5... | collective-permute-start | bytes 2359304 | tf_op jit(solution)/shard_map/ppermute | solution.py:262
  271.9 6.5 %collective-permute-start.49 = (bf16[2,64,3072]{2,1,0:T(8,128)(2,1)S(1)}, bf16[2,64,3072]{2,1,0:T(8,128)(2,1)S(1)}, u32[]{:S(2)}, u32[]{:S(2)}) collective-permute-start(bf16[2,64,3072]{2,1,0:T(8,128)(2,1)S(1)} %collective-permute-done.43.refs_2_), channel_id=1, source_target_pairs={{0,4},{4,0},{8,12},{12,8},{16,20},{20,16},{24,28},{28,24},{1,5},{5... | collective-permute-start | bytes 2359304 | tf_op jit(solution)/shard_map/ppermute | solution.py:262
  280.3 6.6 %collective-permute-start.50 = (bf16[2,64,3072]{2,1,0:T(8,128)(2,1)}, bf16[2,64,3072]{2,1,0:T(8,128)(2,1)}, u32[]{:S(2)}, u32[]{:S(2)}) collective-permute-start(bf16[2,64,3072]{2,1,0:T(8,128)(2,1)} %collective-permute-done.48.refs_3_), channel_id=1, source_target_pairs={{0,4},{4,0},{8,12},{12,8},{16,20},{20,16},{24,28},{28,24},{1,5},{5... | collective-permute-start | bytes 2359304 | tf_op jit(solution)/shard_map/ppermute | solution.py:262
  294.2 5.7 %collect.6 = bf16[4,2,64,3072]{3,2,1,0:T(8,128)(2,1)} custom-call(s32[2]{0:T(128)} %pad_add_fusion.3.place_ref, bf16[2,64,3072]{2,1,0:T(8,128)(2,1)} %copy-done.29, bf16[2,64,3072]{2,1,0:T(8,128)(2,1)} %copy-done.43, bf16[2,64,3072]{2,1,0:T(8,128)(2,1)} %copy-done.45, bf16[2,64,3072]{2,1,0:T(8,128)(2,1)} %collective-permute-done.48.refs_3_, ...), custom_call_target="tpu_custom_call" | custom-call | tf_op jit(solution)/shard_map/collect/pallas_call | solution.py:232
  301.8 8.6 %input_grad.6.rest_0_ = f32[512,1536]{1,0:T(8,128)S(1)} custom-call(bf16[512,3072]{1,0:T(8,128)(2,1)S(1)} %bitcast.110, bf16[1536,6144]{1,0:T(8,128)(2,1)} %w_ref.15), custom_call_target="tpu_custom_call" | custom-call | flops 4831838208 | bytes 18874368 | tf_op jit(solution)/shard_map/input_grad/pallas_call | solution.py:82
  315.4 5.7 %collect.7 = bf16[4,2,64,3072]{3,2,1,0:T(8,128)(2,1)} custom-call(s32[2]{0:T(128)} %pad_add_fusion.3.place_ref, bf16[2,64,3072]{2,1,0:T(8,128)(2,1)} %copy-done.28, bf16[2,64,3072]{2,1,0:T(8,128)(2,1)} %copy-done.39, bf16[2,64,3072]{2,1,0:T(8,128)(2,1)} %copy-done.41, bf16[2,64,3072]{2,1,0:T(8,128)(2,1)} %collective-permute-done.47.refs_3_, ...), custom_call_target="tpu_custom_call" | custom-call | tf_op jit(solution)/shard_map/collect/pallas_call | solution.py:232
  323.0 8.9 %input_grad.7 = bf16[512,1536]{1,0:T(8,128)(2,1)S(1)} custom-call(bf16[512,3072]{1,0:T(8,128)(2,1)S(1)} %bitcast.100, bf16[1536,6144]{1,0:T(8,128)(2,1)} %w_ref.15, f32[512,1536]{1,0:T(8,128)} %copy-done.20), custom_call_target="tpu_custom_call" | custom-call | flops 4831838208 | bytes 18874368 | tf_op jit(solution)/shard_map/input_grad/pallas_call | solution.py:82
  335.6 14.3 %weight_grad.2.refs_4_ = bf16[1536,6144]{1,0:T(8,128)(2,1)} custom-call(bf16[1536,512]{1,0:T(8,128)(2,1)} %bitcast.115, bf16[1536,512]{1,0:T(8,128)(2,1)} %bitcast.117, bf16[512,3072]{1,0:T(8,128)(2,1)} %bitcast.107, bf16[512,3072]{1,0:T(8,128)(2,1)} %bitcast.109), custom_call_target="tpu_custom_call" | custom-call | flops 9663676416 | bytes 18874368 | tf_op jit(solution)/shard_map/weight_grad/pallas_call | solution.py:113
  349.9 14.3 %weight_grad.3 = bf16[1536,6144]{1,0:T(8,128)(2,1)} custom-call(bf16[1536,512]{1,0:T(8,128)(2,1)} %bitcast.116, bf16[1536,512]{1,0:T(8,128)(2,1)} %bitcast.118, bf16[512,3072]{1,0:T(8,128)(2,1)} %bitcast.97, bf16[512,3072]{1,0:T(8,128)(2,1)} %bitcast.99, bf16[1536,6144]{1,0:T(8,128)(2,1)} %weight_grad.2.refs_4_), custom_call_target="tpu_custom_call", output_to_operand_aliasing={{}: (4, {})} | custom-call | flops 9663676416 | bytes 18874368 | tf_op jit(solution)/shard_map/weight_grad/pallas_call | solution.py:113
  (245 shorter events, 182.3 us)
Async XLA Ops:
  43.4 13.1 %collective-permute-start.5 = (bf16[2,64,3072]{2,1,0:T(8,128)(2,1)S(1)}, bf16[2,64,3072]{2,1,0:T(8,128)(2,1)S(1)}, u32[]{:S(2)}, u32[]{:S(2)}) collective-permute-start(bf16[2,64,3072]{2,1,0:T(8,128)(2,1)S(1)} %message.12), channel_id=1, source_target_pairs={{0,8},{28,20},{1,9},{29,21},{2,10},{30,22},{3,11},{31,23}} | collective-permute-start | bytes 2359304 | tf_op jit(solution)/shard_map/ppermute | solution.py:267
  49.7 19.9 %collective-permute-start.9 = (bf16[2,64,3072]{2,1,0:T(8,128)(2,1)}, bf16[2,64,3072]{2,1,0:T(8,128)(2,1)}, u32[]{:S(2)}, u32[]{:S(2)}) collective-permute-start(bf16[2,64,3072]{2,1,0:T(8,128)(2,1)} %message.13), channel_id=1, source_target_pairs={{0,8},{28,20},{1,9},{29,21},{2,10},{30,22},{3,11},{31,23}} | collective-permute-start | bytes 2359304 | tf_op jit(solution)/shard_map/ppermute | solution.py:267
  58.2 14.4 %collective-permute-start.11 = (bf16[2,64,1536]{2,1,0:T(8,128)(2,1)}, bf16[2,64,1536]{2,1,0:T(8,128)(2,1)}, u32[]{:S(2)}, u32[]{:S(2)}) collective-permute-start(bf16[2,64,1536]{2,1,0:T(8,128)(2,1)} %get-tuple-element.142), channel_id=1, source_target_pairs={{0,1},{1,0},{2,3},{3,2},{4,5},{5,4},{6,7},{7,6},{8,9},{9,8},{10,11... | collective-permute-start | bytes 1179656 | tf_op jit(solution)/shard_map/ppermute | solution.py:270
  59.7 12.9 %collective-permute-start.12 = (bf16[2,64,1536]{2,1,0:T(8,128)(2,1)}, bf16[2,64,1536]{2,1,0:T(8,128)(2,1)}, u32[]{:S(2)}, u32[]{:S(2)}) collective-permute-start(bf16[2,64,1536]{2,1,0:T(8,128)(2,1)} %get-tuple-element.142), channel_id=1, source_target_pairs={{0,2},{1,3},{2,0},{3,1},{4,6},{5,7},{6,4},{7,5},{8,10},{9,11},{10,... | collective-permute-start | bytes 1179656 | tf_op jit(solution)/shard_map/ppermute | solution.py:270
  64.3 15.1 %collective-permute-start.7 = (bf16[2,64,3072]{2,1,0:T(8,128)(2,1)}, bf16[2,64,3072]{2,1,0:T(8,128)(2,1)}, u32[]{:S(2)}, u32[]{:S(2)}) collective-permute-start(bf16[2,64,3072]{2,1,0:T(8,128)(2,1)} %message.14), channel_id=1, source_target_pairs={{0,8},{8,16},{28,20},{20,12},{1,9},{9,17},{29,21},{21,13},{2,10},{... | collective-permute-start | bytes 2359304 | tf_op jit(solution)/shard_map/ppermute | solution.py:267
  78.0 20.7 %collective-permute-start.10 = (bf16[2,64,3072]{2,1,0:T(8,128)(2,1)}, bf16[2,64,3072]{2,1,0:T(8,128)(2,1)S(1)}, u32[]{:S(2)}, u32[]{:S(2)}) collective-permute-start(bf16[2,64,3072]{2,1,0:T(8,128)(2,1)} %copy-done.32), channel_id=1, source_target_pairs={{0,8},{8,16},{28,20},{20,12},{1,9},{9,17},{29,21},{21,13},{2,10},{... | collective-permute-start | bytes 2359304 | tf_op jit(solution)/shard_map/ppermute | solution.py:267
  79.3 37.6 %collective-permute-start.18 = (bf16[128,6144]{1,0:T(8,128)(2,1)}, bf16[128,6144]{1,0:T(8,128)(2,1)S(1)}, u32[]{:S(2)}, u32[]{:S(2)}) collective-permute-start(bf16[128,6144]{1,0:T(8,128)(2,1)} %mine_ref.7), channel_id=1, source_target_pairs={{0,4},{4,0},{8,12},{12,8},{16,20},{20,16},{24,28},{28,24},{1,5},{5... | collective-permute-start | bytes 4718600 | tf_op jit(solution)/shard_map/ppermute | solution.py:262
  82.5 32.2 %collective-permute-start.8 = (bf16[2,64,3072]{2,1,0:T(8,128)(2,1)}, bf16[2,64,3072]{2,1,0:T(8,128)(2,1)}, u32[]{:S(2)}, u32[]{:S(2)}) collective-permute-start(bf16[2,64,3072]{2,1,0:T(8,128)(2,1)} %message.15), channel_id=1, source_target_pairs={{0,8},{8,16},{16,24},{28,20},{20,12},{12,4},{1,9},{9,17},{17,25},{... | collective-permute-start | bytes 2359304 | tf_op jit(solution)/shard_map/ppermute | solution.py:267
  98.5 38.5 %collective-permute-start.24 = (bf16[4,2,64,3072]{3,2,1,0:T(8,128)(2,1)S(1)}, bf16[4,2,64,3072]{3,2,1,0:T(8,128)(2,1)S(1)}, u32[]{:S(2)}, u32[]{:S(2)}) collective-permute-start(bf16[4,2,64,3072]{3,2,1,0:T(8,128)(2,1)S(1)} %bitcast.92), channel_id=1, source_target_pairs={{0,4},{4,0},{8,12},{12,8},{16,20},{20,16},{24,28},{28,24},{1,5},{5... | collective-permute-start | bytes 9437192 | tf_op jit(solution)/shard_map/ppermute | solution.py:262
  114.8 31.7 %collective-permute-start.15 = (bf16[4,2,64,3072]{3,2,1,0:T(8,128)(2,1)S(1)}, bf16[4,2,64,3072]{3,2,1,0:T(8,128)(2,1)S(1)}, u32[]{:S(2)}, u32[]{:S(2)}) collective-permute-start(bf16[4,2,64,3072]{3,2,1,0:T(8,128)(2,1)S(1)} %bitcast.87), channel_id=1, source_target_pairs={{0,4},{4,0},{8,12},{12,8},{16,20},{20,16},{24,28},{28,24},{1,5},{5... | collective-permute-start | bytes 9437192 | tf_op jit(solution)/shard_map/ppermute | solution.py:262
  138.2 15.2 %collective-permute-start.25 = (bf16[2,64,3072]{2,1,0:T(8,128)(2,1)S(1)}, bf16[2,64,3072]{2,1,0:T(8,128)(2,1)}, u32[]{:S(2)}, u32[]{:S(2)}) collective-permute-start(bf16[2,64,3072]{2,1,0:T(8,128)(2,1)S(1)} %message.19), channel_id=1, source_target_pairs={{0,8},{8,16},{16,24},{28,20},{20,12},{12,4},{1,9},{9,17},{17,25},{... | collective-permute-start | bytes 2359304 | tf_op jit(solution)/shard_map/ppermute | solution.py:267
  148.4 17.0 %collective-permute-start.23 = (bf16[2,64,3072]{2,1,0:T(8,128)(2,1)}, bf16[2,64,3072]{2,1,0:T(8,128)(2,1)}, u32[]{:S(2)}, u32[]{:S(2)}) collective-permute-start(bf16[2,64,3072]{2,1,0:T(8,128)(2,1)} %message.18), channel_id=1, source_target_pairs={{0,8},{8,16},{16,24},{28,20},{20,12},{12,4},{1,9},{9,17},{17,25},{... | collective-permute-start | bytes 2359304 | tf_op jit(solution)/shard_map/ppermute | solution.py:267
  160.0 14.3 %collective-permute-start.29 = (bf16[2,64,3072]{2,1,0:T(8,128)(2,1)}, bf16[2,64,3072]{2,1,0:T(8,128)(2,1)}, u32[]{:S(2)}, u32[]{:S(2)}) collective-permute-start(bf16[2,64,3072]{2,1,0:T(8,128)(2,1)} %copy-done.38), channel_id=1, source_target_pairs={{0,8},{8,16},{16,24},{28,20},{20,12},{12,4},{1,9},{9,17},{17,25},{... | collective-permute-start | bytes 2359304 | tf_op jit(solution)/shard_map/ppermute | solution.py:267
  174.3 28.9 %collective-permute-start.28 = (bf16[2,64,3072]{2,1,0:T(8,128)(2,1)}, bf16[2,64,3072]{2,1,0:T(8,128)(2,1)S(1)}, u32[]{:S(2)}, u32[]{:S(2)}) collective-permute-start(bf16[2,64,3072]{2,1,0:T(8,128)(2,1)} %copy-done.35), channel_id=1, source_target_pairs={{0,8},{8,16},{16,24},{28,20},{20,12},{12,4},{1,9},{9,17},{17,25},{... | collective-permute-start | bytes 2359304 | tf_op jit(solution)/shard_map/ppermute | solution.py:267
  203.3 26.9 %collective-permute-start.34 = (bf16[2,64,3072]{2,1,0:T(8,128)(2,1)}, bf16[2,64,3072]{2,1,0:T(8,128)(2,1)}, u32[]{:S(2)}, u32[]{:S(2)}) collective-permute-start(bf16[2,64,3072]{2,1,0:T(8,128)(2,1)} %message.22), channel_id=1, source_target_pairs={{0,8},{8,16},{16,24},{28,20},{20,12},{12,4},{1,9},{9,17},{17,25},{... | collective-permute-start | bytes 2359304 | tf_op jit(solution)/shard_map/ppermute | solution.py:267
  208.4 21.8 %collective-permute-start.32 = (bf16[2,64,3072]{2,1,0:T(8,128)(2,1)}, bf16[2,64,3072]{2,1,0:T(8,128)(2,1)}, u32[]{:S(2)}, u32[]{:S(2)}) collective-permute-start(bf16[2,64,3072]{2,1,0:T(8,128)(2,1)} %message.23), channel_id=1, source_target_pairs={{0,8},{8,16},{16,24},{28,20},{20,12},{12,4},{1,9},{9,17},{17,25},{... | collective-permute-start | bytes 2359304 | tf_op jit(solution)/shard_map/ppermute | solution.py:267
  280.3 13.9 %collective-permute-start.50 = (bf16[2,64,3072]{2,1,0:T(8,128)(2,1)}, bf16[2,64,3072]{2,1,0:T(8,128)(2,1)}, u32[]{:S(2)}, u32[]{:S(2)}) collective-permute-start(bf16[2,64,3072]{2,1,0:T(8,128)(2,1)} %collective-permute-done.48.refs_3_), channel_id=1, source_target_pairs={{0,4},{4,0},{8,12},{12,8},{16,20},{20,16},{24,28},{28,24},{1,5},{5... | collective-permute-start | bytes 2359304 | tf_op jit(solution)/shard_map/ppermute | solution.py:262
  286.9 25.1 %collective-permute-start.47 = (bf16[2,64,3072]{2,1,0:T(8,128)(2,1)S(1)}, bf16[2,64,3072]{2,1,0:T(8,128)(2,1)}, u32[]{:S(2)}, u32[]{:S(2)}) collective-permute-start(bf16[2,64,3072]{2,1,0:T(8,128)(2,1)S(1)} %collective-permute-done.43.refs_2_), channel_id=1, source_target_pairs={{16,24},{12,4},{17,25},{13,5},{18,26},{14,6},{19,27},{15,7}} | collective-permute-start | bytes 2359304 | tf_op jit(solution)/shard_map/ppermute | solution.py:267
  290.7 21.3 %collective-permute-start.37 = (bf16[2,64,1536]{2,1,0:T(8,128)(2,1)}, bf16[2,64,1536]{2,1,0:T(8,128)(2,1)}, u32[]{:S(2)}, u32[]{:S(2)}) collective-permute-start(bf16[2,64,1536]{2,1,0:T(8,128)(2,1)} %get-tuple-element.127), channel_id=1, source_target_pairs={{0,1},{1,0},{2,3},{3,2},{4,5},{5,4},{6,7},{7,6},{8,9},{9,8},{10,11... | collective-permute-start | bytes 1179656 | tf_op jit(solution)/shard_map/ppermute | solution.py:270
  291.9 20.2 %collective-permute-start.39 = (bf16[2,64,1536]{2,1,0:T(8,128)(2,1)}, bf16[2,64,1536]{2,1,0:T(8,128)(2,1)}, u32[]{:S(2)}, u32[]{:S(2)}) collective-permute-start(bf16[2,64,1536]{2,1,0:T(8,128)(2,1)} %get-tuple-element.128), channel_id=1, source_target_pairs={{0,3},{1,2},{2,1},{3,0},{4,7},{5,6},{6,5},{7,4},{8,11},{9,10},{10,... | collective-permute-start | bytes 1179656 | tf_op jit(solution)/shard_map/ppermute | solution.py:270
  293.7 18.8 %collective-permute-start.38 = (bf16[2,64,1536]{2,1,0:T(8,128)(2,1)S(1)}, bf16[2,64,1536]{2,1,0:T(8,128)(2,1)}, u32[]{:S(2)}, u32[]{:S(2)}) collective-permute-start(bf16[2,64,1536]{2,1,0:T(8,128)(2,1)S(1)} %get-tuple-element.129), channel_id=1, source_target_pairs={{0,2},{1,3},{2,0},{3,1},{4,6},{5,7},{6,4},{7,5},{8,10},{9,11},{10,... | collective-permute-start | bytes 1179656 | tf_op jit(solution)/shard_map/ppermute | solution.py:270
  332.1 32.2 %collective-permute-start.52 = (bf16[2,64,1536]{2,1,0:T(8,128)(2,1)S(1)}, bf16[2,64,1536]{2,1,0:T(8,128)(2,1)S(1)}, u32[]{:S(2)}, u32[]{:S(2)}) collective-permute-start(bf16[2,64,1536]{2,1,0:T(8,128)(2,1)S(1)} %get-tuple-element.130), channel_id=1, source_target_pairs={{0,1},{1,0},{2,3},{3,2},{4,5},{5,4},{6,7},{7,6},{8,9},{9,8},{10,11... | collective-permute-start | bytes 1179656 | tf_op jit(solution)/shard_map/ppermute | solution.py:270
  333.3 30.9 %collective-permute-start.54 = (bf16[2,64,1536]{2,1,0:T(8,128)(2,1)S(1)}, bf16[2,64,1536]{2,1,0:T(8,128)(2,1)S(1)}, u32[]{:S(2)}, u32[]{:S(2)}) collective-permute-start(bf16[2,64,1536]{2,1,0:T(8,128)(2,1)S(1)} %get-tuple-element.131), channel_id=1, source_target_pairs={{0,3},{1,2},{2,1},{3,0},{4,7},{5,6},{6,5},{7,4},{8,11},{9,10},{10,... | collective-permute-start | bytes 1179656 | tf_op jit(solution)/shard_map/ppermute | solution.py:270
  335.1 29.1 %collective-permute-start.53 = (bf16[2,64,1536]{2,1,0:T(8,128)(2,1)S(1)}, bf16[2,64,1536]{2,1,0:T(8,128)(2,1)S(1)}, u32[]{:S(2)}, u32[]{:S(2)}) collective-permute-start(bf16[2,64,1536]{2,1,0:T(8,128)(2,1)S(1)} %get-tuple-element.132), channel_id=1, source_target_pairs={{0,2},{1,3},{2,0},{3,1},{4,6},{5,7},{6,4},{7,5},{8,10},{9,11},{10,... | collective-permute-start | bytes 1179656 | tf_op jit(solution)/shard_map/ppermute | solution.py:270
  (83 other events, 776.7 us)

commit v3 on v2

--- a/solution.py
+++ b/solution.py
@@ -29,7 +29,7 @@
     return best
 
 
-def matmul_call(body, name, grid, flops, moved, vmem=28, **spec):
+def matmul_call(body, name, grid, flops, moved, vmem=60, **spec):
     if grid is not None:
         spec["grid"] = grid
     return pl.pallas_call(
@@ -55,7 +55,7 @@
         (steps,),
         2 * rows * width * f,
         2 * (rows * width + width * f + rows * f),
-        vmem=47,
+        vmem=14,
         in_specs=[
             pl.BlockSpec((rows, width), lambda j: (0, 0)),
             pl.BlockSpec((width, bn), lambda j: (0, chunk * steps + j)),
@@ -85,7 +85,7 @@
         (width // bn,),
         2 * rows * width * f,
         2 * (rows * f + width * f + 4 * rows * width),
-        vmem=47,
+        vmem=16,
         in_specs=[
             pl.BlockSpec((rows, f), lambda j: (0, 0)),
             pl.BlockSpec((bn, f), lambda j: (j, chunk)),
@@ -116,7 +116,7 @@
         (steps,),
         2 * n * rows * width * f,
         2 * (n * rows * width + n * rows * f + width * f),
-        vmem=56,
+        vmem=24,
         in_specs=[pl.BlockSpec((width, rows), lambda j: (0, 0))] * n
         + [pl.BlockSpec((rows, bn), lambda j: (0, j))] * n
         + [pl.BlockSpec(memory_space=pl.ANY)] * len(kept),
@@ -150,6 +150,7 @@
         None,
         0,
         0,
+        vmem=8,
         grid_spec=pltpu.PrefetchScalarGridSpec(
             num_scalar_prefetch=1,
             grid=(f // bn,),
@@ -189,6 +190,7 @@
         None,
         0,
         0,
+        vmem=8,
         grid_spec=pltpu.PrefetchScalarGridSpec(
             num_scalar_prefetch=1,
             grid=(steps,),
@@ -205,14 +207,11 @@
 
 
 def collect_kernel(place, slope, mine, theirs, depth):
-    cores, few, f = slope.shape
-    bn = tile(f, 1024)
-
     def body(place_ref, *refs):
-        slope_ref, out = refs[0], refs[-1]
+        slope_ref, out, sems = refs[0], refs[-2], refs[-1]
         mine_refs, their_refs = refs[1:depth], refs[depth : 2 * depth - 1]
         z, core = place_ref[0], place_ref[1]
-        out[0] = slope_ref[...]
+        pltpu.make_async_copy(slope_ref, out.at[0], sems.at[0]).start()
         for j in range(1, depth):
             above = z + j < depth
             here = above == (core == 1)
@@ -222,27 +221,31 @@
 
                 @pl.when(side & here)
                 def _():
-                    out[j] = mine_refs[step - 1][...]
+                    pltpu.make_async_copy(mine_refs[step - 1], out.at[j], sems.at[j]).start()
 
                 @pl.when(side & jnp.logical_not(here))
                 def _():
-                    out[j] = their_refs[step - 1][...]
-
-    flat = pl.BlockSpec((cores, few, bn), lambda j, place: (0, 0, j))
+                    pltpu.make_async_copy(their_refs[step - 1], out.at[j], sems.at[j]).start()
+
+        for j in range(depth):
+            pltpu.make_async_copy(slope_ref, out.at[j], sems.at[j]).wait()
+
+    shape = (depth, *slope.shape)
     return matmul_call(
         body,
         "collect",
         None,
         0,
         0,
-        vmem=56,
+        vmem=10,
         grid_spec=pltpu.PrefetchScalarGridSpec(
             num_scalar_prefetch=1,
-            grid=(f // bn,),
-            in_specs=[flat] * (2 * depth - 1),
-            out_specs=pl.BlockSpec((depth, cores, few, bn), lambda j, place: (0, 0, 0, j)),
+            grid=(1,),
+            in_specs=[pl.BlockSpec(memory_space=pl.ANY)] * (2 * depth - 1),
+            out_specs=pl.BlockSpec(shape, lambda j, place: (0, 0, 0, 0)),
+            scratch_shapes=[pltpu.SemaphoreType.DMA((depth,))],
         ),
-        out_shape=jax.ShapeDtypeStruct((depth, *slope.shape), BF16),
+        out_shape=jax.ShapeDtypeStruct(shape, BF16),
     )(place, slope, *mine, *theirs)
 
 
@@ -341,9 +344,9 @@
             units,
         )
 
-    def scatter_input(half):
+    def scatter_input(half, direct):
         pair = env["total", half].reshape(depth, CORES, few, width)
-        if square:
+        if direct:
             blocks = []
             for offset in range(4):
                 at = ((col ^ offset) + depth - z) % depth
@@ -357,7 +360,7 @@
             total = lax.psum_scatter(
                 pair.reshape(n_col, -1, few, width), "col", scatter_dimension=0, tiled=True
             )
-            input_grad[half] = total[0]
+            input_grad[half] = total.reshape(-1, few, width)
 
     core_there = core.astype(jnp.int32).reshape(1)
     place_there = jnp.stack([z, core]).astype(jnp.int32)
@@ -467,8 +470,8 @@
                 gather_far()
         if t == depth - 1 and i == count - 1:
             for half in range(HALVES - 1):
-                scatter_input(half)
-    scatter_input(HALVES - 1)
+                scatter_input(half, False)
+    scatter_input(HALVES - 1, square)
     for chunk in range(CHUNKS):
         fence(("g", HALVES - 1, chunk), ("total", HALVES - 1))
         backward_weight(chunk)

time: 368 us -> 363 us (0.986)
  Pallas kernels: 170 us -> 133 us
  local copies, waits for them, and re-layouts: 44.3 us -> 61.4 us
  between operations: 1.28 us -> 15.2 us
  starting transfers between devices: 109 us -> 104 us
  waiting for transfers between devices: 34.8 us -> 39.3 us
    unnamed x104 -> x136, local copies, waits for them, and re-layouts: 31.2 us -> 50.6 us
    pallas_call x20, Pallas kernels: 69.5 us -> 51.7 us  [the longest x12 25.9 us: message_kernel(): matmul_call(body, 'message', None, 0, 0, vmem=8, grid_spec=pltpu.Prefetch...]
    pallas_call x4, Pallas kernels: 36.1 us -> 28 us  [forward_matmul(): matmul_call(body, 'forward', (steps,), 2 * rows * width * f, 2 * (rows *...]
    pallas_call x4, Pallas kernels: 35.6 us -> 28 us  [input_grad_matmul(): matmul_call(body, 'input_grad', (width // bn,), 2 * rows * width * f, 2 *...]
    ppermute x20, waiting for transfers between devices: 15.8 us -> 23.4 us  [onward(): return lax.ppermute(value, 'row', up + down)]
    pallas_call x2, Pallas kernels: 28.6 us -> 24.9 us  [weight_grad_matmul(): matmul_call(body, 'weight_grad', (steps,), 2 * n * rows * width * f, 2 *...]
    ppermute x14 -> x11, starting transfers between devices: 19 us -> 15.5 us  [cross(): return lax.ppermute(value, 'col', [(c, c ^ offset) for c in range(4)])]
    ppermute x14 -> x11, waiting for transfers between devices: 12.3 us -> 11.8 us  [cross(): return lax.ppermute(value, 'col', [(c, c ^ offset) for c in range(4)])]
  transfers between devices with their start and end apart: 55 -> 53, of which waited for: 17 -> 16; matrix products, arithmetic and copies ran while one was open for 5% -> 4% of each run, Pallas kernels for 40% -> 35%
where the time goes in v3:
time: 363 us; the launch traced here: 361 us
  Pallas kernels  133 us (37%)
  starting transfers between devices  104 us (29%)
  local copies, waits for them, and re-layouts  61.4 us (17%)
  waiting for transfers between devices  39.3 us (11%)
  between operations  15.2 us (4%)
  other arithmetic  8.75 us (2%)
    ppermute x20, starting transfers between devices, onward(): return lax.ppermute(value, 'row', up + down)  62.5 us
    unnamed x136, local copies, waits for them, and re-layouts  50.6 us
    pallas_call x4, Pallas kernels, forward_matmul(): matmul_call(body, 'forward', (steps,), 2 * rows * width * f, 2 * (rows *...  28 us
    pallas_call x4, Pallas kernels, input_grad_matmul(): matmul_call(body, 'input_grad', (width // bn,), 2 * rows * width * f, 2 *...  28 us
    pallas_call x12, Pallas kernels, message_kernel(): matmul_call(body, 'message', None, 0, 0, vmem=8, grid_spec=pltpu.Prefetch...  25.9 us
    ppermute x21, starting transfers between devices, swap(): return lax.ppermute(value, 'row', [(r, r ^ 1) for r in range(n_row)])  25.9 us
    pallas_call x2, Pallas kernels, weight_grad_matmul(): matmul_call(body, 'weight_grad', (steps,), 2 * n * rows * width * f, 2 *...  24.9 us
    ppermute x20, waiting for transfers between devices, onward(): return lax.ppermute(value, 'row', up + down)  23.4 us
  transfers between devices with their start and end apart: 53, of which 16 were waited for; matrix products, arithmetic and copies ran while one was open for 4% of the time, Pallas kernels for 35%

profile of v3, /device:TPU:0, one launch (start us, length us, event | category | flops | bytes accessed | tf_op | source)
XLA Modules:
  0.0 361.2 jit_solution(2305111434286406380)
XLA Ops:
  12.8 7.6 %collective-permute-done = bf16[2,64,1536]{2,1,0:T(8,128)(2,1)S(1)} collective-permute-done((bf16[2,64,1536]{2,1,0:T(8,128)(2,1)S(1)}, bf16[2,64,1536]{2,1,0:T(8,128)(2,1)S(1)}, u32[]{:S(2)}, u32[]{:S(2)}) %collective-permute-start) | collective-permute-done | bytes 393248 | tf_op jit(solution)/shard_map/ppermute | solution.py:273
  28.6 6.9 %copy-done = bf16[1536,6144]{1,0:T(8,128)(2,1)S(1)} copy-done((bf16[1536,6144]{1,0:T(8,128)(2,1)S(1)}, bf16[1536,6144]{1,0:T(8,128)(2,1)}, u32[]{:S(2)}) %copy-start) | copy-done | bytes 18874392
  35.6 7.5 %forward.4 = bf16[512,3072]{1,0:T(8,128)(2,1)} custom-call(bf16[512,1536]{1,0:T(8,128)(2,1)S(1)} %bitcast.98, bf16[1536,6144]{1,0:T(8,128)(2,1)S(1)} %copy-done), custom_call_target="tpu_custom_call" | custom-call | flops 4831838208 | bytes 14155776 | tf_op jit(solution)/shard_map/forward/pallas_call | solution.py:52
  43.1 6.8 %forward.5 = bf16[512,3072]{1,0:T(8,128)(2,1)S(1)} custom-call(bf16[512,1536]{1,0:T(8,128)(2,1)S(1)} %bitcast.99, bf16[1536,6144]{1,0:T(8,128)(2,1)S(1)} %copy-done), custom_call_target="tpu_custom_call" | custom-call | flops 4831838208 | bytes 14155776 | tf_op jit(solution)/shard_map/forward/pallas_call | solution.py:52
  73.5 5.3 %collective-permute-start.7 = (bf16[2,64,3072]{2,1,0:T(8,128)(2,1)}, bf16[2,64,3072]{2,1,0:T(8,128)(2,1)}, u32[]{:S(2)}, u32[]{:S(2)}) collective-permute-start(bf16[2,64,3072]{2,1,0:T(8,128)(2,1)} %message.14), channel_id=1, source_target_pairs={{0,8},{8,16},{28,20},{20,12},{1,9},{9,17},{29,21},{21,13},{2,10},{... | collective-permute-start | bytes 2359304 | tf_op jit(solution)/shard_map/ppermute | solution.py:270
  99.2 6.9 %copy-done.1 = bf16[1536,6144]{1,0:T(8,128)(2,1)S(1)} copy-done((bf16[1536,6144]{1,0:T(8,128)(2,1)S(1)}, bf16[1536,6144]{1,0:T(8,128)(2,1)}, u32[]{:S(2)}) %copy-start.1) | copy-done | bytes 18874392
  106.1 6.8 %forward.6 = bf16[512,3072]{1,0:T(8,128)(2,1)S(1)} custom-call(bf16[512,1536]{1,0:T(8,128)(2,1)S(1)} %bitcast.101, bf16[1536,6144]{1,0:T(8,128)(2,1)S(1)} %copy-done.1), custom_call_target="tpu_custom_call" | custom-call | flops 4831838208 | bytes 14155776 | tf_op jit(solution)/shard_map/forward/pallas_call | solution.py:52
  118.0 6.8 %forward.7 = bf16[512,3072]{1,0:T(8,128)(2,1)S(1)} custom-call(bf16[512,1536]{1,0:T(8,128)(2,1)S(1)} %bitcast.102, bf16[1536,6144]{1,0:T(8,128)(2,1)S(1)} %bitcast.76), custom_call_target="tpu_custom_call" | custom-call | flops 4831838208 | bytes 14155776 | tf_op jit(solution)/shard_map/forward/pallas_call | solution.py:52
  128.6 5.1 %gelu.4 = (bf16[2,64,3072]{2,1,0:T(8,128)(2,1)S(1)}, bf16[128,6144]{1,0:T(8,128)(2,1)}) custom-call(s32[1]{0:T(128)} %bitcast.core_ref, bf16[4,2,64,3072]{3,2,1,0:T(8,128)(2,1)} %bitcast.17.part_ref, bf16[4,2,64,3072]{3,2,1,0:T(8,128)(2,1)} %collective-permute-done.4.theirs_ref, bf16[2,64,3072]{2,1,0:T(8,128)(2,1)} %collective-permute-done.8.came_ref, ...), custom_call_target="tpu_custom_call" | custom-call | tf_op jit(solution)/shard_map/gelu/pallas_call | solution.py:187
  147.7 5.2 %collective-permute-start.25 = (bf16[2,64,3072]{2,1,0:T(8,128)(2,1)S(1)}, bf16[2,64,3072]{2,1,0:T(8,128)(2,1)}, u32[]{:S(2)}, u32[]{:S(2)}) collective-permute-start(bf16[2,64,3072]{2,1,0:T(8,128)(2,1)S(1)} %message.19), channel_id=1, source_target_pairs={{0,8},{8,16},{16,24},{28,20},{20,12},{12,4},{1,9},{9,17},{17,25},{... | collective-permute-start | bytes 2359304 | tf_op jit(solution)/shard_map/ppermute | solution.py:270
  157.8 5.2 %collective-permute-start.23 = (bf16[2,64,3072]{2,1,0:T(8,128)(2,1)}, bf16[2,64,3072]{2,1,0:T(8,128)(2,1)}, u32[]{:S(2)}, u32[]{:S(2)}) collective-permute-start(bf16[2,64,3072]{2,1,0:T(8,128)(2,1)} %message.18), channel_id=1, source_target_pairs={{0,8},{8,16},{16,24},{28,20},{20,12},{12,4},{1,9},{9,17},{17,25},{... | collective-permute-start | bytes 2359304 | tf_op jit(solution)/shard_map/ppermute | solution.py:270
  170.1 5.2 %collective-permute-start.29 = (bf16[2,64,3072]{2,1,0:T(8,128)(2,1)}, bf16[2,64,3072]{2,1,0:T(8,128)(2,1)}, u32[]{:S(2)}, u32[]{:S(2)}) collective-permute-start(bf16[2,64,3072]{2,1,0:T(8,128)(2,1)} %copy-done.56), channel_id=1, source_target_pairs={{0,8},{8,16},{16,24},{28,20},{20,12},{12,4},{1,9},{9,17},{17,25},{... | collective-permute-start | bytes 2359304 | tf_op jit(solution)/shard_map/ppermute | solution.py:270
  197.5 7.5 %copy-done.2 = bf16[1536,6144]{1,0:T(8,128)(2,1)S(1)} copy-done((bf16[1536,6144]{1,0:T(8,128)(2,1)S(1)}, bf16[1536,6144]{1,0:T(8,128)(2,1)}, u32[]{:S(2)}) %copy-start.2) | copy-done | bytes 18874392
  205.0 6.9 %input_grad.4.rest_0_ = f32[512,1536]{1,0:T(8,128)S(1)} custom-call(bf16[512,3072]{1,0:T(8,128)(2,1)S(1)} %bitcast.104, bf16[1536,6144]{1,0:T(8,128)(2,1)S(1)} %copy-done.2), custom_call_target="tpu_custom_call" | custom-call | flops 4831838208 | bytes 18874368 | tf_op jit(solution)/shard_map/input_grad/pallas_call | solution.py:82
  221.5 7.1 %input_grad.5 = bf16[512,1536]{1,0:T(8,128)(2,1)S(1)} custom-call(bf16[512,3072]{1,0:T(8,128)(2,1)S(1)} %bitcast.94, bf16[1536,6144]{1,0:T(8,128)(2,1)S(1)} %bitcast.78, f32[512,1536]{1,0:T(8,128)S(1)} %input_grad.4.rest_0_), custom_call_target="tpu_custom_call" | custom-call | flops 4831838208 | bytes 18874368 | tf_op jit(solution)/shard_map/input_grad/pallas_call | solution.py:82
  252.2 7.6 %collective-permute-done.37.refs_1_ = bf16[2,64,3072]{2,1,0:T(8,128)(2,1)S(1)} collective-permute-done((bf16[2,64,3072]{2,1,0:T(8,128)(2,1)S(1)}, bf16[2,64,3072]{2,1,0:T(8,128)(2,1)S(1)}, u32[]{:S(2)}, u32[]{:S(2)}) %collective-permute-start.37) | collective-permute-done | bytes 786464 | tf_op jit(solution)/shard_map/ppermute | solution.py:270
  263.0 6.2 %collective-permute-start.43 = (bf16[2,64,3072]{2,1,0:T(8,128)(2,1)S(1)}, bf16[2,64,3072]{2,1,0:T(8,128)(2,1)S(1)}, u32[]{:S(2)}, u32[]{:S(2)}) collective-permute-start(bf16[2,64,3072]{2,1,0:T(8,128)(2,1)S(1)} %collective-permute-done.41.refs_2_), channel_id=1, source_target_pairs={{0,4},{4,0},{8,12},{12,8},{16,20},{20,16},{24,28},{28,24},{1,5},{5... | collective-permute-start | bytes 2359304 | tf_op jit(solution)/shard_map/ppermute | solution.py:265
  271.2 5.6 %collective-permute-start.46 = (bf16[2,64,3072]{2,1,0:T(8,128)(2,1)S(1)}, bf16[2,64,3072]{2,1,0:T(8,128)(2,1)S(1)}, u32[]{:S(2)}, u32[]{:S(2)}) collective-permute-start(bf16[2,64,3072]{2,1,0:T(8,128)(2,1)S(1)} %collective-permute-done.40.refs_2_), channel_id=1, source_target_pairs={{0,4},{4,0},{8,12},{12,8},{16,20},{20,16},{24,28},{28,24},{1,5},{5... | collective-permute-start | bytes 2359304 | tf_op jit(solution)/shard_map/ppermute | solution.py:265
  279.6 6.5 %collective-permute-start.47 = (bf16[2,64,3072]{2,1,0:T(8,128)(2,1)S(1)}, bf16[2,64,3072]{2,1,0:T(8,128)(2,1)S(1)}, u32[]{:S(2)}, u32[]{:S(2)}) collective-permute-start(bf16[2,64,3072]{2,1,0:T(8,128)(2,1)S(1)} %collective-permute-done.45.refs_3_), channel_id=1, source_target_pairs={{0,4},{4,0},{8,12},{12,8},{16,20},{20,16},{24,28},{28,24},{1,5},{5... | collective-permute-start | bytes 2359304 | tf_op jit(solution)/shard_map/ppermute | solution.py:265
  288.9 6.9 %input_grad.6.rest_0_ = f32[512,1536]{1,0:T(8,128)S(1)} custom-call(bf16[512,3072]{1,0:T(8,128)(2,1)S(1)} %bitcast.106, bf16[1536,6144]{1,0:T(8,128)(2,1)S(1)} %bitcast.78), custom_call_target="tpu_custom_call" | custom-call | flops 4831838208 | bytes 18874368 | tf_op jit(solution)/shard_map/input_grad/pallas_call | solution.py:82
  309.9 6.6 %copy-done.3 = bf16[1536,6144]{1,0:T(8,128)(2,1)S(1)} copy-done((bf16[1536,6144]{1,0:T(8,128)(2,1)S(1)}, bf16[1536,6144]{1,0:T(8,128)(2,1)}, u32[]{:S(2)}) %copy-start.3) | copy-done | bytes 18874392
  316.5 7.1 %input_grad.7 = bf16[512,1536]{1,0:T(8,128)(2,1)S(1)} custom-call(bf16[512,3072]{1,0:T(8,128)(2,1)S(1)} %bitcast.96, bf16[1536,6144]{1,0:T(8,128)(2,1)S(1)} %copy-done.3, f32[512,1536]{1,0:T(8,128)S(1)} %input_grad.6.rest_0_), custom_call_target="tpu_custom_call" | custom-call | flops 4831838208 | bytes 18874368 | tf_op jit(solution)/shard_map/input_grad/pallas_call | solution.py:82
  327.2 12.4 %weight_grad.2.refs_4_ = bf16[1536,6144]{1,0:T(8,128)(2,1)} custom-call(bf16[1536,512]{1,0:T(8,128)(2,1)S(1)} %bitcast.108, bf16[1536,512]{1,0:T(8,128)(2,1)S(1)} %bitcast.110, bf16[512,3072]{1,0:T(8,128)(2,1)S(1)} %bitcast.105, bf16[512,3072]{1,0:T(8,128)(2,1)S(1)} %bitcast.107), custom_call_target="tpu_custom_call" | custom-call | flops 9663676416 | bytes 18874368 | tf_op jit(solution)/shard_map/weight_grad/pallas_call | solution.py:113
  339.7 12.4 %weight_grad.3 = bf16[1536,6144]{1,0:T(8,128)(2,1)} custom-call(bf16[1536,512]{1,0:T(8,128)(2,1)S(1)} %bitcast.109, bf16[1536,512]{1,0:T(8,128)(2,1)S(1)} %bitcast.111, bf16[512,3072]{1,0:T(8,128)(2,1)S(1)} %bitcast.95, bf16[512,3072]{1,0:T(8,128)(2,1)S(1)} %bitcast.97, bf16[1536,6144]{1,0:T(8,128)(2,1)} %weight_grad.2.refs_4_), custom_call_target="tpu_custom_call", output_to_operand_aliasing={{}: (4, {})} | custom-call | flops 9663676416 | bytes 18874368 | tf_op jit(solution)/shard_map/weight_grad/pallas_call | solution.py:113
  (275 shorter events, 177.7 us)
Async XLA Ops:
  7.2 345.2 %reduce-scatter.4.cloned.1.call-start = ((), (), s32[]{:S(2)}) async-start(), calls=%async_computation.1 | async-start | bytes 1966080
  52.7 13.1 %collective-permute-start.5 = (bf16[2,64,3072]{2,1,0:T(8,128)(2,1)S(1)}, bf16[2,64,3072]{2,1,0:T(8,128)(2,1)S(1)}, u32[]{:S(2)}, u32[]{:S(2)}) collective-permute-start(bf16[2,64,3072]{2,1,0:T(8,128)(2,1)S(1)} %message.12), channel_id=1, source_target_pairs={{0,8},{28,20},{1,9},{29,21},{2,10},{30,22},{3,11},{31,23}} | collective-permute-start | bytes 2359304 | tf_op jit(solution)/shard_map/ppermute | solution.py:270
  58.9 19.9 %collective-permute-start.9 = (bf16[2,64,3072]{2,1,0:T(8,128)(2,1)}, bf16[2,64,3072]{2,1,0:T(8,128)(2,1)}, u32[]{:S(2)}, u32[]{:S(2)}) collective-permute-start(bf16[2,64,3072]{2,1,0:T(8,128)(2,1)} %message.13), channel_id=1, source_target_pairs={{0,8},{28,20},{1,9},{29,21},{2,10},{30,22},{3,11},{31,23}} | collective-permute-start | bytes 2359304 | tf_op jit(solution)/shard_map/ppermute | solution.py:270
  67.5 14.4 %collective-permute-start.11 = (bf16[2,64,1536]{2,1,0:T(8,128)(2,1)}, bf16[2,64,1536]{2,1,0:T(8,128)(2,1)}, u32[]{:S(2)}, u32[]{:S(2)}) collective-permute-start(bf16[2,64,1536]{2,1,0:T(8,128)(2,1)} %get-tuple-element.139), channel_id=1, source_target_pairs={{0,1},{1,0},{2,3},{3,2},{4,5},{5,4},{6,7},{7,6},{8,9},{9,8},{10,11... | collective-permute-start | bytes 1179656 | tf_op jit(solution)/shard_map/ppermute | solution.py:273
  69.0 12.9 %collective-permute-start.12 = (bf16[2,64,1536]{2,1,0:T(8,128)(2,1)}, bf16[2,64,1536]{2,1,0:T(8,128)(2,1)}, u32[]{:S(2)}, u32[]{:S(2)}) collective-permute-start(bf16[2,64,1536]{2,1,0:T(8,128)(2,1)} %get-tuple-element.139), channel_id=1, source_target_pairs={{0,2},{1,3},{2,0},{3,1},{4,6},{5,7},{6,4},{7,5},{8,10},{9,11},{10,... | collective-permute-start | bytes 1179656 | tf_op jit(solution)/shard_map/ppermute | solution.py:273
  73.5 15.9 %collective-permute-start.7 = (bf16[2,64,3072]{2,1,0:T(8,128)(2,1)}, bf16[2,64,3072]{2,1,0:T(8,128)(2,1)}, u32[]{:S(2)}, u32[]{:S(2)}) collective-permute-start(bf16[2,64,3072]{2,1,0:T(8,128)(2,1)} %message.14), channel_id=1, source_target_pairs={{0,8},{8,16},{28,20},{20,12},{1,9},{9,17},{29,21},{21,13},{2,10},{... | collective-permute-start | bytes 2359304 | tf_op jit(solution)/shard_map/ppermute | solution.py:270
  87.2 25.8 %collective-permute-start.10 = (bf16[2,64,3072]{2,1,0:T(8,128)(2,1)}, bf16[2,64,3072]{2,1,0:T(8,128)(2,1)}, u32[]{:S(2)}, u32[]{:S(2)}) collective-permute-start(bf16[2,64,3072]{2,1,0:T(8,128)(2,1)} %copy-done.51), channel_id=1, source_target_pairs={{0,8},{8,16},{28,20},{20,12},{1,9},{9,17},{29,21},{21,13},{2,10},{... | collective-permute-start | bytes 2359304 | tf_op jit(solution)/shard_map/ppermute | solution.py:270
  89.4 39.2 %collective-permute-start.18 = (bf16[128,6144]{1,0:T(8,128)(2,1)}, bf16[128,6144]{1,0:T(8,128)(2,1)}, u32[]{:S(2)}, u32[]{:S(2)}) collective-permute-start(bf16[128,6144]{1,0:T(8,128)(2,1)} %mine_ref.7), channel_id=1, source_target_pairs={{0,4},{4,0},{8,12},{12,8},{16,20},{20,16},{24,28},{28,24},{1,5},{5... | collective-permute-start | bytes 4718600 | tf_op jit(solution)/shard_map/ppermute | solution.py:265
  92.8 32.1 %collective-permute-start.8 = (bf16[2,64,3072]{2,1,0:T(8,128)(2,1)}, bf16[2,64,3072]{2,1,0:T(8,128)(2,1)}, u32[]{:S(2)}, u32[]{:S(2)}) collective-permute-start(bf16[2,64,3072]{2,1,0:T(8,128)(2,1)} %message.15), channel_id=1, source_target_pairs={{0,8},{8,16},{16,24},{28,20},{20,12},{12,4},{1,9},{9,17},{17,25},{... | collective-permute-start | bytes 2359304 | tf_op jit(solution)/shard_map/ppermute | solution.py:270
  113.0 33.5 %collective-permute-start.24 = (bf16[4,2,64,3072]{3,2,1,0:T(8,128)(2,1)S(1)}, bf16[4,2,64,3072]{3,2,1,0:T(8,128)(2,1)S(1)}, u32[]{:S(2)}, u32[]{:S(2)}) collective-permute-start(bf16[4,2,64,3072]{3,2,1,0:T(8,128)(2,1)S(1)} %bitcast.89), channel_id=1, source_target_pairs={{0,4},{4,0},{8,12},{12,8},{16,20},{20,16},{24,28},{28,24},{1,5},{5... | collective-permute-start | bytes 9437192 | tf_op jit(solution)/shard_map/ppermute | solution.py:265
  125.0 30.9 %collective-permute-start.15 = (bf16[4,2,64,3072]{3,2,1,0:T(8,128)(2,1)S(1)}, bf16[4,2,64,3072]{3,2,1,0:T(8,128)(2,1)S(1)}, u32[]{:S(2)}, u32[]{:S(2)}) collective-permute-start(bf16[4,2,64,3072]{3,2,1,0:T(8,128)(2,1)S(1)} %bitcast.84), channel_id=1, source_target_pairs={{0,4},{4,0},{8,12},{12,8},{16,20},{20,16},{24,28},{28,24},{1,5},{5... | collective-permute-start | bytes 9437192 | tf_op jit(solution)/shard_map/ppermute | solution.py:265
  133.7 12.7 %collective-permute-start.21 = (bf16[2,64,3072]{2,1,0:T(8,128)(2,1)S(1)}, bf16[2,64,3072]{2,1,0:T(8,128)(2,1)S(1)}, u32[]{:S(2)}, u32[]{:S(2)}) collective-permute-start(bf16[2,64,3072]{2,1,0:T(8,128)(2,1)S(1)} %get-tuple-element.86.refs_0_), channel_id=1, source_target_pairs={{0,8},{8,16},{16,24},{28,20},{20,12},{12,4},{1,9},{9,17},{17,25},{... | collective-permute-start | bytes 2359304 | tf_op jit(solution)/shard_map/ppermute | solution.py:270
  141.8 13.1 %collective-permute-start.20 = (bf16[2,64,3072]{2,1,0:T(8,128)(2,1)S(1)}, bf16[2,64,3072]{2,1,0:T(8,128)(2,1)S(1)}, u32[]{:S(2)}, u32[]{:S(2)}) collective-permute-start(bf16[2,64,3072]{2,1,0:T(8,128)(2,1)S(1)} %get-tuple-element.85.refs_0_), channel_id=1, source_target_pairs={{0,8},{8,16},{16,24},{28,20},{20,12},{12,4},{1,9},{9,17},{17,25},{... | collective-permute-start | bytes 2359304 | tf_op jit(solution)/shard_map/ppermute | solution.py:270
  147.7 15.6 %collective-permute-start.25 = (bf16[2,64,3072]{2,1,0:T(8,128)(2,1)S(1)}, bf16[2,64,3072]{2,1,0:T(8,128)(2,1)}, u32[]{:S(2)}, u32[]{:S(2)}) collective-permute-start(bf16[2,64,3072]{2,1,0:T(8,128)(2,1)S(1)} %message.19), channel_id=1, source_target_pairs={{0,8},{8,16},{16,24},{28,20},{20,12},{12,4},{1,9},{9,17},{17,25},{... | collective-permute-start | bytes 2359304 | tf_op jit(solution)/shard_map/ppermute | solution.py:270
  157.8 17.5 %collective-permute-start.23 = (bf16[2,64,3072]{2,1,0:T(8,128)(2,1)}, bf16[2,64,3072]{2,1,0:T(8,128)(2,1)}, u32[]{:S(2)}, u32[]{:S(2)}) collective-permute-start(bf16[2,64,3072]{2,1,0:T(8,128)(2,1)} %message.18), channel_id=1, source_target_pairs={{0,8},{8,16},{16,24},{28,20},{20,12},{12,4},{1,9},{9,17},{17,25},{... | collective-permute-start | bytes 2359304 | tf_op jit(solution)/shard_map/ppermute | solution.py:270
  170.1 14.1 %collective-permute-start.29 = (bf16[2,64,3072]{2,1,0:T(8,128)(2,1)}, bf16[2,64,3072]{2,1,0:T(8,128)(2,1)}, u32[]{:S(2)}, u32[]{:S(2)}) collective-permute-start(bf16[2,64,3072]{2,1,0:T(8,128)(2,1)} %copy-done.56), channel_id=1, source_target_pairs={{0,8},{8,16},{16,24},{28,20},{20,12},{12,4},{1,9},{9,17},{17,25},{... | collective-permute-start | bytes 2359304 | tf_op jit(solution)/shard_map/ppermute | solution.py:270
  184.3 27.6 %collective-permute-start.28 = (bf16[2,64,3072]{2,1,0:T(8,128)(2,1)}, bf16[2,64,3072]{2,1,0:T(8,128)(2,1)S(1)}, u32[]{:S(2)}, u32[]{:S(2)}) collective-permute-start(bf16[2,64,3072]{2,1,0:T(8,128)(2,1)} %copy-done.53), channel_id=1, source_target_pairs={{0,8},{8,16},{16,24},{28,20},{20,12},{12,4},{1,9},{9,17},{17,25},{... | collective-permute-start | bytes 2359304 | tf_op jit(solution)/shard_map/ppermute | solution.py:270
  212.1 16.5 %collective-permute-start.34 = (bf16[2,64,3072]{2,1,0:T(8,128)(2,1)}, bf16[2,64,3072]{2,1,0:T(8,128)(2,1)S(1)}, u32[]{:S(2)}, u32[]{:S(2)}) collective-permute-start(bf16[2,64,3072]{2,1,0:T(8,128)(2,1)} %copy-done.52), channel_id=1, source_target_pairs={{0,8},{8,16},{16,24},{28,20},{20,12},{12,4},{1,9},{9,17},{17,25},{... | collective-permute-start | bytes 2359304 | tf_op jit(solution)/shard_map/ppermute | solution.py:270
  215.8 16.9 %collective-permute-start.32 = (bf16[2,64,3072]{2,1,0:T(8,128)(2,1)S(1)}, bf16[2,64,3072]{2,1,0:T(8,128)(2,1)S(1)}, u32[]{:S(2)}, u32[]{:S(2)}) collective-permute-start(bf16[2,64,3072]{2,1,0:T(8,128)(2,1)S(1)} %message.23), channel_id=1, source_target_pairs={{0,8},{8,16},{16,24},{28,20},{20,12},{12,4},{1,9},{9,17},{17,25},{... | collective-permute-start | bytes 2359304 | tf_op jit(solution)/shard_map/ppermute | solution.py:270
  238.7 12.6 %collective-permute-start.38 = (bf16[2,64,3072]{2,1,0:T(8,128)(2,1)S(1)}, bf16[2,64,3072]{2,1,0:T(8,128)(2,1)S(1)}, u32[]{:S(2)}, u32[]{:S(2)}) collective-permute-start(bf16[2,64,3072]{2,1,0:T(8,128)(2,1)S(1)} %get-tuple-element.113.refs_0_), channel_id=1, source_target_pairs={{0,8},{8,16},{16,24},{28,20},{20,12},{12,4},{1,9},{9,17},{17,25},{... | collective-permute-start | bytes 2359304 | tf_op jit(solution)/shard_map/ppermute | solution.py:270
  246.6 13.2 %collective-permute-start.37 = (bf16[2,64,3072]{2,1,0:T(8,128)(2,1)S(1)}, bf16[2,64,3072]{2,1,0:T(8,128)(2,1)S(1)}, u32[]{:S(2)}, u32[]{:S(2)}) collective-permute-start(bf16[2,64,3072]{2,1,0:T(8,128)(2,1)S(1)} %get-tuple-element.112.refs_0_), channel_id=1, source_target_pairs={{0,8},{8,16},{16,24},{28,20},{20,12},{12,4},{1,9},{9,17},{17,25},{... | collective-permute-start | bytes 2359304 | tf_op jit(solution)/shard_map/ppermute | solution.py:270
  323.7 28.5 %collective-permute-start.49 = (bf16[2,64,1536]{2,1,0:T(8,128)(2,1)S(1)}, bf16[2,64,1536]{2,1,0:T(8,128)(2,1)S(1)}, u32[]{:S(2)}, u32[]{:S(2)}) collective-permute-start(bf16[2,64,1536]{2,1,0:T(8,128)(2,1)S(1)} %get-tuple-element.127), channel_id=1, source_target_pairs={{0,1},{1,0},{2,3},{3,2},{4,5},{5,4},{6,7},{7,6},{8,9},{9,8},{10,11... | collective-permute-start | bytes 1179656 | tf_op jit(solution)/shard_map/ppermute | solution.py:273
  325.2 26.9 %collective-permute-start.51 = (bf16[2,64,1536]{2,1,0:T(8,128)(2,1)S(1)}, bf16[2,64,1536]{2,1,0:T(8,128)(2,1)S(1)}, u32[]{:S(2)}, u32[]{:S(2)}) collective-permute-start(bf16[2,64,1536]{2,1,0:T(8,128)(2,1)S(1)} %get-tuple-element.128), channel_id=1, source_target_pairs={{0,3},{1,2},{2,1},{3,0},{4,7},{5,6},{6,5},{7,4},{8,11},{9,10},{10,... | collective-permute-start | bytes 1179656 | tf_op jit(solution)/shard_map/ppermute | solution.py:273
  326.4 25.8 %collective-permute-start.50 = (bf16[2,64,1536]{2,1,0:T(8,128)(2,1)S(1)}, bf16[2,64,1536]{2,1,0:T(8,128)(2,1)S(1)}, u32[]{:S(2)}, u32[]{:S(2)}) collective-permute-start(bf16[2,64,1536]{2,1,0:T(8,128)(2,1)S(1)} %get-tuple-element.129), channel_id=1, source_target_pairs={{0,2},{1,3},{2,0},{3,1},{4,6},{5,7},{6,4},{7,5},{8,10},{9,11},{10,... | collective-permute-start | bytes 1179656 | tf_op jit(solution)/shard_map/ppermute | solution.py:273
  (97 other events, 831.2 us)
Sparse Core Ops, SparseCore 0:
  302.3 36.0 reduce-scatter.3

commit v4 on v3

--- a/solution.py
+++ b/solution.py
@@ -55,7 +55,7 @@
         (steps,),
         2 * rows * width * f,
         2 * (rows * width + width * f + rows * f),
-        vmem=14,
+        vmem=47,
         in_specs=[
             pl.BlockSpec((rows, width), lambda j: (0, 0)),
             pl.BlockSpec((width, bn), lambda j: (0, chunk * steps + j)),
@@ -85,7 +85,7 @@
         (width // bn,),
         2 * rows * width * f,
         2 * (rows * f + width * f + 4 * rows * width),
-        vmem=16,
+        vmem=47,
         in_specs=[
             pl.BlockSpec((rows, f), lambda j: (0, 0)),
             pl.BlockSpec((bn, f), lambda j: (j, chunk)),

time: 363 us -> 359 us (0.989)
  local copies, waits for them, and re-layouts: 61.4 us -> 40.9 us
  Pallas kernels: 133 us -> 153 us
  waiting for transfers between devices: 39.3 us -> 34.9 us
    unnamed x136 -> x114, local copies, waits for them, and re-layouts: 50.6 us -> 30 us
    pallas_call x4, Pallas kernels: 28 us -> 38 us  [input_grad_matmul(): matmul_call(body, 'input_grad', (width // bn,), 2 * rows * width * f, 2 *...]
    pallas_call x4, Pallas kernels: 28 us -> 36.1 us  [forward_matmul(): matmul_call(body, 'forward', (steps,), 2 * rows * width * f, 2 * (rows *...]
    ppermute x20, waiting for transfers between devices: 23.4 us -> 16.6 us  [onward(): return lax.ppermute(value, 'row', up + down)]
  transfers between devices with their start and end apart: 53 -> 53, of which waited for: 16 -> 16; matrix products, arithmetic and copies ran while one was open for 4% -> 4% of each run, Pallas kernels for 35% -> 40%
where the time goes in v4:
time: 359 us; the launch traced here: 356 us
  Pallas kernels  153 us (43%)
  starting transfers between devices  103 us (29%)
  local copies, waits for them, and re-layouts  40.9 us (11%)
  waiting for transfers between devices  34.9 us (10%)
  between operations  14.9 us (4%)
  other arithmetic  8.58 us (2%)
    ppermute x20, starting transfers between devices, onward(): return lax.ppermute(value, 'row', up + down)  60.2 us
    pallas_call x4, Pallas kernels, input_grad_matmul(): matmul_call(body, 'input_grad', (width // bn,), 2 * rows * width * f, 2 *...  38 us
    pallas_call x4, Pallas kernels, forward_matmul(): matmul_call(body, 'forward', (steps,), 2 * rows * width * f, 2 * (rows *...  36.1 us
    unnamed x114, local copies, waits for them, and re-layouts  30 us
    pallas_call x12, Pallas kernels, message_kernel(): matmul_call(body, 'message', None, 0, 0, vmem=8, grid_spec=pltpu.Prefetch...  28.1 us
    ppermute x21, starting transfers between devices, swap(): return lax.ppermute(value, 'row', [(r, r ^ 1) for r in range(n_row)])  27.6 us
    pallas_call x2, Pallas kernels, weight_grad_matmul(): matmul_call(body, 'weight_grad', (steps,), 2 * n * rows * width * f, 2 *...  24.9 us
    pallas_call x4, Pallas kernels, gelu_kernel(): matmul_call(body, 'gelu', None, 0, 0, vmem=8, grid_spec=pltpu.PrefetchSca...  19.6 us
  transfers between devices with their start and end apart: 53, of which 16 were waited for; matrix products, arithmetic and copies ran while one was open for 4% of the time, Pallas kernels for 40%

profile of v4, /device:TPU:0, one launch (start us, length us, event | category | flops | bytes accessed | tf_op | source)
XLA Modules:
  0.0 355.9 jit_solution(13098097706863975567)
XLA Ops:
  12.8 7.6 %collective-permute-done = bf16[2,64,1536]{2,1,0:T(8,128)(2,1)S(1)} collective-permute-done((bf16[2,64,1536]{2,1,0:T(8,128)(2,1)S(1)}, bf16[2,64,1536]{2,1,0:T(8,128)(2,1)S(1)}, u32[]{:S(2)}, u32[]{:S(2)}) %collective-permute-start) | collective-permute-done | bytes 393248 | tf_op jit(solution)/shard_map/ppermute | solution.py:273
  28.6 10.2 %forward.4 = bf16[512,3072]{1,0:T(8,128)(2,1)} custom-call(bf16[512,1536]{1,0:T(8,128)(2,1)S(1)} %bitcast.94, bf16[1536,6144]{1,0:T(8,128)(2,1)} %w_ref.15), custom_call_target="tpu_custom_call" | custom-call | flops 4831838208 | bytes 14155776 | tf_op jit(solution)/shard_map/forward/pallas_call | solution.py:52
  38.8 8.5 %forward.5 = bf16[512,3072]{1,0:T(8,128)(2,1)S(1)} custom-call(bf16[512,1536]{1,0:T(8,128)(2,1)S(1)} %bitcast.95, bf16[1536,6144]{1,0:T(8,128)(2,1)} %w_ref.15), custom_call_target="tpu_custom_call" | custom-call | flops 4831838208 | bytes 14155776 | tf_op jit(solution)/shard_map/forward/pallas_call | solution.py:52
  70.8 5.3 %collective-permute-start.7 = (bf16[2,64,3072]{2,1,0:T(8,128)(2,1)}, bf16[2,64,3072]{2,1,0:T(8,128)(2,1)}, u32[]{:S(2)}, u32[]{:S(2)}) collective-permute-start(bf16[2,64,3072]{2,1,0:T(8,128)(2,1)} %message.14), channel_id=1, source_target_pairs={{0,8},{8,16},{28,20},{20,12},{1,9},{9,17},{29,21},{21,13},{2,10},{... | collective-permute-start | bytes 2359304 | tf_op jit(solution)/shard_map/ppermute | solution.py:270
  96.1 9.0 %forward.6 = bf16[512,3072]{1,0:T(8,128)(2,1)S(1)} custom-call(bf16[512,1536]{1,0:T(8,128)(2,1)S(1)} %bitcast.97, bf16[1536,6144]{1,0:T(8,128)(2,1)} %w_ref.15), custom_call_target="tpu_custom_call" | custom-call | flops 4831838208 | bytes 14155776 | tf_op jit(solution)/shard_map/forward/pallas_call | solution.py:52
  112.8 8.5 %forward.7 = bf16[512,3072]{1,0:T(8,128)(2,1)S(1)} custom-call(bf16[512,1536]{1,0:T(8,128)(2,1)S(1)} %bitcast.98, bf16[1536,6144]{1,0:T(8,128)(2,1)} %w_ref.15), custom_call_target="tpu_custom_call" | custom-call | flops 4831838208 | bytes 14155776 | tf_op jit(solution)/shard_map/forward/pallas_call | solution.py:52
  125.6 5.2 %gelu.4 = (bf16[2,64,3072]{2,1,0:T(8,128)(2,1)S(1)}, bf16[128,6144]{1,0:T(8,128)(2,1)}) custom-call(s32[1]{0:T(128)} %bitcast.core_ref, bf16[4,2,64,3072]{3,2,1,0:T(8,128)(2,1)} %bitcast.17.part_ref, bf16[4,2,64,3072]{3,2,1,0:T(8,128)(2,1)} %collective-permute-done.4.theirs_ref, bf16[2,64,3072]{2,1,0:T(8,128)(2,1)} %collective-permute-done.8.came_ref, ...), custom_call_target="tpu_custom_call" | custom-call | tf_op jit(solution)/shard_map/gelu/pallas_call | solution.py:187
  133.7 5.0 %gelu.5 = (bf16[2,64,3072]{2,1,0:T(8,128)(2,1)S(1)}, bf16[128,6144]{1,0:T(8,128)(2,1)}) custom-call(s32[1]{0:T(128)} %bitcast.core_ref, bf16[4,2,64,3072]{3,2,1,0:T(8,128)(2,1)S(1)} %bitcast.79, bf16[4,2,64,3072]{3,2,1,0:T(8,128)(2,1)} %collective-permute-done.6.theirs_ref, ...), custom_call_target="tpu_custom_call", output_to_operand_aliasing={{1}: (7, {})} | custom-call | tf_op jit(solution)/shard_map/gelu/pallas_call | solution.py:187
  144.8 4.8 %collective-permute-start.25 = (bf16[2,64,3072]{2,1,0:T(8,128)(2,1)S(1)}, bf16[2,64,3072]{2,1,0:T(8,128)(2,1)}, u32[]{:S(2)}, u32[]{:S(2)}) collective-permute-start(bf16[2,64,3072]{2,1,0:T(8,128)(2,1)S(1)} %message.19), channel_id=1, source_target_pairs={{0,8},{8,16},{16,24},{28,20},{20,12},{12,4},{1,9},{9,17},{17,25},{... | collective-permute-start | bytes 2359304 | tf_op jit(solution)/shard_map/ppermute | solution.py:270
  155.0 4.8 %collective-permute-start.23 = (bf16[2,64,3072]{2,1,0:T(8,128)(2,1)}, bf16[2,64,3072]{2,1,0:T(8,128)(2,1)}, u32[]{:S(2)}, u32[]{:S(2)}) collective-permute-start(bf16[2,64,3072]{2,1,0:T(8,128)(2,1)} %message.18), channel_id=1, source_target_pairs={{0,8},{8,16},{16,24},{28,20},{20,12},{12,4},{1,9},{9,17},{17,25},{... | collective-permute-start | bytes 2359304 | tf_op jit(solution)/shard_map/ppermute | solution.py:270
  167.3 4.7 %collective-permute-start.29 = (bf16[2,64,3072]{2,1,0:T(8,128)(2,1)}, bf16[2,64,3072]{2,1,0:T(8,128)(2,1)}, u32[]{:S(2)}, u32[]{:S(2)}) collective-permute-start(bf16[2,64,3072]{2,1,0:T(8,128)(2,1)} %copy-done.55), channel_id=1, source_target_pairs={{0,8},{8,16},{16,24},{28,20},{20,12},{12,4},{1,9},{9,17},{17,25},{... | collective-permute-start | bytes 2359304 | tf_op jit(solution)/shard_map/ppermute | solution.py:270
  181.0 5.2 %collective-permute-start.28 = (bf16[2,64,3072]{2,1,0:T(8,128)(2,1)}, bf16[2,64,3072]{2,1,0:T(8,128)(2,1)}, u32[]{:S(2)}, u32[]{:S(2)}) collective-permute-start(bf16[2,64,3072]{2,1,0:T(8,128)(2,1)} %copy-done.52), channel_id=1, source_target_pairs={{0,8},{8,16},{16,24},{28,20},{20,12},{12,4},{1,9},{9,17},{17,25},{... | collective-permute-start | bytes 2359304 | tf_op jit(solution)/shard_map/ppermute | solution.py:270
  194.8 9.7 %input_grad.4.rest_0_ = f32[512,1536]{1,0:T(8,128)S(1)} custom-call(bf16[512,3072]{1,0:T(8,128)(2,1)S(1)} %bitcast.100, bf16[1536,6144]{1,0:T(8,128)(2,1)} %w_ref.15), custom_call_target="tpu_custom_call" | custom-call | flops 4831838208 | bytes 18874368 | tf_op jit(solution)/shard_map/input_grad/pallas_call | solution.py:82
  215.6 10.5 %input_grad.5 = bf16[512,1536]{1,0:T(8,128)(2,1)S(1)} custom-call(bf16[512,3072]{1,0:T(8,128)(2,1)S(1)} %bitcast.90, bf16[1536,6144]{1,0:T(8,128)(2,1)} %w_ref.15, f32[512,1536]{1,0:T(8,128)} %copy-done.21), custom_call_target="tpu_custom_call" | custom-call | flops 4831838208 | bytes 18874368 | tf_op jit(solution)/shard_map/input_grad/pallas_call | solution.py:82
  232.6 4.7 %gelu.6 = (bf16[2,64,3072]{2,1,0:T(8,128)(2,1)S(1)}, bf16[128,6144]{1,0:T(8,128)(2,1)}) custom-call(s32[1]{0:T(128)} %bitcast.core_ref, bf16[4,2,64,3072]{3,2,1,0:T(8,128)(2,1)S(1)} %bitcast.89, bf16[4,2,64,3072]{3,2,1,0:T(8,128)(2,1)S(1)} %copy-done.7, bf16[2,64,3072]{2,1,0:T(8,128)(2,1)} %collective-permute-done.34.came_ref, ...), custom_call_target="tpu_custom_call", output_to_operand_aliasing={{1}: (7, {})} | custom-call | tf_op jit(solution)/shard_map/gelu/pallas_call | solution.py:187
  239.1 4.8 %gelu.7 = (bf16[2,64,3072]{2,1,0:T(8,128)(2,1)S(1)}, bf16[128,6144]{1,0:T(8,128)(2,1)}) custom-call(s32[1]{0:T(128)} %bitcast.core_ref, bf16[4,2,64,3072]{3,2,1,0:T(8,128)(2,1)S(1)} %bitcast.84, bf16[4,2,64,3072]{3,2,1,0:T(8,128)(2,1)S(1)} %copy-done.10, bf16[2,64,3072]{2,1,0:T(8,128)(2,1)} %collective-permute-done.32.came_ref, ...), custom_call_target="tpu_custom_call", output_to_operand_aliasing={{1}: (7, {})} | custom-call | tf_op jit(solution)/shard_map/gelu/pallas_call | solution.py:187
  250.9 6.1 %collective-permute-done.37.refs_1_ = bf16[2,64,3072]{2,1,0:T(8,128)(2,1)S(1)} collective-permute-done((bf16[2,64,3072]{2,1,0:T(8,128)(2,1)S(1)}, bf16[2,64,3072]{2,1,0:T(8,128)(2,1)S(1)}, u32[]{:S(2)}, u32[]{:S(2)}) %collective-permute-start.37) | collective-permute-done | bytes 786464 | tf_op jit(solution)/shard_map/ppermute | solution.py:270
  261.4 6.5 %collective-permute-start.43 = (bf16[2,64,3072]{2,1,0:T(8,128)(2,1)S(1)}, bf16[2,64,3072]{2,1,0:T(8,128)(2,1)S(1)}, u32[]{:S(2)}, u32[]{:S(2)}) collective-permute-start(bf16[2,64,3072]{2,1,0:T(8,128)(2,1)S(1)} %collective-permute-done.41.refs_2_), channel_id=1, source_target_pairs={{0,4},{4,0},{8,12},{12,8},{16,20},{20,16},{24,28},{28,24},{1,5},{5... | collective-permute-start | bytes 2359304 | tf_op jit(solution)/shard_map/ppermute | solution.py:265
  269.8 5.6 %collective-permute-start.46 = (bf16[2,64,3072]{2,1,0:T(8,128)(2,1)S(1)}, bf16[2,64,3072]{2,1,0:T(8,128)(2,1)S(1)}, u32[]{:S(2)}, u32[]{:S(2)}) collective-permute-start(bf16[2,64,3072]{2,1,0:T(8,128)(2,1)S(1)} %collective-permute-done.40.refs_2_), channel_id=1, source_target_pairs={{0,4},{4,0},{8,12},{12,8},{16,20},{20,16},{24,28},{28,24},{1,5},{5... | collective-permute-start | bytes 2359304 | tf_op jit(solution)/shard_map/ppermute | solution.py:265
  278.3 6.5 %collective-permute-start.47 = (bf16[2,64,3072]{2,1,0:T(8,128)(2,1)S(1)}, bf16[2,64,3072]{2,1,0:T(8,128)(2,1)S(1)}, u32[]{:S(2)}, u32[]{:S(2)}) collective-permute-start(bf16[2,64,3072]{2,1,0:T(8,128)(2,1)S(1)} %collective-permute-done.45.refs_3_), channel_id=1, source_target_pairs={{0,4},{4,0},{8,12},{12,8},{16,20},{20,16},{24,28},{28,24},{1,5},{5... | collective-permute-start | bytes 2359304 | tf_op jit(solution)/shard_map/ppermute | solution.py:265
  287.6 8.6 %input_grad.6.rest_0_ = f32[512,1536]{1,0:T(8,128)S(1)} custom-call(bf16[512,3072]{1,0:T(8,128)(2,1)S(1)} %bitcast.102, bf16[1536,6144]{1,0:T(8,128)(2,1)} %w_ref.15), custom_call_target="tpu_custom_call" | custom-call | flops 4831838208 | bytes 18874368 | tf_op jit(solution)/shard_map/input_grad/pallas_call | solution.py:82
  309.1 9.2 %input_grad.7 = bf16[512,1536]{1,0:T(8,128)(2,1)S(1)} custom-call(bf16[512,3072]{1,0:T(8,128)(2,1)S(1)} %bitcast.92, bf16[1536,6144]{1,0:T(8,128)(2,1)} %w_ref.15, f32[512,1536]{1,0:T(8,128)} %copy-done.20), custom_call_target="tpu_custom_call" | custom-call | flops 4831838208 | bytes 18874368 | tf_op jit(solution)/shard_map/input_grad/pallas_call | solution.py:82
  322.0 12.4 %weight_grad.2.refs_4_ = bf16[1536,6144]{1,0:T(8,128)(2,1)} custom-call(bf16[1536,512]{1,0:T(8,128)(2,1)S(1)} %bitcast.104, bf16[1536,512]{1,0:T(8,128)(2,1)S(1)} %bitcast.106, bf16[512,3072]{1,0:T(8,128)(2,1)S(1)} %bitcast.101, bf16[512,3072]{1,0:T(8,128)(2,1)S(1)} %bitcast.103), custom_call_target="tpu_custom_call" | custom-call | flops 9663676416 | bytes 18874368 | tf_op jit(solution)/shard_map/weight_grad/pallas_call | solution.py:113
  334.4 12.4 %weight_grad.3 = bf16[1536,6144]{1,0:T(8,128)(2,1)} custom-call(bf16[1536,512]{1,0:T(8,128)(2,1)S(1)} %bitcast.105, bf16[1536,512]{1,0:T(8,128)(2,1)S(1)} %bitcast.107, bf16[512,3072]{1,0:T(8,128)(2,1)S(1)} %bitcast.91, bf16[512,3072]{1,0:T(8,128)(2,1)S(1)} %bitcast.93, bf16[1536,6144]{1,0:T(8,128)(2,1)} %weight_grad.2.refs_4_), custom_call_target="tpu_custom_call", output_to_operand_aliasing={{}: (4, {})} | custom-call | flops 9663676416 | bytes 18874368 | tf_op jit(solution)/shard_map/weight_grad/pallas_call | solution.py:113
  (251 shorter events, 165.3 us)
Async XLA Ops:
  7.2 340.0 %reduce-scatter.4.cloned.1.call-start = ((), (), s32[]{:S(2)}) async-start(), calls=%async_computation.1 | async-start | bytes 1966080
  50.0 13.1 %collective-permute-start.5 = (bf16[2,64,3072]{2,1,0:T(8,128)(2,1)S(1)}, bf16[2,64,3072]{2,1,0:T(8,128)(2,1)S(1)}, u32[]{:S(2)}, u32[]{:S(2)}) collective-permute-start(bf16[2,64,3072]{2,1,0:T(8,128)(2,1)S(1)} %message.12), channel_id=1, source_target_pairs={{0,8},{28,20},{1,9},{29,21},{2,10},{30,22},{3,11},{31,23}} | collective-permute-start | bytes 2359304 | tf_op jit(solution)/shard_map/ppermute | solution.py:270
  56.2 19.9 %collective-permute-start.9 = (bf16[2,64,3072]{2,1,0:T(8,128)(2,1)}, bf16[2,64,3072]{2,1,0:T(8,128)(2,1)}, u32[]{:S(2)}, u32[]{:S(2)}) collective-permute-start(bf16[2,64,3072]{2,1,0:T(8,128)(2,1)} %message.13), channel_id=1, source_target_pairs={{0,8},{28,20},{1,9},{29,21},{2,10},{30,22},{3,11},{31,23}} | collective-permute-start | bytes 2359304 | tf_op jit(solution)/shard_map/ppermute | solution.py:270
  64.8 14.4 %collective-permute-start.11 = (bf16[2,64,1536]{2,1,0:T(8,128)(2,1)}, bf16[2,64,1536]{2,1,0:T(8,128)(2,1)}, u32[]{:S(2)}, u32[]{:S(2)}) collective-permute-start(bf16[2,64,1536]{2,1,0:T(8,128)(2,1)} %get-tuple-element.139), channel_id=1, source_target_pairs={{0,1},{1,0},{2,3},{3,2},{4,5},{5,4},{6,7},{7,6},{8,9},{9,8},{10,11... | collective-permute-start | bytes 1179656 | tf_op jit(solution)/shard_map/ppermute | solution.py:273
  66.3 12.9 %collective-permute-start.12 = (bf16[2,64,1536]{2,1,0:T(8,128)(2,1)}, bf16[2,64,1536]{2,1,0:T(8,128)(2,1)}, u32[]{:S(2)}, u32[]{:S(2)}) collective-permute-start(bf16[2,64,1536]{2,1,0:T(8,128)(2,1)} %get-tuple-element.139), channel_id=1, source_target_pairs={{0,2},{1,3},{2,0},{3,1},{4,6},{5,7},{6,4},{7,5},{8,10},{9,11},{10,... | collective-permute-start | bytes 1179656 | tf_op jit(solution)/shard_map/ppermute | solution.py:273
  70.8 15.1 %collective-permute-start.7 = (bf16[2,64,3072]{2,1,0:T(8,128)(2,1)}, bf16[2,64,3072]{2,1,0:T(8,128)(2,1)}, u32[]{:S(2)}, u32[]{:S(2)}) collective-permute-start(bf16[2,64,3072]{2,1,0:T(8,128)(2,1)} %message.14), channel_id=1, source_target_pairs={{0,8},{8,16},{28,20},{20,12},{1,9},{9,17},{29,21},{21,13},{2,10},{... | collective-permute-start | bytes 2359304 | tf_op jit(solution)/shard_map/ppermute | solution.py:270
  84.6 20.7 %collective-permute-start.10 = (bf16[2,64,3072]{2,1,0:T(8,128)(2,1)}, bf16[2,64,3072]{2,1,0:T(8,128)(2,1)S(1)}, u32[]{:S(2)}, u32[]{:S(2)}) collective-permute-start(bf16[2,64,3072]{2,1,0:T(8,128)(2,1)} %copy-done.49), channel_id=1, source_target_pairs={{0,8},{8,16},{28,20},{20,12},{1,9},{9,17},{29,21},{21,13},{2,10},{... | collective-permute-start | bytes 2359304 | tf_op jit(solution)/shard_map/ppermute | solution.py:270
  85.9 37.6 %collective-permute-start.18 = (bf16[128,6144]{1,0:T(8,128)(2,1)}, bf16[128,6144]{1,0:T(8,128)(2,1)S(1)}, u32[]{:S(2)}, u32[]{:S(2)}) collective-permute-start(bf16[128,6144]{1,0:T(8,128)(2,1)} %mine_ref.7), channel_id=1, source_target_pairs={{0,4},{4,0},{8,12},{12,8},{16,20},{20,16},{24,28},{28,24},{1,5},{5... | collective-permute-start | bytes 4718600 | tf_op jit(solution)/shard_map/ppermute | solution.py:265
  89.1 32.2 %collective-permute-start.8 = (bf16[2,64,3072]{2,1,0:T(8,128)(2,1)}, bf16[2,64,3072]{2,1,0:T(8,128)(2,1)}, u32[]{:S(2)}, u32[]{:S(2)}) collective-permute-start(bf16[2,64,3072]{2,1,0:T(8,128)(2,1)} %message.15), channel_id=1, source_target_pairs={{0,8},{8,16},{16,24},{28,20},{20,12},{12,4},{1,9},{9,17},{17,25},{... | collective-permute-start | bytes 2359304 | tf_op jit(solution)/shard_map/ppermute | solution.py:270
  105.1 38.5 %collective-permute-start.24 = (bf16[4,2,64,3072]{3,2,1,0:T(8,128)(2,1)S(1)}, bf16[4,2,64,3072]{3,2,1,0:T(8,128)(2,1)S(1)}, u32[]{:S(2)}, u32[]{:S(2)}) collective-permute-start(bf16[4,2,64,3072]{3,2,1,0:T(8,128)(2,1)S(1)} %bitcast.85), channel_id=1, source_target_pairs={{0,4},{4,0},{8,12},{12,8},{16,20},{20,16},{24,28},{28,24},{1,5},{5... | collective-permute-start | bytes 9437192 | tf_op jit(solution)/shard_map/ppermute | solution.py:265
  121.4 31.6 %collective-permute-start.15 = (bf16[4,2,64,3072]{3,2,1,0:T(8,128)(2,1)S(1)}, bf16[4,2,64,3072]{3,2,1,0:T(8,128)(2,1)S(1)}, u32[]{:S(2)}, u32[]{:S(2)}) collective-permute-start(bf16[4,2,64,3072]{3,2,1,0:T(8,128)(2,1)S(1)} %bitcast.80), channel_id=1, source_target_pairs={{0,4},{4,0},{8,12},{12,8},{16,20},{20,16},{24,28},{28,24},{1,5},{5... | collective-permute-start | bytes 9437192 | tf_op jit(solution)/shard_map/ppermute | solution.py:265
  130.8 12.3 %collective-permute-start.21 = (bf16[2,64,3072]{2,1,0:T(8,128)(2,1)S(1)}, bf16[2,64,3072]{2,1,0:T(8,128)(2,1)S(1)}, u32[]{:S(2)}, u32[]{:S(2)}) collective-permute-start(bf16[2,64,3072]{2,1,0:T(8,128)(2,1)S(1)} %get-tuple-element.86.refs_0_), channel_id=1, source_target_pairs={{0,8},{8,16},{16,24},{28,20},{20,12},{12,4},{1,9},{9,17},{17,25},{... | collective-permute-start | bytes 2359304 | tf_op jit(solution)/shard_map/ppermute | solution.py:270
  138.7 12.9 %collective-permute-start.20 = (bf16[2,64,3072]{2,1,0:T(8,128)(2,1)S(1)}, bf16[2,64,3072]{2,1,0:T(8,128)(2,1)S(1)}, u32[]{:S(2)}, u32[]{:S(2)}) collective-permute-start(bf16[2,64,3072]{2,1,0:T(8,128)(2,1)S(1)} %get-tuple-element.85.refs_0_), channel_id=1, source_target_pairs={{0,8},{8,16},{16,24},{28,20},{20,12},{12,4},{1,9},{9,17},{17,25},{... | collective-permute-start | bytes 2359304 | tf_op jit(solution)/shard_map/ppermute | solution.py:270
  144.8 15.2 %collective-permute-start.25 = (bf16[2,64,3072]{2,1,0:T(8,128)(2,1)S(1)}, bf16[2,64,3072]{2,1,0:T(8,128)(2,1)}, u32[]{:S(2)}, u32[]{:S(2)}) collective-permute-start(bf16[2,64,3072]{2,1,0:T(8,128)(2,1)S(1)} %message.19), channel_id=1, source_target_pairs={{0,8},{8,16},{16,24},{28,20},{20,12},{12,4},{1,9},{9,17},{17,25},{... | collective-permute-start | bytes 2359304 | tf_op jit(solution)/shard_map/ppermute | solution.py:270
  155.0 17.0 %collective-permute-start.23 = (bf16[2,64,3072]{2,1,0:T(8,128)(2,1)}, bf16[2,64,3072]{2,1,0:T(8,128)(2,1)}, u32[]{:S(2)}, u32[]{:S(2)}) collective-permute-start(bf16[2,64,3072]{2,1,0:T(8,128)(2,1)} %message.18), channel_id=1, source_target_pairs={{0,8},{8,16},{16,24},{28,20},{20,12},{12,4},{1,9},{9,17},{17,25},{... | collective-permute-start | bytes 2359304 | tf_op jit(solution)/shard_map/ppermute | solution.py:270
  167.3 13.7 %collective-permute-start.29 = (bf16[2,64,3072]{2,1,0:T(8,128)(2,1)}, bf16[2,64,3072]{2,1,0:T(8,128)(2,1)}, u32[]{:S(2)}, u32[]{:S(2)}) collective-permute-start(bf16[2,64,3072]{2,1,0:T(8,128)(2,1)} %copy-done.55), channel_id=1, source_target_pairs={{0,8},{8,16},{16,24},{28,20},{20,12},{12,4},{1,9},{9,17},{17,25},{... | collective-permute-start | bytes 2359304 | tf_op jit(solution)/shard_map/ppermute | solution.py:270
  181.0 23.6 %collective-permute-start.28 = (bf16[2,64,3072]{2,1,0:T(8,128)(2,1)}, bf16[2,64,3072]{2,1,0:T(8,128)(2,1)}, u32[]{:S(2)}, u32[]{:S(2)}) collective-permute-start(bf16[2,64,3072]{2,1,0:T(8,128)(2,1)} %copy-done.52), channel_id=1, source_target_pairs={{0,8},{8,16},{16,24},{28,20},{20,12},{12,4},{1,9},{9,17},{17,25},{... | collective-permute-start | bytes 2359304 | tf_op jit(solution)/shard_map/ppermute | solution.py:270
  204.7 22.6 %collective-permute-start.34 = (bf16[2,64,3072]{2,1,0:T(8,128)(2,1)}, bf16[2,64,3072]{2,1,0:T(8,128)(2,1)}, u32[]{:S(2)}, u32[]{:S(2)}) collective-permute-start(bf16[2,64,3072]{2,1,0:T(8,128)(2,1)} %message.22), channel_id=1, source_target_pairs={{0,8},{8,16},{16,24},{28,20},{20,12},{12,4},{1,9},{9,17},{17,25},{... | collective-permute-start | bytes 2359304 | tf_op jit(solution)/shard_map/ppermute | solution.py:270
  210.2 17.1 %collective-permute-start.32 = (bf16[2,64,3072]{2,1,0:T(8,128)(2,1)}, bf16[2,64,3072]{2,1,0:T(8,128)(2,1)}, u32[]{:S(2)}, u32[]{:S(2)}) collective-permute-start(bf16[2,64,3072]{2,1,0:T(8,128)(2,1)} %message.23), channel_id=1, source_target_pairs={{0,8},{8,16},{16,24},{28,20},{20,12},{12,4},{1,9},{9,17},{17,25},{... | collective-permute-start | bytes 2359304 | tf_op jit(solution)/shard_map/ppermute | solution.py:270
  243.9 13.1 %collective-permute-start.37 = (bf16[2,64,3072]{2,1,0:T(8,128)(2,1)S(1)}, bf16[2,64,3072]{2,1,0:T(8,128)(2,1)S(1)}, u32[]{:S(2)}, u32[]{:S(2)}) collective-permute-start(bf16[2,64,3072]{2,1,0:T(8,128)(2,1)S(1)} %get-tuple-element.112.refs_0_), channel_id=1, source_target_pairs={{0,8},{8,16},{16,24},{28,20},{20,12},{12,4},{1,9},{9,17},{17,25},{... | collective-permute-start | bytes 2359304 | tf_op jit(solution)/shard_map/ppermute | solution.py:270
  284.8 13.1 %collective-permute-start.44 = (bf16[2,64,3072]{2,1,0:T(8,128)(2,1)S(1)}, bf16[2,64,3072]{2,1,0:T(8,128)(2,1)}, u32[]{:S(2)}, u32[]{:S(2)}) collective-permute-start(bf16[2,64,3072]{2,1,0:T(8,128)(2,1)S(1)} %collective-permute-done.40.refs_2_), channel_id=1, source_target_pairs={{16,24},{12,4},{17,25},{13,5},{18,26},{14,6},{19,27},{15,7}} | collective-permute-start | bytes 2359304 | tf_op jit(solution)/shard_map/ppermute | solution.py:270
  318.4 28.5 %collective-permute-start.49 = (bf16[2,64,1536]{2,1,0:T(8,128)(2,1)S(1)}, bf16[2,64,1536]{2,1,0:T(8,128)(2,1)S(1)}, u32[]{:S(2)}, u32[]{:S(2)}) collective-permute-start(bf16[2,64,1536]{2,1,0:T(8,128)(2,1)S(1)} %get-tuple-element.127), channel_id=1, source_target_pairs={{0,1},{1,0},{2,3},{3,2},{4,5},{5,4},{6,7},{7,6},{8,9},{9,8},{10,11... | collective-permute-start | bytes 1179656 | tf_op jit(solution)/shard_map/ppermute | solution.py:273
  319.7 27.2 %collective-permute-start.51 = (bf16[2,64,1536]{2,1,0:T(8,128)(2,1)S(1)}, bf16[2,64,1536]{2,1,0:T(8,128)(2,1)S(1)}, u32[]{:S(2)}, u32[]{:S(2)}) collective-permute-start(bf16[2,64,1536]{2,1,0:T(8,128)(2,1)S(1)} %get-tuple-element.128), channel_id=1, source_target_pairs={{0,3},{1,2},{2,1},{3,0},{4,7},{5,6},{6,5},{7,4},{8,11},{9,10},{10,... | collective-permute-start | bytes 1179656 | tf_op jit(solution)/shard_map/ppermute | solution.py:273
  321.5 25.4 %collective-permute-start.50 = (bf16[2,64,1536]{2,1,0:T(8,128)(2,1)S(1)}, bf16[2,64,1536]{2,1,0:T(8,128)(2,1)S(1)}, u32[]{:S(2)}, u32[]{:S(2)}) collective-permute-start(bf16[2,64,1536]{2,1,0:T(8,128)(2,1)S(1)} %get-tuple-element.129), channel_id=1, source_target_pairs={{0,2},{1,3},{2,0},{3,1},{4,6},{5,7},{6,4},{7,5},{8,10},{9,11},{10,... | collective-permute-start | bytes 1179656 | tf_op jit(solution)/shard_map/ppermute | solution.py:273
  (86 other events, 679.1 us)
Sparse Core Ops, SparseCore 0:
  301.5 43.0 reduce-scatter.3

commit v5 on v4

--- a/solution.py
+++ b/solution.py
@@ -94,6 +94,37 @@
         out_specs=pl.BlockSpec((rows, bn), lambda j: (0, j)),
         out_shape=jax.ShapeDtypeStruct((rows, width), BF16 if last else F32),
     )(g, weight, *kept)
+
+
+def input_grad_whole(gs, weight):
+    rows, f = gs[0].shape
+    width, units = weight.shape
+    bn = tile(width, 256)
+
+    def body(*refs):
+        g_refs, w_ref, out = refs[:-2], refs[-2], refs[-1]
+        total = 0.0
+        for chunk, g_ref in enumerate(g_refs):
+            total += lax.dot_general(
+                g_ref[...],
+                w_ref[:, chunk * f : (chunk + 1) * f],
+                (((1,), (1,)), ((), ())),
+                preferred_element_type=F32,
+            )
+        out[...] = total.astype(BF16)
+
+    return matmul_call(
+        body,
+        "input_grad_whole",
+        (width // bn,),
+        2 * rows * width * units,
+        2 * (rows * units + width * units + rows * width),
+        vmem=47,
+        in_specs=[pl.BlockSpec((rows, f), lambda j: (0, 0))] * len(gs)
+        + [pl.BlockSpec((bn, units), lambda j: (j, 0))],
+        out_specs=pl.BlockSpec((rows, bn), lambda j: (0, j)),
+        out_shape=jax.ShapeDtypeStruct((rows, width), BF16),
+    )(*gs, weight)
 
 
 def weight_grad_matmul(lefts, rights, buffer, chunk, units):
@@ -237,7 +268,7 @@
         None,
         0,
         0,
-        vmem=10,
+        vmem=47,
         grid_spec=pltpu.PrefetchScalarGridSpec(
             num_scalar_prefetch=1,
             grid=(1,),
@@ -333,6 +364,16 @@
             env["g", half, chunk], weight, chunk, env.get(("total", half)), last
         )
         done.append(("total", half))
+
+    def backward_half(q, i):
+        collect(q, i)
+        half = items[q][i][0]
+        if q == STREAMS - 1:
+            gs = [env["g", half, chunk] for chunk in range(CHUNKS)]
+            env["total", half] = input_grad_whole(gs, weight)
+            done.append(("total", half))
+        else:
+            done.append(("g", *items[q][i]))
 
     def backward_weight(chunk):
         halves = range(HALVES)
@@ -452,7 +493,7 @@
                 if t_next == 1 and i_next == 1 and q < HALVES:
                     work.append((transpose, (q,), ("x", q)))
                 if t_next == depth - 2 and i_next > 0:
-                    work.append((backward_input, (q, i_next - 1), ("got", q, depth - 1)))
+                    work.append((backward_half, (q, i_next - 1), ("got", q, depth - 1)))
                 fence(("msg", q), *[name for _, _, name in work])
                 start(q, step + 1)
             else:

time: 359 us -> 359 us (level)
    pallas_call x4 -> x5, Pallas kernels: 6.46 us -> 27.8 us  [the longest x1 14.1 us: input_grad_whole(): matmul_call(body, 'input_grad_whole', (width // bn,), 2 * rows * width *...]
    pallas_call x4 -> x2, Pallas kernels: 38 us -> 18.6 us  [input_grad_matmul(): matmul_call(body, 'input_grad', (width // bn,), 2 * rows * width * f, 2 *...]
  transfers between devices with their start and end apart: 53 -> 53, of which waited for: 16 -> 17; matrix products, arithmetic and copies ran while one was open for 4% -> 4% of each run, Pallas kernels for 40% -> 40%
where the time goes in v5:
time: 359 us; the launch traced here: 357 us
  Pallas kernels  154 us (43%)
  starting transfers between devices  105 us (29%)
  local copies, waits for them, and re-layouts  40.6 us (11%)
  waiting for transfers between devices  35.1 us (10%)
  between operations  14.9 us (4%)
  other arithmetic  7.17 us (2%)
    ppermute x20, starting transfers between devices, onward(): return lax.ppermute(value, 'row', up + down)  59.7 us
    pallas_call x4, Pallas kernels, forward_matmul(): matmul_call(body, 'forward', (steps,), 2 * rows * width * f, 2 * (rows *...  36.1 us
    unnamed x114, local copies, waits for them, and re-layouts  29.8 us
    ppermute x21, starting transfers between devices, swap(): return lax.ppermute(value, 'row', [(r, r ^ 1) for r in range(n_row)])  29.4 us
    pallas_call x12, Pallas kernels, message_kernel(): matmul_call(body, 'message', None, 0, 0, vmem=8, grid_spec=pltpu.Prefetch...  27.3 us
    pallas_call x2, Pallas kernels, weight_grad_matmul(): matmul_call(body, 'weight_grad', (steps,), 2 * n * rows * width * f, 2 *...  24.9 us
    pallas_call x4, Pallas kernels, gelu_kernel(): matmul_call(body, 'gelu', None, 0, 0, vmem=8, grid_spec=pltpu.PrefetchSca...  19.6 us
    pallas_call x2, Pallas kernels, input_grad_matmul(): matmul_call(body, 'input_grad', (width // bn,), 2 * rows * width * f, 2 *...  18.6 us
  transfers between devices with their start and end apart: 53, of which 17 were waited for; matrix products, arithmetic and copies ran while one was open for 4% of the time, Pallas kernels for 40%

profile of v5, /device:TPU:0, one launch (start us, length us, event | category | flops | bytes accessed | tf_op | source)
XLA Modules:
  0.0 356.7 jit_solution(17891855351792707974)
XLA Ops:
  12.8 7.6 %collective-permute-done = bf16[2,64,1536]{2,1,0:T(8,128)(2,1)S(1)} collective-permute-done((bf16[2,64,1536]{2,1,0:T(8,128)(2,1)S(1)}, bf16[2,64,1536]{2,1,0:T(8,128)(2,1)S(1)}, u32[]{:S(2)}, u32[]{:S(2)}) %collective-permute-start) | collective-permute-done | bytes 393248 | tf_op jit(solution)/shard_map/ppermute | solution.py:304
  28.6 10.2 %forward.4 = bf16[512,3072]{1,0:T(8,128)(2,1)} custom-call(bf16[512,1536]{1,0:T(8,128)(2,1)S(1)} %bitcast.92, bf16[1536,6144]{1,0:T(8,128)(2,1)} %w_ref.11), custom_call_target="tpu_custom_call" | custom-call | flops 4831838208 | bytes 14155776 | tf_op jit(solution)/shard_map/forward/pallas_call | solution.py:52
  38.8 8.5 %forward.5 = bf16[512,3072]{1,0:T(8,128)(2,1)S(1)} custom-call(bf16[512,1536]{1,0:T(8,128)(2,1)S(1)} %bitcast.93, bf16[1536,6144]{1,0:T(8,128)(2,1)} %w_ref.11), custom_call_target="tpu_custom_call" | custom-call | flops 4831838208 | bytes 14155776 | tf_op jit(solution)/shard_map/forward/pallas_call | solution.py:52
  70.8 5.3 %collective-permute-start.7 = (bf16[2,64,3072]{2,1,0:T(8,128)(2,1)}, bf16[2,64,3072]{2,1,0:T(8,128)(2,1)}, u32[]{:S(2)}, u32[]{:S(2)}) collective-permute-start(bf16[2,64,3072]{2,1,0:T(8,128)(2,1)} %message.14), channel_id=1, source_target_pairs={{0,8},{8,16},{28,20},{20,12},{1,9},{9,17},{29,21},{21,13},{2,10},{... | collective-permute-start | bytes 2359304 | tf_op jit(solution)/shard_map/ppermute | solution.py:301
  96.1 9.0 %forward.6 = bf16[512,3072]{1,0:T(8,128)(2,1)S(1)} custom-call(bf16[512,1536]{1,0:T(8,128)(2,1)S(1)} %bitcast.95, bf16[1536,6144]{1,0:T(8,128)(2,1)} %w_ref.11), custom_call_target="tpu_custom_call" | custom-call | flops 4831838208 | bytes 14155776 | tf_op jit(solution)/shard_map/forward/pallas_call | solution.py:52
  112.8 8.5 %forward.7 = bf16[512,3072]{1,0:T(8,128)(2,1)S(1)} custom-call(bf16[512,1536]{1,0:T(8,128)(2,1)S(1)} %bitcast.96, bf16[1536,6144]{1,0:T(8,128)(2,1)} %w_ref.11), custom_call_target="tpu_custom_call" | custom-call | flops 4831838208 | bytes 14155776 | tf_op jit(solution)/shard_map/forward/pallas_call | solution.py:52
  125.6 5.2 %gelu.4 = (bf16[2,64,3072]{2,1,0:T(8,128)(2,1)S(1)}, bf16[128,6144]{1,0:T(8,128)(2,1)}) custom-call(s32[1]{0:T(128)} %bitcast.core_ref, bf16[4,2,64,3072]{3,2,1,0:T(8,128)(2,1)} %bitcast.17.part_ref, bf16[4,2,64,3072]{3,2,1,0:T(8,128)(2,1)} %collective-permute-done.4.theirs_ref, bf16[2,64,3072]{2,1,0:T(8,128)(2,1)} %collective-permute-done.8.came_ref, ...), custom_call_target="tpu_custom_call" | custom-call | tf_op jit(solution)/shard_map/gelu/pallas_call | solution.py:218
  133.7 5.0 %gelu.5 = (bf16[2,64,3072]{2,1,0:T(8,128)(2,1)S(1)}, bf16[128,6144]{1,0:T(8,128)(2,1)}) custom-call(s32[1]{0:T(128)} %bitcast.core_ref, bf16[4,2,64,3072]{3,2,1,0:T(8,128)(2,1)S(1)} %bitcast.79, bf16[4,2,64,3072]{3,2,1,0:T(8,128)(2,1)} %collective-permute-done.6.theirs_ref, ...), custom_call_target="tpu_custom_call", output_to_operand_aliasing={{1}: (7, {})} | custom-call | tf_op jit(solution)/shard_map/gelu/pallas_call | solution.py:218
  144.8 4.8 %collective-permute-start.25 = (bf16[2,64,3072]{2,1,0:T(8,128)(2,1)S(1)}, bf16[2,64,3072]{2,1,0:T(8,128)(2,1)}, u32[]{:S(2)}, u32[]{:S(2)}) collective-permute-start(bf16[2,64,3072]{2,1,0:T(8,128)(2,1)S(1)} %message.19), channel_id=1, source_target_pairs={{0,8},{8,16},{16,24},{28,20},{20,12},{12,4},{1,9},{9,17},{17,25},{... | collective-permute-start | bytes 2359304 | tf_op jit(solution)/shard_map/ppermute | solution.py:301
  155.0 4.8 %collective-permute-start.23 = (bf16[2,64,3072]{2,1,0:T(8,128)(2,1)}, bf16[2,64,3072]{2,1,0:T(8,128)(2,1)}, u32[]{:S(2)}, u32[]{:S(2)}) collective-permute-start(bf16[2,64,3072]{2,1,0:T(8,128)(2,1)} %message.18), channel_id=1, source_target_pairs={{0,8},{8,16},{16,24},{28,20},{20,12},{12,4},{1,9},{9,17},{17,25},{... | collective-permute-start | bytes 2359304 | tf_op jit(solution)/shard_map/ppermute | solution.py:301
  167.2 4.8 %collective-permute-start.29 = (bf16[2,64,3072]{2,1,0:T(8,128)(2,1)}, bf16[2,64,3072]{2,1,0:T(8,128)(2,1)}, u32[]{:S(2)}, u32[]{:S(2)}) collective-permute-start(bf16[2,64,3072]{2,1,0:T(8,128)(2,1)} %copy-done.55), channel_id=1, source_target_pairs={{0,8},{8,16},{16,24},{28,20},{20,12},{12,4},{1,9},{9,17},{17,25},{... | collective-permute-start | bytes 2359304 | tf_op jit(solution)/shard_map/ppermute | solution.py:301
  181.0 4.3 %collective-permute-start.28 = (bf16[2,64,3072]{2,1,0:T(8,128)(2,1)}, bf16[2,64,3072]{2,1,0:T(8,128)(2,1)S(1)}, u32[]{:S(2)}, u32[]{:S(2)}) collective-permute-start(bf16[2,64,3072]{2,1,0:T(8,128)(2,1)} %copy-done.52), channel_id=1, source_target_pairs={{0,8},{8,16},{16,24},{28,20},{20,12},{12,4},{1,9},{9,17},{17,25},{... | collective-permute-start | bytes 2359304 | tf_op jit(solution)/shard_map/ppermute | solution.py:301
  195.9 4.5 %collective-permute-start.34 = (bf16[2,64,3072]{2,1,0:T(8,128)(2,1)}, bf16[2,64,3072]{2,1,0:T(8,128)(2,1)}, u32[]{:S(2)}, u32[]{:S(2)}) collective-permute-start(bf16[2,64,3072]{2,1,0:T(8,128)(2,1)} %message.22), channel_id=1, source_target_pairs={{0,8},{8,16},{16,24},{28,20},{20,12},{12,4},{1,9},{9,17},{17,25},{... | collective-permute-start | bytes 2359304 | tf_op jit(solution)/shard_map/ppermute | solution.py:301
  208.9 14.1 %input_grad_whole.1 = bf16[512,1536]{1,0:T(8,128)(2,1)S(1)} custom-call(bf16[512,3072]{1,0:T(8,128)(2,1)S(1)} %bitcast.108, bf16[512,3072]{1,0:T(8,128)(2,1)} %bitcast.98, bf16[1536,6144]{1,0:T(8,128)(2,1)} %w_ref.11), custom_call_target="tpu_custom_call" | custom-call | flops 9663676416 | bytes 26738688 | tf_op jit(solution)/shard_map/input_grad_whole/pallas_call | solution.py:116
  229.5 4.7 %gelu.6 = (bf16[2,64,3072]{2,1,0:T(8,128)(2,1)S(1)}, bf16[128,6144]{1,0:T(8,128)(2,1)}) custom-call(s32[1]{0:T(128)} %bitcast.core_ref, bf16[4,2,64,3072]{3,2,1,0:T(8,128)(2,1)S(1)} %bitcast.89, bf16[4,2,64,3072]{3,2,1,0:T(8,128)(2,1)S(1)} %copy-done.7, bf16[2,64,3072]{2,1,0:T(8,128)(2,1)} %collective-permute-done.34.came_ref, ...), custom_call_target="tpu_custom_call", output_to_operand_aliasing={{1}: (7, {})} | custom-call | tf_op jit(solution)/shard_map/gelu/pallas_call | solution.py:218
  235.6 4.8 %gelu.7 = (bf16[2,64,3072]{2,1,0:T(8,128)(2,1)S(1)}, bf16[128,6144]{1,0:T(8,128)(2,1)}) custom-call(s32[1]{0:T(128)} %bitcast.core_ref, bf16[4,2,64,3072]{3,2,1,0:T(8,128)(2,1)S(1)} %bitcast.84, bf16[4,2,64,3072]{3,2,1,0:T(8,128)(2,1)S(1)} %copy-done.10, bf16[2,64,3072]{2,1,0:T(8,128)(2,1)} %collective-permute-done.32.came_ref, ...), custom_call_target="tpu_custom_call", output_to_operand_aliasing={{1}: (7, {})} | custom-call | tf_op jit(solution)/shard_map/gelu/pallas_call | solution.py:218
  247.8 5.6 %collective-permute-done.37.refs_1_ = bf16[2,64,3072]{2,1,0:T(8,128)(2,1)S(1)} collective-permute-done((bf16[2,64,3072]{2,1,0:T(8,128)(2,1)S(1)}, bf16[2,64,3072]{2,1,0:T(8,128)(2,1)S(1)}, u32[]{:S(2)}, u32[]{:S(2)}) %collective-permute-start.37) | collective-permute-done | bytes 786464 | tf_op jit(solution)/shard_map/ppermute | solution.py:301
  257.5 6.5 %collective-permute-start.43 = (bf16[2,64,3072]{2,1,0:T(8,128)(2,1)S(1)}, bf16[2,64,3072]{2,1,0:T(8,128)(2,1)S(1)}, u32[]{:S(2)}, u32[]{:S(2)}) collective-permute-start(bf16[2,64,3072]{2,1,0:T(8,128)(2,1)S(1)} %collective-permute-done.41.refs_2_), channel_id=1, source_target_pairs={{0,4},{4,0},{8,12},{12,8},{16,20},{20,16},{24,28},{28,24},{1,5},{5... | collective-permute-start | bytes 2359304 | tf_op jit(solution)/shard_map/ppermute | solution.py:296
  265.9 6.5 %collective-permute-start.46 = (bf16[2,64,3072]{2,1,0:T(8,128)(2,1)S(1)}, bf16[2,64,3072]{2,1,0:T(8,128)(2,1)S(1)}, u32[]{:S(2)}, u32[]{:S(2)}) collective-permute-start(bf16[2,64,3072]{2,1,0:T(8,128)(2,1)S(1)} %collective-permute-done.40.refs_2_), channel_id=1, source_target_pairs={{0,4},{4,0},{8,12},{12,8},{16,20},{20,16},{24,28},{28,24},{1,5},{5... | collective-permute-start | bytes 2359304 | tf_op jit(solution)/shard_map/ppermute | solution.py:296
  274.3 6.5 %collective-permute-start.47 = (bf16[2,64,3072]{2,1,0:T(8,128)(2,1)S(1)}, bf16[2,64,3072]{2,1,0:T(8,128)(2,1)S(1)}, u32[]{:S(2)}, u32[]{:S(2)}) collective-permute-start(bf16[2,64,3072]{2,1,0:T(8,128)(2,1)S(1)} %collective-permute-done.45.refs_3_), channel_id=1, source_target_pairs={{0,4},{4,0},{8,12},{12,8},{16,20},{20,16},{24,28},{28,24},{1,5},{5... | collective-permute-start | bytes 2359304 | tf_op jit(solution)/shard_map/ppermute | solution.py:296
  288.3 8.7 %input_grad.2.rest_0_ = f32[512,1536]{1,0:T(8,128)S(1)} custom-call(bf16[512,3072]{1,0:T(8,128)(2,1)S(1)} %bitcast.100, bf16[1536,6144]{1,0:T(8,128)(2,1)} %w_ref.11), custom_call_target="tpu_custom_call" | custom-call | flops 4831838208 | bytes 18874368 | tf_op jit(solution)/shard_map/input_grad/pallas_call | solution.py:82
  309.1 9.9 %input_grad.3 = bf16[512,1536]{1,0:T(8,128)(2,1)S(1)} custom-call(bf16[512,3072]{1,0:T(8,128)(2,1)S(1)} %bitcast.90, bf16[1536,6144]{1,0:T(8,128)(2,1)} %w_ref.11, f32[512,1536]{1,0:T(8,128)} %copy-done.19), custom_call_target="tpu_custom_call" | custom-call | flops 4831838208 | bytes 18874368 | tf_op jit(solution)/shard_map/input_grad/pallas_call | solution.py:82
  322.8 12.4 %weight_grad.2.refs_4_ = bf16[1536,6144]{1,0:T(8,128)(2,1)} custom-call(bf16[1536,512]{1,0:T(8,128)(2,1)S(1)} %bitcast.102, bf16[1536,512]{1,0:T(8,128)(2,1)S(1)} %bitcast.104, bf16[512,3072]{1,0:T(8,128)(2,1)S(1)} %bitcast.109, bf16[512,3072]{1,0:T(8,128)(2,1)S(1)} %bitcast.101), custom_call_target="tpu_custom_call" | custom-call | flops 9663676416 | bytes 18874368 | tf_op jit(solution)/shard_map/weight_grad/pallas_call | solution.py:144
  335.2 12.4 %weight_grad.3 = bf16[1536,6144]{1,0:T(8,128)(2,1)} custom-call(bf16[1536,512]{1,0:T(8,128)(2,1)S(1)} %bitcast.103, bf16[1536,512]{1,0:T(8,128)(2,1)S(1)} %bitcast.105, bf16[512,3072]{1,0:T(8,128)(2,1)S(1)} %bitcast.99, bf16[512,3072]{1,0:T(8,128)(2,1)S(1)} %bitcast.91, bf16[1536,6144]{1,0:T(8,128)(2,1)} %weight_grad.2.refs_4_), custom_call_target="tpu_custom_call", output_to_operand_aliasing={{}: (4, {})} | custom-call | flops 9663676416 | bytes 18874368 | tf_op jit(solution)/shard_map/weight_grad/pallas_call | solution.py:144
  (250 shorter events, 167.2 us)
Async XLA Ops:
  7.2 340.7 %reduce-scatter.4.cloned.1.call-start = ((), (), s32[]{:S(2)}) async-start(), calls=%async_computation.1 | async-start | bytes 1966080
  50.0 13.1 %collective-permute-start.5 = (bf16[2,64,3072]{2,1,0:T(8,128)(2,1)S(1)}, bf16[2,64,3072]{2,1,0:T(8,128)(2,1)S(1)}, u32[]{:S(2)}, u32[]{:S(2)}) collective-permute-start(bf16[2,64,3072]{2,1,0:T(8,128)(2,1)S(1)} %message.12), channel_id=1, source_target_pairs={{0,8},{28,20},{1,9},{29,21},{2,10},{30,22},{3,11},{31,23}} | collective-permute-start | bytes 2359304 | tf_op jit(solution)/shard_map/ppermute | solution.py:301
  56.2 19.9 %collective-permute-start.9 = (bf16[2,64,3072]{2,1,0:T(8,128)(2,1)}, bf16[2,64,3072]{2,1,0:T(8,128)(2,1)}, u32[]{:S(2)}, u32[]{:S(2)}) collective-permute-start(bf16[2,64,3072]{2,1,0:T(8,128)(2,1)} %message.13), channel_id=1, source_target_pairs={{0,8},{28,20},{1,9},{29,21},{2,10},{30,22},{3,11},{31,23}} | collective-permute-start | bytes 2359304 | tf_op jit(solution)/shard_map/ppermute | solution.py:301
  64.8 14.4 %collective-permute-start.11 = (bf16[2,64,1536]{2,1,0:T(8,128)(2,1)}, bf16[2,64,1536]{2,1,0:T(8,128)(2,1)}, u32[]{:S(2)}, u32[]{:S(2)}) collective-permute-start(bf16[2,64,1536]{2,1,0:T(8,128)(2,1)} %get-tuple-element.139), channel_id=1, source_target_pairs={{0,1},{1,0},{2,3},{3,2},{4,5},{5,4},{6,7},{7,6},{8,9},{9,8},{10,11... | collective-permute-start | bytes 1179656 | tf_op jit(solution)/shard_map/ppermute | solution.py:304
  66.3 12.9 %collective-permute-start.12 = (bf16[2,64,1536]{2,1,0:T(8,128)(2,1)}, bf16[2,64,1536]{2,1,0:T(8,128)(2,1)}, u32[]{:S(2)}, u32[]{:S(2)}) collective-permute-start(bf16[2,64,1536]{2,1,0:T(8,128)(2,1)} %get-tuple-element.139), channel_id=1, source_target_pairs={{0,2},{1,3},{2,0},{3,1},{4,6},{5,7},{6,4},{7,5},{8,10},{9,11},{10,... | collective-permute-start | bytes 1179656 | tf_op jit(solution)/shard_map/ppermute | solution.py:304
  70.8 15.2 %collective-permute-start.7 = (bf16[2,64,3072]{2,1,0:T(8,128)(2,1)}, bf16[2,64,3072]{2,1,0:T(8,128)(2,1)}, u32[]{:S(2)}, u32[]{:S(2)}) collective-permute-start(bf16[2,64,3072]{2,1,0:T(8,128)(2,1)} %message.14), channel_id=1, source_target_pairs={{0,8},{8,16},{28,20},{20,12},{1,9},{9,17},{29,21},{21,13},{2,10},{... | collective-permute-start | bytes 2359304 | tf_op jit(solution)/shard_map/ppermute | solution.py:301
  84.6 20.7 %collective-permute-start.10 = (bf16[2,64,3072]{2,1,0:T(8,128)(2,1)}, bf16[2,64,3072]{2,1,0:T(8,128)(2,1)S(1)}, u32[]{:S(2)}, u32[]{:S(2)}) collective-permute-start(bf16[2,64,3072]{2,1,0:T(8,128)(2,1)} %copy-done.49), channel_id=1, source_target_pairs={{0,8},{8,16},{28,20},{20,12},{1,9},{9,17},{29,21},{21,13},{2,10},{... | collective-permute-start | bytes 2359304 | tf_op jit(solution)/shard_map/ppermute | solution.py:301
  85.9 37.6 %collective-permute-start.18 = (bf16[128,6144]{1,0:T(8,128)(2,1)}, bf16[128,6144]{1,0:T(8,128)(2,1)S(1)}, u32[]{:S(2)}, u32[]{:S(2)}) collective-permute-start(bf16[128,6144]{1,0:T(8,128)(2,1)} %mine_ref.7), channel_id=1, source_target_pairs={{0,4},{4,0},{8,12},{12,8},{16,20},{20,16},{24,28},{28,24},{1,5},{5... | collective-permute-start | bytes 4718600 | tf_op jit(solution)/shard_map/ppermute | solution.py:296
  89.1 32.2 %collective-permute-start.8 = (bf16[2,64,3072]{2,1,0:T(8,128)(2,1)}, bf16[2,64,3072]{2,1,0:T(8,128)(2,1)}, u32[]{:S(2)}, u32[]{:S(2)}) collective-permute-start(bf16[2,64,3072]{2,1,0:T(8,128)(2,1)} %message.15), channel_id=1, source_target_pairs={{0,8},{8,16},{16,24},{28,20},{20,12},{12,4},{1,9},{9,17},{17,25},{... | collective-permute-start | bytes 2359304 | tf_op jit(solution)/shard_map/ppermute | solution.py:301
  105.2 38.5 %collective-permute-start.24 = (bf16[4,2,64,3072]{3,2,1,0:T(8,128)(2,1)S(1)}, bf16[4,2,64,3072]{3,2,1,0:T(8,128)(2,1)S(1)}, u32[]{:S(2)}, u32[]{:S(2)}) collective-permute-start(bf16[4,2,64,3072]{3,2,1,0:T(8,128)(2,1)S(1)} %bitcast.85), channel_id=1, source_target_pairs={{0,4},{4,0},{8,12},{12,8},{16,20},{20,16},{24,28},{28,24},{1,5},{5... | collective-permute-start | bytes 9437192 | tf_op jit(solution)/shard_map/ppermute | solution.py:296
  121.4 31.7 %collective-permute-start.15 = (bf16[4,2,64,3072]{3,2,1,0:T(8,128)(2,1)S(1)}, bf16[4,2,64,3072]{3,2,1,0:T(8,128)(2,1)S(1)}, u32[]{:S(2)}, u32[]{:S(2)}) collective-permute-start(bf16[4,2,64,3072]{3,2,1,0:T(8,128)(2,1)S(1)} %bitcast.80), channel_id=1, source_target_pairs={{0,4},{4,0},{8,12},{12,8},{16,20},{20,16},{24,28},{28,24},{1,5},{5... | collective-permute-start | bytes 9437192 | tf_op jit(solution)/shard_map/ppermute | solution.py:296
  130.8 12.3 %collective-permute-start.21 = (bf16[2,64,3072]{2,1,0:T(8,128)(2,1)S(1)}, bf16[2,64,3072]{2,1,0:T(8,128)(2,1)S(1)}, u32[]{:S(2)}, u32[]{:S(2)}) collective-permute-start(bf16[2,64,3072]{2,1,0:T(8,128)(2,1)S(1)} %get-tuple-element.86.refs_0_), channel_id=1, source_target_pairs={{0,8},{8,16},{16,24},{28,20},{20,12},{12,4},{1,9},{9,17},{17,25},{... | collective-permute-start | bytes 2359304 | tf_op jit(solution)/shard_map/ppermute | solution.py:301
  138.7 12.9 %collective-permute-start.20 = (bf16[2,64,3072]{2,1,0:T(8,128)(2,1)S(1)}, bf16[2,64,3072]{2,1,0:T(8,128)(2,1)S(1)}, u32[]{:S(2)}, u32[]{:S(2)}) collective-permute-start(bf16[2,64,3072]{2,1,0:T(8,128)(2,1)S(1)} %get-tuple-element.85.refs_0_), channel_id=1, source_target_pairs={{0,8},{8,16},{16,24},{28,20},{20,12},{12,4},{1,9},{9,17},{17,25},{... | collective-permute-start | bytes 2359304 | tf_op jit(solution)/shard_map/ppermute | solution.py:301
  144.8 15.2 %collective-permute-start.25 = (bf16[2,64,3072]{2,1,0:T(8,128)(2,1)S(1)}, bf16[2,64,3072]{2,1,0:T(8,128)(2,1)}, u32[]{:S(2)}, u32[]{:S(2)}) collective-permute-start(bf16[2,64,3072]{2,1,0:T(8,128)(2,1)S(1)} %message.19), channel_id=1, source_target_pairs={{0,8},{8,16},{16,24},{28,20},{20,12},{12,4},{1,9},{9,17},{17,25},{... | collective-permute-start | bytes 2359304 | tf_op jit(solution)/shard_map/ppermute | solution.py:301
  155.0 17.0 %collective-permute-start.23 = (bf16[2,64,3072]{2,1,0:T(8,128)(2,1)}, bf16[2,64,3072]{2,1,0:T(8,128)(2,1)}, u32[]{:S(2)}, u32[]{:S(2)}) collective-permute-start(bf16[2,64,3072]{2,1,0:T(8,128)(2,1)} %message.18), channel_id=1, source_target_pairs={{0,8},{8,16},{16,24},{28,20},{20,12},{12,4},{1,9},{9,17},{17,25},{... | collective-permute-start | bytes 2359304 | tf_op jit(solution)/shard_map/ppermute | solution.py:301
  167.2 13.7 %collective-permute-start.29 = (bf16[2,64,3072]{2,1,0:T(8,128)(2,1)}, bf16[2,64,3072]{2,1,0:T(8,128)(2,1)}, u32[]{:S(2)}, u32[]{:S(2)}) collective-permute-start(bf16[2,64,3072]{2,1,0:T(8,128)(2,1)} %copy-done.55), channel_id=1, source_target_pairs={{0,8},{8,16},{16,24},{28,20},{20,12},{12,4},{1,9},{9,17},{17,25},{... | collective-permute-start | bytes 2359304 | tf_op jit(solution)/shard_map/ppermute | solution.py:301
  181.0 14.8 %collective-permute-start.28 = (bf16[2,64,3072]{2,1,0:T(8,128)(2,1)}, bf16[2,64,3072]{2,1,0:T(8,128)(2,1)S(1)}, u32[]{:S(2)}, u32[]{:S(2)}) collective-permute-start(bf16[2,64,3072]{2,1,0:T(8,128)(2,1)} %copy-done.52), channel_id=1, source_target_pairs={{0,8},{8,16},{16,24},{28,20},{20,12},{12,4},{1,9},{9,17},{17,25},{... | collective-permute-start | bytes 2359304 | tf_op jit(solution)/shard_map/ppermute | solution.py:301
  195.9 28.3 %collective-permute-start.34 = (bf16[2,64,3072]{2,1,0:T(8,128)(2,1)}, bf16[2,64,3072]{2,1,0:T(8,128)(2,1)}, u32[]{:S(2)}, u32[]{:S(2)}) collective-permute-start(bf16[2,64,3072]{2,1,0:T(8,128)(2,1)} %message.22), channel_id=1, source_target_pairs={{0,8},{8,16},{16,24},{28,20},{20,12},{12,4},{1,9},{9,17},{17,25},{... | collective-permute-start | bytes 2359304 | tf_op jit(solution)/shard_map/ppermute | solution.py:301
  202.3 21.9 %collective-permute-start.32 = (bf16[2,64,3072]{2,1,0:T(8,128)(2,1)}, bf16[2,64,3072]{2,1,0:T(8,128)(2,1)}, u32[]{:S(2)}, u32[]{:S(2)}) collective-permute-start(bf16[2,64,3072]{2,1,0:T(8,128)(2,1)} %message.23), channel_id=1, source_target_pairs={{0,8},{8,16},{16,24},{28,20},{20,12},{12,4},{1,9},{9,17},{17,25},{... | collective-permute-start | bytes 2359304 | tf_op jit(solution)/shard_map/ppermute | solution.py:301
  240.4 13.1 %collective-permute-start.37 = (bf16[2,64,3072]{2,1,0:T(8,128)(2,1)S(1)}, bf16[2,64,3072]{2,1,0:T(8,128)(2,1)S(1)}, u32[]{:S(2)}, u32[]{:S(2)}) collective-permute-start(bf16[2,64,3072]{2,1,0:T(8,128)(2,1)S(1)} %get-tuple-element.112.refs_0_), channel_id=1, source_target_pairs={{0,8},{8,16},{16,24},{28,20},{20,12},{12,4},{1,9},{9,17},{17,25},{... | collective-permute-start | bytes 2359304 | tf_op jit(solution)/shard_map/ppermute | solution.py:301
  280.8 18.0 %collective-permute-start.44 = (bf16[2,64,3072]{2,1,0:T(8,128)(2,1)S(1)}, bf16[2,64,3072]{2,1,0:T(8,128)(2,1)}, u32[]{:S(2)}, u32[]{:S(2)}) collective-permute-start(bf16[2,64,3072]{2,1,0:T(8,128)(2,1)S(1)} %collective-permute-done.40.refs_2_), channel_id=1, source_target_pairs={{16,24},{12,4},{17,25},{13,5},{18,26},{14,6},{19,27},{15,7}} | collective-permute-start | bytes 2359304 | tf_op jit(solution)/shard_map/ppermute | solution.py:301
  319.2 28.5 %collective-permute-start.49 = (bf16[2,64,1536]{2,1,0:T(8,128)(2,1)S(1)}, bf16[2,64,1536]{2,1,0:T(8,128)(2,1)S(1)}, u32[]{:S(2)}, u32[]{:S(2)}) collective-permute-start(bf16[2,64,1536]{2,1,0:T(8,128)(2,1)S(1)} %get-tuple-element.127), channel_id=1, source_target_pairs={{0,1},{1,0},{2,3},{3,2},{4,5},{5,4},{6,7},{7,6},{8,9},{9,8},{10,11... | collective-permute-start | bytes 1179656 | tf_op jit(solution)/shard_map/ppermute | solution.py:304
  320.1 27.6 %collective-permute-start.51 = (bf16[2,64,1536]{2,1,0:T(8,128)(2,1)S(1)}, bf16[2,64,1536]{2,1,0:T(8,128)(2,1)S(1)}, u32[]{:S(2)}, u32[]{:S(2)}) collective-permute-start(bf16[2,64,1536]{2,1,0:T(8,128)(2,1)S(1)} %get-tuple-element.128), channel_id=1, source_target_pairs={{0,3},{1,2},{2,1},{3,0},{4,7},{5,6},{6,5},{7,4},{8,11},{9,10},{10,... | collective-permute-start | bytes 1179656 | tf_op jit(solution)/shard_map/ppermute | solution.py:304
  322.2 25.5 %collective-permute-start.50 = (bf16[2,64,1536]{2,1,0:T(8,128)(2,1)S(1)}, bf16[2,64,1536]{2,1,0:T(8,128)(2,1)S(1)}, u32[]{:S(2)}, u32[]{:S(2)}) collective-permute-start(bf16[2,64,1536]{2,1,0:T(8,128)(2,1)S(1)} %get-tuple-element.129), channel_id=1, source_target_pairs={{0,2},{1,3},{2,0},{3,1},{4,6},{5,7},{6,4},{7,5},{8,10},{9,11},{10,... | collective-permute-start | bytes 1179656 | tf_op jit(solution)/shard_map/ppermute | solution.py:304
  (86 other events, 665.5 us)
Sparse Core Ops, SparseCore 0:
  301.1 44.3 reduce-scatter.3

commit v6 on v5

--- a/solution.py
+++ b/solution.py
@@ -237,7 +237,7 @@
     )(core, part, theirs, came, came_there, cotangent, cotangent_there, *kept)
 
 
-def collect_kernel(place, slope, mine, theirs, depth):
+def collect_kernel(place, slope, mine, theirs, depth, vmem):
     def body(place_ref, *refs):
         slope_ref, out, sems = refs[0], refs[-2], refs[-1]
         mine_refs, their_refs = refs[1:depth], refs[depth : 2 * depth - 1]
@@ -268,7 +268,7 @@
         None,
         0,
         0,
-        vmem=47,
+        vmem=vmem,
         grid_spec=pltpu.PrefetchScalarGridSpec(
             num_scalar_prefetch=1,
             grid=(1,),
@@ -430,6 +430,7 @@
             [env["got", q, j] for j in order],
             [env["got_there", q, j] for j in order],
             depth,
+            10 if half == 0 else 47,
         )
         env["g", half, chunk] = g.reshape(n_row * few, f)
 
@@ -490,7 +491,7 @@
                 i_next, t_next = steps[step + 1]
                 if t_next == depth - 2 and i_next + 1 < count:
                     work.append((forward, (q, i_next + 1), ("x", items[q][i_next + 1][0])))
-                if t_next == 1 and i_next == 1 and q < HALVES:
+                if t_next == 1 and i_next == count and q < HALVES:
                     work.append((transpose, (q,), ("x", q)))
                 if t_next == depth - 2 and i_next > 0:
                     work.append((backward_half, (q, i_next - 1), ("got", q, depth - 1)))

time: 359 us -> 352 us (0.981)
  waiting for transfers between devices: 35.1 us -> 50 us
  local copies, waits for them, and re-layouts: 40.6 us -> 29.6 us
  Pallas kernels: 154 us -> 146 us
    ppermute x20, waiting for transfers between devices: 15.4 us -> 33.1 us  [onward(): return lax.ppermute(value, 'row', up + down)]
    unnamed x114 -> x78, local copies, waits for them, and re-layouts: 29.8 us -> 21.8 us
    pallas_call x4, Pallas kernels: 13.6 us -> 9.23 us  [collect_kernel(): matmul_call(body, 'collect', None, 0, 0, vmem=vmem, grid_spec=pltpu.Prefe...]
  transfers between devices with their start and end apart: 53 -> 53, of which waited for: 17 -> 17; matrix products, arithmetic and copies ran while one was open for 4% -> 3% of each run, Pallas kernels for 40% -> 39%
where the time goes in v6:
time: 352 us; the launch traced here: 350 us
  Pallas kernels  146 us (41%)
  starting transfers between devices  102 us (29%)
  waiting for transfers between devices  50 us (14%)
  local copies, waits for them, and re-layouts  29.6 us (8%)
  between operations  14.7 us (4%)
  other arithmetic  7.16 us (2%)
    ppermute x20, starting transfers between devices, onward(): return lax.ppermute(value, 'row', up + down)  58.9 us
    pallas_call x4, Pallas kernels, forward_matmul(): matmul_call(body, 'forward', (steps,), 2 * rows * width * f, 2 * (rows *...  36.1 us
    ppermute x20, waiting for transfers between devices, onward(): return lax.ppermute(value, 'row', up + down)  33.1 us
    ppermute x21, starting transfers between devices, swap(): return lax.ppermute(value, 'row', [(r, r ^ 1) for r in range(n_row)])  27.4 us
    pallas_call x2, Pallas kernels, weight_grad_matmul(): matmul_call(body, 'weight_grad', (steps,), 2 * n * rows * width * f, 2 *...  24.9 us
    pallas_call x12, Pallas kernels, message_kernel(): matmul_call(body, 'message', None, 0, 0, vmem=8, grid_spec=pltpu.Prefetch...  23.8 us
    unnamed x78, local copies, waits for them, and re-layouts  21.8 us
    pallas_call x4, Pallas kernels, gelu_kernel(): matmul_call(body, 'gelu', None, 0, 0, vmem=8, grid_spec=pltpu.PrefetchSca...  20 us
  transfers between devices with their start and end apart: 53, of which 17 were waited for; matrix products, arithmetic and copies ran while one was open for 3% of the time, Pallas kernels for 39%

profile of v6, /device:TPU:0, one launch (start us, length us, event | category | flops | bytes accessed | tf_op | source)
XLA Modules:
  0.0 349.6 jit_solution(13935476995727987050)
XLA Ops:
  12.8 7.6 %collective-permute-done = bf16[2,64,1536]{2,1,0:T(8,128)(2,1)S(1)} collective-permute-done((bf16[2,64,1536]{2,1,0:T(8,128)(2,1)S(1)}, bf16[2,64,1536]{2,1,0:T(8,128)(2,1)S(1)}, u32[]{:S(2)}, u32[]{:S(2)}) %collective-permute-start) | collective-permute-done | bytes 393248 | tf_op jit(solution)/shard_map/ppermute | solution.py:304
  28.6 10.1 %forward.4 = bf16[512,3072]{1,0:T(8,128)(2,1)} custom-call(bf16[512,1536]{1,0:T(8,128)(2,1)S(1)} %bitcast.92, bf16[1536,6144]{1,0:T(8,128)(2,1)} %w_ref.11), custom_call_target="tpu_custom_call" | custom-call | flops 4831838208 | bytes 14155776 | tf_op jit(solution)/shard_map/forward/pallas_call | solution.py:52
  38.8 8.5 %forward.5 = bf16[512,3072]{1,0:T(8,128)(2,1)S(1)} custom-call(bf16[512,1536]{1,0:T(8,128)(2,1)S(1)} %bitcast.93, bf16[1536,6144]{1,0:T(8,128)(2,1)} %w_ref.11), custom_call_target="tpu_custom_call" | custom-call | flops 4831838208 | bytes 14155776 | tf_op jit(solution)/shard_map/forward/pallas_call | solution.py:52
  56.2 4.0 %collective-permute-start.9 = (bf16[2,64,3072]{2,1,0:T(8,128)(2,1)}, bf16[2,64,3072]{2,1,0:T(8,128)(2,1)}, u32[]{:S(2)}, u32[]{:S(2)}) collective-permute-start(bf16[2,64,3072]{2,1,0:T(8,128)(2,1)} %message.13), channel_id=1, source_target_pairs={{0,8},{28,20},{1,9},{29,21},{2,10},{30,22},{3,11},{31,23}} | collective-permute-start | bytes 2359304 | tf_op jit(solution)/shard_map/ppermute | solution.py:301
  70.8 5.3 %collective-permute-start.7 = (bf16[2,64,3072]{2,1,0:T(8,128)(2,1)}, bf16[2,64,3072]{2,1,0:T(8,128)(2,1)}, u32[]{:S(2)}, u32[]{:S(2)}) collective-permute-start(bf16[2,64,3072]{2,1,0:T(8,128)(2,1)} %message.14), channel_id=1, source_target_pairs={{0,8},{8,16},{28,20},{20,12},{1,9},{9,17},{29,21},{21,13},{2,10},{... | collective-permute-start | bytes 2359304 | tf_op jit(solution)/shard_map/ppermute | solution.py:301
  89.0 4.4 %collective-permute-start.8 = (bf16[2,64,3072]{2,1,0:T(8,128)(2,1)}, bf16[2,64,3072]{2,1,0:T(8,128)(2,1)}, u32[]{:S(2)}, u32[]{:S(2)}) collective-permute-start(bf16[2,64,3072]{2,1,0:T(8,128)(2,1)} %message.15), channel_id=1, source_target_pairs={{0,8},{8,16},{16,24},{28,20},{20,12},{12,4},{1,9},{9,17},{17,25},{... | collective-permute-start | bytes 2359304 | tf_op jit(solution)/shard_map/ppermute | solution.py:301
  96.1 9.0 %forward.6 = bf16[512,3072]{1,0:T(8,128)(2,1)S(1)} custom-call(bf16[512,1536]{1,0:T(8,128)(2,1)S(1)} %bitcast.95, bf16[1536,6144]{1,0:T(8,128)(2,1)} %w_ref.11), custom_call_target="tpu_custom_call" | custom-call | flops 4831838208 | bytes 14155776 | tf_op jit(solution)/shard_map/forward/pallas_call | solution.py:52
  110.4 8.5 %forward.7 = bf16[512,3072]{1,0:T(8,128)(2,1)S(1)} custom-call(bf16[512,1536]{1,0:T(8,128)(2,1)S(1)} %bitcast.96, bf16[1536,6144]{1,0:T(8,128)(2,1)} %w_ref.11), custom_call_target="tpu_custom_call" | custom-call | flops 4831838208 | bytes 14155776 | tf_op jit(solution)/shard_map/forward/pallas_call | solution.py:52
  125.4 5.2 %gelu.4 = (bf16[2,64,3072]{2,1,0:T(8,128)(2,1)S(1)}, bf16[128,6144]{1,0:T(8,128)(2,1)}) custom-call(s32[1]{0:T(128)} %bitcast.core_ref, bf16[4,2,64,3072]{3,2,1,0:T(8,128)(2,1)} %bitcast.17.part_ref, bf16[4,2,64,3072]{3,2,1,0:T(8,128)(2,1)} %collective-permute-done.4.theirs_ref, bf16[2,64,3072]{2,1,0:T(8,128)(2,1)} %collective-permute-done.8.came_ref, ...), custom_call_target="tpu_custom_call" | custom-call | tf_op jit(solution)/shard_map/gelu/pallas_call | solution.py:218
  133.1 5.0 %gelu.5 = (bf16[2,64,3072]{2,1,0:T(8,128)(2,1)S(1)}, bf16[128,6144]{1,0:T(8,128)(2,1)}) custom-call(s32[1]{0:T(128)} %bitcast.core_ref, bf16[4,2,64,3072]{3,2,1,0:T(8,128)(2,1)S(1)} %bitcast.79, bf16[4,2,64,3072]{3,2,1,0:T(8,128)(2,1)} %collective-permute-done.6.theirs_ref, ...), custom_call_target="tpu_custom_call", output_to_operand_aliasing={{1}: (7, {})} | custom-call | tf_op jit(solution)/shard_map/gelu/pallas_call | solution.py:218
  168.6 7.6 %collective-permute-done.29.rest_0_.refs_3_ = bf16[2,64,3072]{2,1,0:T(8,128)(2,1)S(1)} collective-permute-done((bf16[2,64,3072]{2,1,0:T(8,128)(2,1)S(1)}, bf16[2,64,3072]{2,1,0:T(8,128)(2,1)S(1)}, u32[]{:S(2)}, u32[]{:S(2)}) %collective-permute-start.29) | collective-permute-done | bytes 786464 | tf_op jit(solution)/shard_map/ppermute | solution.py:301
  184.7 6.6 %collective-permute-done.28.rest_0_.refs_3_ = bf16[2,64,3072]{2,1,0:T(8,128)(2,1)S(1)} collective-permute-done((bf16[2,64,3072]{2,1,0:T(8,128)(2,1)S(1)}, bf16[2,64,3072]{2,1,0:T(8,128)(2,1)S(1)}, u32[]{:S(2)}, u32[]{:S(2)}) %collective-permute-start.28) | collective-permute-done | bytes 786464 | tf_op jit(solution)/shard_map/ppermute | solution.py:301
  191.4 5.2 %collective-permute-start.34 = (bf16[2,64,3072]{2,1,0:T(8,128)(2,1)}, bf16[2,64,3072]{2,1,0:T(8,128)(2,1)}, u32[]{:S(2)}, u32[]{:S(2)}) collective-permute-start(bf16[2,64,3072]{2,1,0:T(8,128)(2,1)} %message.22), channel_id=1, source_target_pairs={{0,8},{8,16},{16,24},{28,20},{20,12},{12,4},{1,9},{9,17},{17,25},{... | collective-permute-start | bytes 2359304 | tf_op jit(solution)/shard_map/ppermute | solution.py:301
  203.4 14.1 %input_grad_whole.1 = bf16[512,1536]{1,0:T(8,128)(2,1)S(1)} custom-call(bf16[512,3072]{1,0:T(8,128)(2,1)S(1)} %bitcast.108, bf16[512,3072]{1,0:T(8,128)(2,1)} %bitcast.98, bf16[1536,6144]{1,0:T(8,128)(2,1)} %w_ref.11), custom_call_target="tpu_custom_call" | custom-call | flops 9663676416 | bytes 26738688 | tf_op jit(solution)/shard_map/input_grad_whole/pallas_call | solution.py:116
  220.1 4.9 %gelu.6 = (bf16[2,64,3072]{2,1,0:T(8,128)(2,1)S(1)}, bf16[128,6144]{1,0:T(8,128)(2,1)}) custom-call(s32[1]{0:T(128)} %bitcast.core_ref, bf16[4,2,64,3072]{3,2,1,0:T(8,128)(2,1)S(1)} %bitcast.89, bf16[4,2,64,3072]{3,2,1,0:T(8,128)(2,1)S(1)} %collective-permute-done.24.theirs_ref, ...), custom_call_target="tpu_custom_call", output_to_operand_aliasing={{1}: (7, {})} | custom-call | tf_op jit(solution)/shard_map/gelu/pallas_call | solution.py:218
  227.2 4.9 %gelu.7 = (bf16[2,64,3072]{2,1,0:T(8,128)(2,1)S(1)}, bf16[128,6144]{1,0:T(8,128)(2,1)}) custom-call(s32[1]{0:T(128)} %bitcast.core_ref, bf16[4,2,64,3072]{3,2,1,0:T(8,128)(2,1)S(1)} %bitcast.84, bf16[4,2,64,3072]{3,2,1,0:T(8,128)(2,1)S(1)} %copy-done.1, bf16[2,64,3072]{2,1,0:T(8,128)(2,1)} %collective-permute-done.32.came_ref, ...), custom_call_target="tpu_custom_call", output_to_operand_aliasing={{1}: (7, {})} | custom-call | tf_op jit(solution)/shard_map/gelu/pallas_call | solution.py:218
  240.3 4.7 %collective-permute-done.37.refs_1_ = bf16[2,64,3072]{2,1,0:T(8,128)(2,1)} collective-permute-done((bf16[2,64,3072]{2,1,0:T(8,128)(2,1)S(1)}, bf16[2,64,3072]{2,1,0:T(8,128)(2,1)}, u32[]{:S(2)}, u32[]{:S(2)}) %collective-permute-start.37) | collective-permute-done | bytes 786464 | tf_op jit(solution)/shard_map/ppermute | solution.py:301
  250.3 5.4 %collective-permute-start.43 = (bf16[2,64,3072]{2,1,0:T(8,128)(2,1)}, bf16[2,64,3072]{2,1,0:T(8,128)(2,1)}, u32[]{:S(2)}, u32[]{:S(2)}) collective-permute-start(bf16[2,64,3072]{2,1,0:T(8,128)(2,1)} %collective-permute-done.41.refs_2_), channel_id=1, source_target_pairs={{0,4},{4,0},{8,12},{12,8},{16,20},{20,16},{24,28},{28,24},{1,5},{5... | collective-permute-start | bytes 2359304 | tf_op jit(solution)/shard_map/ppermute | solution.py:296
  258.9 4.4 %collective-permute-start.46 = (bf16[2,64,3072]{2,1,0:T(8,128)(2,1)}, bf16[2,64,3072]{2,1,0:T(8,128)(2,1)}, u32[]{:S(2)}, u32[]{:S(2)}) collective-permute-start(bf16[2,64,3072]{2,1,0:T(8,128)(2,1)} %collective-permute-done.40.refs_2_), channel_id=1, source_target_pairs={{0,4},{4,0},{8,12},{12,8},{16,20},{20,16},{24,28},{28,24},{1,5},{5... | collective-permute-start | bytes 2359304 | tf_op jit(solution)/shard_map/ppermute | solution.py:296
  265.5 6.2 %collective-permute-start.47 = (bf16[2,64,3072]{2,1,0:T(8,128)(2,1)}, bf16[2,64,3072]{2,1,0:T(8,128)(2,1)S(1)}, u32[]{:S(2)}, u32[]{:S(2)}) collective-permute-start(bf16[2,64,3072]{2,1,0:T(8,128)(2,1)} %collective-permute-done.45.refs_3_), channel_id=1, source_target_pairs={{0,4},{4,0},{8,12},{12,8},{16,20},{20,16},{24,28},{28,24},{1,5},{5... | collective-permute-start | bytes 2359304 | tf_op jit(solution)/shard_map/ppermute | solution.py:296
  282.7 8.7 %input_grad.2.rest_0_ = f32[512,1536]{1,0:T(8,128)S(1)} custom-call(bf16[512,3072]{1,0:T(8,128)(2,1)S(1)} %bitcast.100, bf16[1536,6144]{1,0:T(8,128)(2,1)} %w_ref.11), custom_call_target="tpu_custom_call" | custom-call | flops 4831838208 | bytes 18874368 | tf_op jit(solution)/shard_map/input_grad/pallas_call | solution.py:82
  302.5 9.5 %input_grad.3 = bf16[512,1536]{1,0:T(8,128)(2,1)S(1)} custom-call(bf16[512,3072]{1,0:T(8,128)(2,1)S(1)} %bitcast.90, bf16[1536,6144]{1,0:T(8,128)(2,1)} %w_ref.11, f32[512,1536]{1,0:T(8,128)} %copy-done.14), custom_call_target="tpu_custom_call" | custom-call | flops 4831838208 | bytes 18874368 | tf_op jit(solution)/shard_map/input_grad/pallas_call | solution.py:82
  315.7 12.4 %weight_grad.2.refs_4_ = bf16[1536,6144]{1,0:T(8,128)(2,1)} custom-call(bf16[1536,512]{1,0:T(8,128)(2,1)S(1)} %bitcast.102, bf16[1536,512]{1,0:T(8,128)(2,1)S(1)} %bitcast.104, bf16[512,3072]{1,0:T(8,128)(2,1)S(1)} %bitcast.109, bf16[512,3072]{1,0:T(8,128)(2,1)S(1)} %bitcast.101), custom_call_target="tpu_custom_call" | custom-call | flops 9663676416 | bytes 18874368 | tf_op jit(solution)/shard_map/weight_grad/pallas_call | solution.py:144
  328.2 12.4 %weight_grad.3 = bf16[1536,6144]{1,0:T(8,128)(2,1)} custom-call(bf16[1536,512]{1,0:T(8,128)(2,1)S(1)} %bitcast.103, bf16[1536,512]{1,0:T(8,128)(2,1)S(1)} %bitcast.105, bf16[512,3072]{1,0:T(8,128)(2,1)S(1)} %bitcast.99, bf16[512,3072]{1,0:T(8,128)(2,1)S(1)} %bitcast.91, bf16[1536,6144]{1,0:T(8,128)(2,1)} %weight_grad.2.refs_4_), custom_call_target="tpu_custom_call", output_to_operand_aliasing={{}: (4, {})} | custom-call | flops 9663676416 | bytes 18874368 | tf_op jit(solution)/shard_map/weight_grad/pallas_call | solution.py:144
  (214 shorter events, 160.5 us)
Async XLA Ops:
  7.2 333.7 %reduce-scatter.4.cloned.1.call-start = ((), (), s32[]{:S(2)}) async-start(), calls=%async_computation.1 | async-start | bytes 1966080
  50.0 13.1 %collective-permute-start.5 = (bf16[2,64,3072]{2,1,0:T(8,128)(2,1)S(1)}, bf16[2,64,3072]{2,1,0:T(8,128)(2,1)S(1)}, u32[]{:S(2)}, u32[]{:S(2)}) collective-permute-start(bf16[2,64,3072]{2,1,0:T(8,128)(2,1)S(1)} %message.12), channel_id=1, source_target_pairs={{0,8},{28,20},{1,9},{29,21},{2,10},{30,22},{3,11},{31,23}} | collective-permute-start | bytes 2359304 | tf_op jit(solution)/shard_map/ppermute | solution.py:301
  56.2 19.9 %collective-permute-start.9 = (bf16[2,64,3072]{2,1,0:T(8,128)(2,1)}, bf16[2,64,3072]{2,1,0:T(8,128)(2,1)}, u32[]{:S(2)}, u32[]{:S(2)}) collective-permute-start(bf16[2,64,3072]{2,1,0:T(8,128)(2,1)} %message.13), channel_id=1, source_target_pairs={{0,8},{28,20},{1,9},{29,21},{2,10},{30,22},{3,11},{31,23}} | collective-permute-start | bytes 2359304 | tf_op jit(solution)/shard_map/ppermute | solution.py:301
  64.8 14.4 %collective-permute-start.11 = (bf16[2,64,1536]{2,1,0:T(8,128)(2,1)}, bf16[2,64,1536]{2,1,0:T(8,128)(2,1)}, u32[]{:S(2)}, u32[]{:S(2)}) collective-permute-start(bf16[2,64,1536]{2,1,0:T(8,128)(2,1)} %get-tuple-element.139), channel_id=1, source_target_pairs={{0,1},{1,0},{2,3},{3,2},{4,5},{5,4},{6,7},{7,6},{8,9},{9,8},{10,11... | collective-permute-start | bytes 1179656 | tf_op jit(solution)/shard_map/ppermute | solution.py:304
  66.3 12.9 %collective-permute-start.12 = (bf16[2,64,1536]{2,1,0:T(8,128)(2,1)}, bf16[2,64,1536]{2,1,0:T(8,128)(2,1)}, u32[]{:S(2)}, u32[]{:S(2)}) collective-permute-start(bf16[2,64,1536]{2,1,0:T(8,128)(2,1)} %get-tuple-element.139), channel_id=1, source_target_pairs={{0,2},{1,3},{2,0},{3,1},{4,6},{5,7},{6,4},{7,5},{8,10},{9,11},{10,... | collective-permute-start | bytes 1179656 | tf_op jit(solution)/shard_map/ppermute | solution.py:304
  70.8 15.1 %collective-permute-start.7 = (bf16[2,64,3072]{2,1,0:T(8,128)(2,1)}, bf16[2,64,3072]{2,1,0:T(8,128)(2,1)}, u32[]{:S(2)}, u32[]{:S(2)}) collective-permute-start(bf16[2,64,3072]{2,1,0:T(8,128)(2,1)} %message.14), channel_id=1, source_target_pairs={{0,8},{8,16},{28,20},{20,12},{1,9},{9,17},{29,21},{21,13},{2,10},{... | collective-permute-start | bytes 2359304 | tf_op jit(solution)/shard_map/ppermute | solution.py:301
  84.5 20.7 %collective-permute-start.10 = (bf16[2,64,3072]{2,1,0:T(8,128)(2,1)}, bf16[2,64,3072]{2,1,0:T(8,128)(2,1)S(1)}, u32[]{:S(2)}, u32[]{:S(2)}) collective-permute-start(bf16[2,64,3072]{2,1,0:T(8,128)(2,1)} %copy-done.35), channel_id=1, source_target_pairs={{0,8},{8,16},{28,20},{20,12},{1,9},{9,17},{29,21},{21,13},{2,10},{... | collective-permute-start | bytes 2359304 | tf_op jit(solution)/shard_map/ppermute | solution.py:301
  85.8 35.6 %collective-permute-start.18 = (bf16[128,6144]{1,0:T(8,128)(2,1)}, bf16[128,6144]{1,0:T(8,128)(2,1)S(1)}, u32[]{:S(2)}, u32[]{:S(2)}) collective-permute-start(bf16[128,6144]{1,0:T(8,128)(2,1)} %mine_ref.7), channel_id=1, source_target_pairs={{0,4},{4,0},{8,12},{12,8},{16,20},{20,16},{24,28},{28,24},{1,5},{5... | collective-permute-start | bytes 4718600 | tf_op jit(solution)/shard_map/ppermute | solution.py:296
  89.0 29.9 %collective-permute-start.8 = (bf16[2,64,3072]{2,1,0:T(8,128)(2,1)}, bf16[2,64,3072]{2,1,0:T(8,128)(2,1)}, u32[]{:S(2)}, u32[]{:S(2)}) collective-permute-start(bf16[2,64,3072]{2,1,0:T(8,128)(2,1)} %message.15), channel_id=1, source_target_pairs={{0,8},{8,16},{16,24},{28,20},{20,12},{12,4},{1,9},{9,17},{17,25},{... | collective-permute-start | bytes 2359304 | tf_op jit(solution)/shard_map/ppermute | solution.py:301
  105.1 38.2 %collective-permute-start.24 = (bf16[4,2,64,3072]{3,2,1,0:T(8,128)(2,1)S(1)}, bf16[4,2,64,3072]{3,2,1,0:T(8,128)(2,1)S(1)}, u32[]{:S(2)}, u32[]{:S(2)}) collective-permute-start(bf16[4,2,64,3072]{3,2,1,0:T(8,128)(2,1)S(1)} %bitcast.85), channel_id=1, source_target_pairs={{0,4},{4,0},{8,12},{12,8},{16,20},{20,16},{24,28},{28,24},{1,5},{5... | collective-permute-start | bytes 9437192 | tf_op jit(solution)/shard_map/ppermute | solution.py:296
  119.0 32.8 %collective-permute-start.15 = (bf16[4,2,64,3072]{3,2,1,0:T(8,128)(2,1)S(1)}, bf16[4,2,64,3072]{3,2,1,0:T(8,128)(2,1)S(1)}, u32[]{:S(2)}, u32[]{:S(2)}) collective-permute-start(bf16[4,2,64,3072]{3,2,1,0:T(8,128)(2,1)S(1)} %bitcast.80), channel_id=1, source_target_pairs={{0,4},{4,0},{8,12},{12,8},{16,20},{20,16},{24,28},{28,24},{1,5},{5... | collective-permute-start | bytes 9437192 | tf_op jit(solution)/shard_map/ppermute | solution.py:296
  119.5 13.6 %collective-permute-start.17 = (bf16[2,64,3072]{2,1,0:T(8,128)(2,1)}, bf16[2,64,3072]{2,1,0:T(8,128)(2,1)S(1)}, u32[]{:S(2)}, u32[]{:S(2)}) collective-permute-start(bf16[2,64,3072]{2,1,0:T(8,128)(2,1)} %collective-permute-done.16.came_ref), channel_id=1, source_target_pairs={{0,4},{4,0},{8,12},{12,8},{16,20},{20,16},{24,28},{28,24},{1,5},{5... | collective-permute-start | bytes 2359304 | tf_op jit(solution)/shard_map/ppermute | solution.py:296
  138.1 12.9 %collective-permute-start.20 = (bf16[2,64,3072]{2,1,0:T(8,128)(2,1)S(1)}, bf16[2,64,3072]{2,1,0:T(8,128)(2,1)S(1)}, u32[]{:S(2)}, u32[]{:S(2)}) collective-permute-start(bf16[2,64,3072]{2,1,0:T(8,128)(2,1)S(1)} %get-tuple-element.85.refs_0_), channel_id=1, source_target_pairs={{0,8},{8,16},{16,24},{28,20},{20,12},{12,4},{1,9},{9,17},{17,25},{... | collective-permute-start | bytes 2359304 | tf_op jit(solution)/shard_map/ppermute | solution.py:301
  144.5 14.9 %collective-permute-start.25 = (bf16[2,64,3072]{2,1,0:T(8,128)(2,1)S(1)}, bf16[2,64,3072]{2,1,0:T(8,128)(2,1)S(1)}, u32[]{:S(2)}, u32[]{:S(2)}) collective-permute-start(bf16[2,64,3072]{2,1,0:T(8,128)(2,1)S(1)} %message.19), channel_id=1, source_target_pairs={{0,8},{8,16},{16,24},{28,20},{20,12},{12,4},{1,9},{9,17},{17,25},{... | collective-permute-start | bytes 2359304 | tf_op jit(solution)/shard_map/ppermute | solution.py:301
  152.9 14.9 %collective-permute-start.23 = (bf16[2,64,3072]{2,1,0:T(8,128)(2,1)S(1)}, bf16[2,64,3072]{2,1,0:T(8,128)(2,1)S(1)}, u32[]{:S(2)}, u32[]{:S(2)}) collective-permute-start(bf16[2,64,3072]{2,1,0:T(8,128)(2,1)S(1)} %message.18), channel_id=1, source_target_pairs={{0,8},{8,16},{16,24},{28,20},{20,12},{12,4},{1,9},{9,17},{17,25},{... | collective-permute-start | bytes 2359304 | tf_op jit(solution)/shard_map/ppermute | solution.py:301
  161.4 14.8 %collective-permute-start.29 = (bf16[2,64,3072]{2,1,0:T(8,128)(2,1)S(1)}, bf16[2,64,3072]{2,1,0:T(8,128)(2,1)S(1)}, u32[]{:S(2)}, u32[]{:S(2)}) collective-permute-start(bf16[2,64,3072]{2,1,0:T(8,128)(2,1)S(1)} %message.21), channel_id=1, source_target_pairs={{0,8},{8,16},{16,24},{28,20},{20,12},{12,4},{1,9},{9,17},{17,25},{... | collective-permute-start | bytes 2359304 | tf_op jit(solution)/shard_map/ppermute | solution.py:301
  178.3 13.0 %collective-permute-start.28 = (bf16[2,64,3072]{2,1,0:T(8,128)(2,1)S(1)}, bf16[2,64,3072]{2,1,0:T(8,128)(2,1)S(1)}, u32[]{:S(2)}, u32[]{:S(2)}) collective-permute-start(bf16[2,64,3072]{2,1,0:T(8,128)(2,1)S(1)} %message.20), channel_id=1, source_target_pairs={{0,8},{8,16},{16,24},{28,20},{20,12},{12,4},{1,9},{9,17},{17,25},{... | collective-permute-start | bytes 2359304 | tf_op jit(solution)/shard_map/ppermute | solution.py:301
  191.4 26.1 %collective-permute-start.34 = (bf16[2,64,3072]{2,1,0:T(8,128)(2,1)}, bf16[2,64,3072]{2,1,0:T(8,128)(2,1)}, u32[]{:S(2)}, u32[]{:S(2)}) collective-permute-start(bf16[2,64,3072]{2,1,0:T(8,128)(2,1)} %message.22), channel_id=1, source_target_pairs={{0,8},{8,16},{16,24},{28,20},{20,12},{12,4},{1,9},{9,17},{17,25},{... | collective-permute-start | bytes 2359304 | tf_op jit(solution)/shard_map/ppermute | solution.py:301
  198.4 19.2 %collective-permute-start.32 = (bf16[2,64,3072]{2,1,0:T(8,128)(2,1)}, bf16[2,64,3072]{2,1,0:T(8,128)(2,1)}, u32[]{:S(2)}, u32[]{:S(2)}) collective-permute-start(bf16[2,64,3072]{2,1,0:T(8,128)(2,1)} %message.23), channel_id=1, source_target_pairs={{0,8},{8,16},{16,24},{28,20},{20,12},{12,4},{1,9},{9,17},{17,25},{... | collective-permute-start | bytes 2359304 | tf_op jit(solution)/shard_map/ppermute | solution.py:301
  232.1 13.0 %collective-permute-start.37 = (bf16[2,64,3072]{2,1,0:T(8,128)(2,1)S(1)}, bf16[2,64,3072]{2,1,0:T(8,128)(2,1)}, u32[]{:S(2)}, u32[]{:S(2)}) collective-permute-start(bf16[2,64,3072]{2,1,0:T(8,128)(2,1)S(1)} %get-tuple-element.107.refs_0_), channel_id=1, source_target_pairs={{0,8},{8,16},{16,24},{28,20},{20,12},{12,4},{1,9},{9,17},{17,25},{... | collective-permute-start | bytes 2359304 | tf_op jit(solution)/shard_map/ppermute | solution.py:301
  271.7 21.5 %collective-permute-start.44 = (bf16[2,64,3072]{2,1,0:T(8,128)(2,1)}, bf16[2,64,3072]{2,1,0:T(8,128)(2,1)}, u32[]{:S(2)}, u32[]{:S(2)}) collective-permute-start(bf16[2,64,3072]{2,1,0:T(8,128)(2,1)} %collective-permute-done.40.refs_2_), channel_id=1, source_target_pairs={{16,24},{12,4},{17,25},{13,5},{18,26},{14,6},{19,27},{15,7}} | collective-permute-start | bytes 2359304 | tf_op jit(solution)/shard_map/ppermute | solution.py:301
  312.1 28.5 %collective-permute-start.49 = (bf16[2,64,1536]{2,1,0:T(8,128)(2,1)S(1)}, bf16[2,64,1536]{2,1,0:T(8,128)(2,1)S(1)}, u32[]{:S(2)}, u32[]{:S(2)}) collective-permute-start(bf16[2,64,1536]{2,1,0:T(8,128)(2,1)S(1)} %get-tuple-element.127), channel_id=1, source_target_pairs={{0,1},{1,0},{2,3},{3,2},{4,5},{5,4},{6,7},{7,6},{8,9},{9,8},{10,11... | collective-permute-start | bytes 1179656 | tf_op jit(solution)/shard_map/ppermute | solution.py:304
  313.8 26.8 %collective-permute-start.51 = (bf16[2,64,1536]{2,1,0:T(8,128)(2,1)S(1)}, bf16[2,64,1536]{2,1,0:T(8,128)(2,1)S(1)}, u32[]{:S(2)}, u32[]{:S(2)}) collective-permute-start(bf16[2,64,1536]{2,1,0:T(8,128)(2,1)S(1)} %get-tuple-element.128), channel_id=1, source_target_pairs={{0,3},{1,2},{2,1},{3,0},{4,7},{5,6},{6,5},{7,4},{8,11},{9,10},{10,... | collective-permute-start | bytes 1179656 | tf_op jit(solution)/shard_map/ppermute | solution.py:304
  315.3 25.3 %collective-permute-start.50 = (bf16[2,64,1536]{2,1,0:T(8,128)(2,1)S(1)}, bf16[2,64,1536]{2,1,0:T(8,128)(2,1)S(1)}, u32[]{:S(2)}, u32[]{:S(2)}) collective-permute-start(bf16[2,64,1536]{2,1,0:T(8,128)(2,1)S(1)} %get-tuple-element.129), channel_id=1, source_target_pairs={{0,2},{1,3},{2,0},{3,1},{4,6},{5,7},{6,4},{7,5},{8,10},{9,11},{10,... | collective-permute-start | bytes 1179656 | tf_op jit(solution)/shard_map/ppermute | solution.py:304
  (68 other events, 547.4 us)
Sparse Core Ops, SparseCore 0:
  295.6 43.6 reduce-scatter.3
